TPU v7x, 512 devices: a whole 4x4x16 slice. The times are simulated.
512 devices in a mesh: gx: 32 (over z, y_hi), gy: 4 (over x), gz: 4 (over y_lo, core).
Axes of the slice: x: 4, y: 4 (y_hi: 2, y_lo: 2; y = y_hi * 2 + y_lo), z: 16, core: 2. Of those that a mesh axis runs over, the one named last changes fastest.
Arguments:
- field: bfloat16 [32, 96, 32, 512], P(None, 'gx', 'gy', 'gz'), may hold values from -6 to 6
- cotangent: bfloat16 [32, 96, 32, 512], P(None, 'gx', 'gy', 'gz'), may hold values from -6 to 6
- cosmology: float32 [2], replicated, may hold values from -1 to 1
- lift_weight: float32 [2, 256], replicated, may hold values from -4 to 4
- lift_bias: float32 [256], replicated, may hold values from -3 to 3
- style_weight: float32 [256, 32], replicated, may hold values from -0.375 to 0.375
- style_bias: float32 [32], replicated, may hold values from -2 to 2
- kernel: float32 [32, 32, 3, 3, 3], replicated, may hold values from -0.21875 to 0.21875
- offset: float32 [32], replicated, may hold values from -3 to 3
Outputs:
- grad_field: bfloat16 [32, 96, 32, 512], P(None, 'gx', 'gy', 'gz')
- grad_kernel: float32 [32, 32, 3, 3, 3], replicated
- grad_offset: float32 [32], replicated
- grad_lift: float32 [2, 256], replicated
- grad_liftbias: float32 [256], replicated
- grad_style: float32 [256, 32], replicated
- grad_stylebias: float32 [32], replicated
All inputs are finite; a program needn't handle non-finite values.
Results may differ from a plain program's by a relative error of at most 0.013.
Values may be sent and summed in bfloat16 or wider, within the bound.
No kernel may reach another device: no remote copies, remote signals or barrier semaphores. Data moves between devices by JAX's collectives and lax.ppermute only.
A program may use at most 64 MiB of HBM per device.

v0:
```python
import jax
import jax.numpy as jnp
from jax import lax
from jax.sharding import PartitionSpec as P

demod_eps = 1e-06
clip_eps = 1e-06


def padded(shard, sides, width):
    for axis, dim in sides:
        devices, length = (lax.axis_size(axis), shard.shape[dim])
        up = [(i, (i + 1) % devices) for i in range(devices)]
        down = [(j, i) for i, j in up]
        last = lax.slice_in_dim(shard, length - width, length, axis=dim)
        leading = lax.slice_in_dim(shard, 0, width, axis=dim)
        before = lax.ppermute(last, axis, up)
        after = lax.ppermute(leading, axis, down)
        shard = jnp.concatenate([before, shard, after], axis=dim)
    return shard


def silu_slope(values):
    logistic = jax.nn.sigmoid(values)
    return logistic * (1.0 + values * (1.0 - logistic))


def modulate(cosmology, lift_weight, lift_bias, style_weight, style_bias, kernel):
    lifted = (
        jnp.dot(cosmology[None, :], lift_weight, precision=lax.Precision.HIGHEST)[0] + lift_bias
    )
    hidden = jax.nn.silu(lifted)
    styles = (
        jnp.dot(hidden[None, :], style_weight, precision=lax.Precision.HIGHEST)[0]
        + style_bias
        + 1.0
    )
    modded = kernel * styles[None, :, None, None, None]
    inv_norm = lax.rsqrt(jnp.sum(modded * modded, axis=(1, 2, 3, 4)) + demod_eps)
    scaled = (modded * inv_norm[:, None, None, None, None]).astype(jnp.bfloat16)
    return (lifted, hidden, styles, modded, inv_norm, scaled)


def param_backward(
    sums_kernel,
    sums_offset,
    cosmology,
    style_weight,
    kernel,
    lifted,
    hidden,
    styles,
    modded,
    inv_norm,
):
    projected = jnp.sum(sums_kernel * modded, axis=(1, 2, 3, 4))
    mod_grad = inv_norm[:, None, None, None, None] * (
        sums_kernel - modded * (inv_norm * inv_norm * projected)[:, None, None, None, None]
    )
    kernel_raw = mod_grad * styles[None, :, None, None, None]
    styles_grad = jnp.sum(mod_grad * kernel, axis=(0, 2, 3, 4))
    hidden_grad = jnp.dot(style_weight, styles_grad[:, None], precision=lax.Precision.HIGHEST)[:, 0]
    lifted_grad = hidden_grad * silu_slope(lifted)
    style_raw = hidden[:, None] * styles_grad[None, :]
    lift_raw = cosmology[:, None] * lifted_grad[None, :]
    members = (kernel_raw, sums_offset, lift_raw, lifted_grad, style_raw, styles_grad)
    square_sum = sum((jnp.sum(member * member) for member in members))
    entries = sum((member.size for member in members))
    factor = jnp.minimum(1.0, lax.rsqrt(square_sum / entries + clip_eps))
    return tuple((factor * member for member in members))


def conv_local(operand, filters):
    return lax.conv_general_dilated(
        operand[None],
        filters,
        (1, 1, 1),
        "VALID",
        dimension_numbers=("NCDHW", "OIDHW", "NCDHW"),
        preferred_element_type=jnp.float32,
    )[0]


def weight_conv(operand, upstream):
    result = lax.conv_general_dilated(
        operand[None],
        upstream[None],
        (1, 1, 1),
        "VALID",
        dimension_numbers=("CNDHW", "IODHW", "NCDHW"),
        preferred_element_type=jnp.float32,
    )
    return jnp.transpose(result, (1, 0, 2, 3, 4))


def body(
    field, cotangent, cosmology, lift_weight, lift_bias, style_weight, style_bias, kernel, offset
):
    lifted, hidden, styles, modded, inv_norm, scaled = modulate(
        cosmology, lift_weight, lift_bias, style_weight, style_bias, kernel
    )
    flipped = jnp.transpose(scaled[:, :, ::-1, ::-1, ::-1], (1, 0, 2, 3, 4))
    deep_field = padded(field, (("gx", 1), ("gy", 2), ("gz", 3)), 2)
    beside_all = padded(cotangent, (("gx", 1), ("gy", 2), ("gz", 3)), 1)
    preact = conv_local(deep_field, scaled) + offset[:, None, None, None]
    upstream_ext = (beside_all.astype(jnp.float32) * silu_slope(preact)).astype(jnp.bfloat16)
    upstream = upstream_ext[:, 1:-1, 1:-1, 1:-1]
    rimmed = deep_field[:, 1:-1, 1:-1, 1:-1]
    part_kernel = weight_conv(rimmed, upstream)
    part_offset = jnp.sum(upstream.astype(jnp.float32), axis=(1, 2, 3))
    sums_kernel, sums_offset = lax.psum((part_kernel, part_offset), ("gx", "gy", "gz"))
    grad_field = conv_local(upstream_ext, flipped).astype(jnp.bfloat16)
    grad_kernel, grad_offset, grad_lift, grad_liftbias, grad_style, grad_stylebias = param_backward(
        sums_kernel,
        sums_offset,
        cosmology,
        style_weight,
        kernel,
        lifted,
        hidden,
        styles,
        modded,
        inv_norm,
    )
    return (
        grad_field,
        grad_kernel,
        grad_offset,
        grad_lift,
        grad_liftbias,
        grad_style,
        grad_stylebias,
    )


def solution(mesh):
    placed = (
        P(None, "gx", "gy", "gz"),
        P(None, "gx", "gy", "gz"),
        P(),
        P(),
        P(),
        P(),
        P(),
        P(),
        P(),
    )
    return jax.shard_map(
        body,
        mesh=mesh,
        in_specs=placed,
        out_specs=(P(None, "gx", "gy", "gz"), P(), P(), P(), P(), P(), P()),
        check_vma=False,
    )
```

profile of v0, /device:TPU:1, one launch (start us, length us, event | category | flops | bytes accessed | tf_op | source)
XLA Modules:
  0.0 636.3 jit_solution(10629559583520585487)
XLA Ops:
  8.3 5.7 collective-permute-start.6
  14.0 10.9 %collective-permute-start.7 = (bf16[32,2,8,128]{3,0,2,1:T(8,128)(2,1)S(1)}, bf16[32,2,8,128]{3,0,2,1:T(8,128)(2,1)S(1)}, u32[]{:S(2)}, u32[]{:S(2)}) collective-permute-start(bf16[32,2,8,128]{3,0,2,1:T(8,128)(2,1)S(1)} %copy.119), channel_id=1, source_target_pairs={{16,0},{32,16},{48,32},{64,48},{80,64},{96,80},{112,96},{128,112},... | collective-permute-start | bytes 393224 | tf_op jit(solution)/shard_map/ppermute | solution.py:18
  27.7 7.0 %collective-permute-start.1 = (bf16[32,1,8,128]{3,2,1,0:T(8,128)(2,1)S(1)}, bf16[32,1,8,128]{3,2,1,0:T(8,128)(2,1)S(1)}, u32[]{:S(2)}, u32[]{:S(2)}) collective-permute-start(bf16[32,1,8,128]{3,2,1,0:T(8,128)(2,1)S(1)} %get-tuple-element.54), channel_id=1, source_target_pairs={{16,0},{32,16},{48,32},{64,48},{80,64},{96,80},{112,96},{128,112},... | collective-permute-start | bytes 196616 | tf_op jit(solution)/shard_map/ppermute | solution.py:18
  41.1 3.1 collective-permute-start.2
  44.2 3.4 collective-permute-start.3
  47.8 4.1 collective-permute-done.2
  53.5 4.6 fusion.45
  62.3 3.4 collective-permute-start.9
  66.3 5.4 collective-permute-start.4
  76.9 3.6 collective-permute-start.10
  87.0 4.0 copy.87
  100.4 4.0 copy.116
  106.3 9.0 %add_multiply_fusion = (f32[5,10,8,17,32]{4,2,3,1,0:T(8,128)}, f32[5,10,8,17,32]{4,2,3,1,0:T(8,128)S(1)}) fusion(f32[32]{0:T(128)S(1)} %copy-done.32, f32[32,32,3,3,3]{0,1,4,3,2:T(8,128)S(1)} %copy-done.2, f32[32]{0:T(128)S(1)} %add_rsqrt_fusion, f32[32]{0:T(128)S(1)} %fusion.26, bf16[32,7,12,1,7,2]{0,4,5,2,1,3:T(8,128)(2,1)S(1)} %slice.71, ...), kind=kOutput, calls=%fused_computation.4 | convolution fusion | flops 380505600 | bytes 2658312 | tf_op jit(solution)/shard_map/conv_general_dilated | solution.py:74
  115.4 5.0 copy.107
  120.3 4.3 reshape.91
  131.8 6.5 %copy.109 = bf16[1,32,5,10,130]{1,0,4,3,2:T(2,128)(2,1)S(1)} copy(bf16[1,32,5,10,130]{4,1,3,2,0:T(8,128)(2,1)} %slice_bitcast_fusion.2) | data formatting | bytes 832000 | tf_op jit(solution)/shard_map/broadcast_in_dim | solution.py:86
  138.4 22.7 %fusion.54 = f32[32,32,3,3,3]{0,1,4,3,2:T(8,128)} fusion(bf16[1,32,5,10,130]{1,0,4,3,2:T(2,128)(2,1)S(1)} %copy.109, bf16[1,32,3,8,128]{1,0,4,3,2:T(2,128)(2,1)} %copy.110), kind=kOutput, calls=%fused_computation.89 | convolution fusion | flops 169869312 | bytes 723200 | tf_op jit(solution)/shard_map/transpose | solution.py:93
  161.1 102.1 %psum.15 = f32[32]{0:T(128)S(1)} all-reduce(f32[32]{0:T(128)S(1)} %copy-done.35), channel_id=1, replica_groups=mesh['gx'=32,'gy'=4,'gz'=4] {'gx','gy','gz'}, use_global_device_ids=true, to_apply=%region_5.6 | all-reduce | flops 32 | bytes 256 | tf_op jit(solution)/shard_map/psum | solution.py:111
  263.2 6.6 %copy.100 = f32[5,10,8,17,32]{3,2,4,1,0:T(8,128)} copy(f32[5,10,8,17,32]{4,2,3,1,0:T(8,128)} %get-tuple-element.57) | data formatting | bytes 1740800 | tf_op jit(solution)/shard_map/mul | solution.py:25
  269.9 4.4 reshape.100
  276.0 3.8 reshape.94
  279.8 4.8 copy.102
  285.6 4.2 select_convert_fusion
  291.8 323.0 %all-reduce.2.cloned.1.call-done = f32[32,32,3,3,3]{0,1,4,3,2:T(8,128)} async-done(((f32[32,32,3,3,3]{0,1,4,3,2:T(8,128)}), f32[32,32,3,3,3]{0,1,4,3,2:T(8,128)}) %all-reduce.2.cloned.1.call-update) | async-done | bytes 110608 | tf_op jit(solution)/shard_map/psum | solution.py:111
  (152 shorter events, 61.6 us)
Async XLA Ops:
  7.2 29.0 %copy-start = (f32[256,32]{0,1:T(8,128)S(1)}, f32[256,32]{0,1:T(8,128)}, u32[]{:S(2)}) copy-start(f32[256,32]{0,1:T(8,128)} %param.14) | copy-start | bytes 98308
  7.2 607.6 %all-reduce.2.cloned.1.call-start = ((), (), s32[]{:S(2)}) async-start(), calls=%async_computation | async-start | bytes 884736 | tf_op jit(solution)/shard_map/psum | solution.py:111
  8.3 49.9 %collective-permute-start.6 = (bf16[32,2,8,128]{3,0,2,1:T(8,128)(2,1)S(1)}, bf16[32,2,8,128]{3,0,2,1:T(8,128)(2,1)}, u32[]{:S(2)}, u32[]{:S(2)}) collective-permute-start(bf16[32,2,8,128]{3,0,2,1:T(8,128)(2,1)S(1)} %copy.118), channel_id=1, source_target_pairs={{0,16},{16,32},{32,48},{48,64},{64,80},{80,96},{96,112},{112,128},... | collective-permute-start | bytes 393224 | tf_op jit(solution)/shard_map/ppermute | solution.py:17
  14.0 45.2 %collective-permute-start.7 = (bf16[32,2,8,128]{3,0,2,1:T(8,128)(2,1)S(1)}, bf16[32,2,8,128]{3,0,2,1:T(8,128)(2,1)S(1)}, u32[]{:S(2)}, u32[]{:S(2)}) collective-permute-start(bf16[32,2,8,128]{3,0,2,1:T(8,128)(2,1)S(1)} %copy.119), channel_id=1, source_target_pairs={{16,0},{32,16},{48,32},{64,48},{80,64},{96,80},{112,96},{128,112},... | collective-permute-start | bytes 393224 | tf_op jit(solution)/shard_map/ppermute | solution.py:18
  25.7 12.5 %collective-permute-start = (bf16[32,1,8,128]{3,2,1,0:T(8,128)(2,1)S(1)}, bf16[32,1,8,128]{3,2,1,0:T(8,128)(2,1)S(1)}, u32[]{:S(2)}, u32[]{:S(2)}) collective-permute-start(bf16[32,1,8,128]{3,2,1,0:T(8,128)(2,1)S(1)} %get-tuple-element.53), channel_id=1, source_target_pairs={{0,16},{16,32},{32,48},{48,64},{64,80},{80,96},{96,112},{112,128},... | collective-permute-start | bytes 196616 | tf_op jit(solution)/shard_map/ppermute | solution.py:17
  27.7 10.6 %collective-permute-start.1 = (bf16[32,1,8,128]{3,2,1,0:T(8,128)(2,1)S(1)}, bf16[32,1,8,128]{3,2,1,0:T(8,128)(2,1)S(1)}, u32[]{:S(2)}, u32[]{:S(2)}) collective-permute-start(bf16[32,1,8,128]{3,2,1,0:T(8,128)(2,1)S(1)} %get-tuple-element.54), channel_id=1, source_target_pairs={{16,0},{32,16},{48,32},{64,48},{80,64},{96,80},{112,96},{128,112},... | collective-permute-start | bytes 196616 | tf_op jit(solution)/shard_map/ppermute | solution.py:18
  37.0 68.9 %copy-start.24 = (f32[32]{0:T(128)}, f32[32]{0:T(128)S(1)}, u32[]{:S(2)}) copy-start(f32[32]{0:T(128)S(1)} %fusion.26) | copy-start | bytes 388
  41.1 10.8 %collective-permute-start.2 = (bf16[32,5,1,128]{0,2,3,1:T(2,128)(2,1)S(1)}, bf16[32,5,1,128]{0,2,3,1:T(2,128)(2,1)S(1)}, u32[]{:S(2)}, u32[]{:S(2)}) collective-permute-start(bf16[32,5,1,128]{0,2,3,1:T(2,128)(2,1)S(1)} %get-tuple-element.47), channel_id=1, source_target_pairs={{0,4},{4,8},{8,12},{12,0},{1,5},{5,9},{9,13},{13,1},{2,6},{6,10},{... | collective-permute-start | bytes 122888 | tf_op jit(solution)/shard_map/ppermute | solution.py:17
  44.2 9.3 %collective-permute-start.3 = (bf16[32,5,1,128]{0,2,3,1:T(2,128)(2,1)S(1)}, bf16[32,5,1,128]{0,2,3,1:T(2,128)(2,1)S(1)}, u32[]{:S(2)}, u32[]{:S(2)}) collective-permute-start(bf16[32,5,1,128]{0,2,3,1:T(2,128)(2,1)S(1)} %get-tuple-element.48), channel_id=1, source_target_pairs={{4,0},{8,4},{12,8},{0,12},{5,1},{9,5},{13,9},{1,13},{6,2},{10,6},{... | collective-permute-start | bytes 122888 | tf_op jit(solution)/shard_map/ppermute | solution.py:18
  47.8 36.3 %copy-start.33 = (f32[32]{0:T(128)}, f32[32]{0:T(128)S(1)}, u32[]{:S(2)}) copy-start(f32[32]{0:T(128)S(1)} %multiply_reduce_fusion.3) | copy-start | bytes 388
  59.2 38.4 %copy-start.5 = (bf16[32,7,8,128]{3,0,2,1:T(8,128)(2,1)}, bf16[32,7,8,128]{3,0,2,1:T(8,128)(2,1)S(1)}, u32[]{:S(2)}) copy-start(bf16[32,7,8,128]{3,0,2,1:T(8,128)(2,1)S(1)} %constant_dynamic-update-slice_fusion) | copy-start | bytes 1376260
  59.2 14.5 %collective-permute-start.8 = (bf16[32,7,2,128]{3,0,2,1:T(8,128)(2,1)S(1)}, bf16[32,7,2,128]{3,0,2,1:T(8,128)(2,1)S(1)}, u32[]{:S(2)}, u32[]{:S(2)}) collective-permute-start(bf16[32,7,2,128]{3,0,2,1:T(8,128)(2,1)S(1)} %get-tuple-element.51), channel_id=1, source_target_pairs={{0,4},{4,8},{8,12},{12,0},{1,5},{5,9},{9,13},{13,1},{2,6},{6,10},{... | collective-permute-start | bytes 344072 | tf_op jit(solution)/shard_map/ppermute | solution.py:17
  62.3 11.4 %collective-permute-start.9 = (bf16[32,7,2,128]{3,0,2,1:T(8,128)(2,1)S(1)}, bf16[32,7,2,128]{3,0,2,1:T(8,128)(2,1)S(1)}, u32[]{:S(2)}, u32[]{:S(2)}) collective-permute-start(bf16[32,7,2,128]{3,0,2,1:T(8,128)(2,1)S(1)} %get-tuple-element.52), channel_id=1, source_target_pairs={{4,0},{8,4},{12,8},{0,12},{5,1},{9,5},{13,9},{1,13},{6,2},{10,6},{... | collective-permute-start | bytes 344072 | tf_op jit(solution)/shard_map/ppermute | solution.py:18
  66.3 24.6 %collective-permute-start.4 = (bf16[32,5,10,1]{0,2,3,1:T(8,128)(2,1)}, bf16[32,5,10,1]{0,2,3,1:T(8,128)(2,1)S(1)}, u32[]{:S(2)}, u32[]{:S(2)}) collective-permute-start(bf16[32,5,10,1]{0,2,3,1:T(8,128)(2,1)} %get-tuple-element.43), channel_id=1, source_target_pairs={{0,1},{1,2},{2,3},{3,0},{4,5},{5,6},{6,7},{7,4},{8,9},{9,10},{10,1... | collective-permute-start | bytes 9608 | tf_op jit(solution)/shard_map/ppermute | solution.py:17
  71.8 20.3 %collective-permute-start.5 = (bf16[32,5,10,1]{0,2,3,1:T(8,128)(2,1)S(1)}, bf16[32,5,10,1]{0,2,3,1:T(8,128)(2,1)S(1)}, u32[]{:S(2)}, u32[]{:S(2)}) collective-permute-start(bf16[32,5,10,1]{0,2,3,1:T(8,128)(2,1)S(1)} %get-tuple-element.44), channel_id=1, source_target_pairs={{1,0},{2,1},{3,2},{0,3},{5,4},{6,5},{7,6},{4,7},{9,8},{10,9},{11,1... | collective-permute-start | bytes 9608 | tf_op jit(solution)/shard_map/ppermute | solution.py:18
  73.7 23.9 %copy-start.18 = (bf16[32,7,2,128]{3,0,2,1:T(8,128)(2,1)}, bf16[32,7,2,128]{3,0,2,1:T(8,128)(2,1)S(1)}, u32[]{:S(2)}) copy-start(bf16[32,7,2,128]{3,0,2,1:T(8,128)(2,1)S(1)} %collective-permute-done.8) | copy-start | bytes 344068
  76.9 18.6 %collective-permute-start.10 = (bf16[32,7,12,2]{0,3,2,1:T(2,128)(2,1)S(1)}, bf16[32,7,12,2]{0,3,2,1:T(2,128)(2,1)S(1)}, u32[]{:S(2)}, u32[]{:S(2)}) collective-permute-start(bf16[32,7,12,2]{0,3,2,1:T(2,128)(2,1)S(1)} %copy.92), channel_id=1, source_target_pairs={{0,1},{1,2},{2,3},{3,0},{4,5},{5,6},{6,7},{7,4},{8,9},{9,10},{10,1... | collective-permute-start | bytes 32264 | tf_op jit(solution)/shard_map/ppermute | solution.py:17
  82.2 14.0 %collective-permute-start.11 = (bf16[32,7,12,2]{0,3,2,1:T(2,128)(2,1)S(1)}, bf16[32,7,12,2]{0,3,2,1:T(2,128)(2,1)}, u32[]{:S(2)}, u32[]{:S(2)}) collective-permute-start(bf16[32,7,12,2]{0,3,2,1:T(2,128)(2,1)S(1)} %copy.93), channel_id=1, source_target_pairs={{1,0},{2,1},{3,2},{0,3},{5,4},{6,5},{7,6},{4,7},{9,8},{10,9},{11,1... | collective-permute-start | bytes 32264 | tf_op jit(solution)/shard_map/ppermute | solution.py:18
  289.8 325.0 %copy-start.3 = (f32[32,32,3,3,3]{0,1,4,3,2:T(8,128)S(1)}, f32[32,32,3,3,3]{0,1,4,3,2:T(8,128)}, u32[]{:S(2)}) copy-start(f32[32,32,3,3,3]{0,1,4,3,2:T(8,128)} %copy-done.1) | copy-start | bytes 331780
  289.8 326.2 %copy-start.34 = (f32[32]{0:T(128)S(1)}, f32[32]{0:T(128)}, u32[]{:S(2)}) copy-start(f32[32]{0:T(128)} %copy-done.33) | copy-start | bytes 388
  289.8 328.2 %copy-start.23 = (f32[256]{0:T(256)S(1)}, f32[256]{0:T(256)}, u32[]{:S(2)}) copy-start(f32[256]{0:T(256)} %copy-done.22) | copy-start | bytes 3076
  289.8 329.4 %copy-start.26 = (f32[256]{0:T(256)S(1)}, f32[256]{0:T(256)}, u32[]{:S(2)}) copy-start(f32[256]{0:T(256)} %param.13) | copy-start | bytes 3076
  289.8 329.4 %copy-start.28 = (f32[1,256]{1,0:T(1,128)S(1)}, f32[1,256]{1,0:T(1,128)}, u32[]{:S(2)}) copy-start(f32[1,256]{1,0:T(1,128)} %copy-done.27) | copy-start | bytes 3076
  289.9 330.0 %copy-start.31 = (f32[2]{0:T(128)S(1)}, f32[2]{0:T(128)}, u32[]{:S(2)}) copy-start(f32[2]{0:T(128)} %param.11) | copy-start | bytes 28
  (27 other events, 179.3 us)
Sparse Core Ops, SparseCore 0:
  161.2 453.5 all-reduce.1
where the time goes:
time: 646 us; the launch traced here: 636 us
  waiting for transfers between devices  329 us (51%)
  blocking collectives  102 us (16%)
  local copies, waits for them, and re-layouts  76 us (12%)
  starting transfers between devices  51.4 us (8%)
  matrix products  37.6 us (6%)
  other arithmetic  21.4 us (3%)
  between operations  19.2 us (3%)
    psum x1, waiting for transfers between devices, body(): lax.psum((part_kernel, part_offset), ('gx', 'gy', 'gz'))  323 us
    psum x1, blocking collectives, body(): lax.psum((part_kernel, part_offset), ('gx', 'gy', 'gz'))  102 us
    ppermute x6, starting transfers between devices, padded(): after = lax.ppermute(leading, axis, down)  28.4 us
    ppermute x6, starting transfers between devices, padded(): before = lax.ppermute(last, axis, up)  22.9 us
    transpose x1, matrix products, weight_conv(): return jnp.transpose(result, (1, 0, 2, 3, 4))  22.7 us
    conv_general_dilated x7, local copies, waits for them, and re-layouts, conv_local(): lax.conv_general_dilated(operand[None], filters, (1, 1, 1), 'VALID', dime...  19.3 us
    conv_general_dilated x2, matrix products, conv_local(): lax.conv_general_dilated(operand[None], filters, (1, 1, 1), 'VALID', dime...  13.2 us
  transfers between devices with their start and end apart: 13, of which 3 were waited for; matrix products, arithmetic and copies ran while one was open for 9% of the time, Pallas kernels for 0%

commit v1 on v0

v1 whole, which is shorter than its diff:
```python
import numpy as np
import jax
import jax.numpy as jnp
from jax import lax
from jax.experimental import pallas as pl
from jax.experimental.pallas import tpu as pltpu
from jax.sharding import PartitionSpec as P

demod_eps = 1e-06
clip_eps = 1e-06

C = 32
TAPS = 27
PITCH = 132
PLANE = 14 * 128
OUT = 11 * 128
GRAD = 9 * 128
FIELD_ROWS = 7 * 12 * C
COT_ROWS = 5 * 10 * C
f32 = jnp.float32
bf16 = jnp.bfloat16
VMEM = pl.BlockSpec(memory_space=pltpu.VMEM)


def call(kernel, outs, n_in, flops=0, limit=40):
    return pl.pallas_call(
        kernel,
        out_shape=outs,
        in_specs=[VMEM] * n_in,
        out_specs=[VMEM] * len(outs),
        cost_estimate=pl.CostEstimate(flops=flops, bytes_accessed=1 << 20, transcendentals=0),
        compiler_params=pltpu.CompilerParams(vmem_limit_bytes=limit * 1024 * 1024),
    )


def shape(*dims, dtype=bf16):
    return jax.ShapeDtypeStruct(dims, dtype)


def split_kernel(field_ref, cot_ref, perm_ref, low_ref, high_ref, mid_ref):
    def rows(ref, x):
        block = ref[:, x].astype(f32).reshape(C * 8, 128).astype(bf16)
        moved = jnp.dot(perm_ref[...], block, preferred_element_type=f32)
        return moved.astype(bf16).reshape(8, C, 128)

    f0, f1, f2 = (rows(field_ref, x) for x in range(3))
    c0, c1, c2 = (rows(cot_ref, x) for x in range(3))
    low_ref[0], low_ref[1], low_ref[2] = f0, f1, c0
    high_ref[0], high_ref[1], high_ref[2] = f1, f2, c2
    mid_ref[0] = c1


def planes(low_ref, high_ref, mid_ref, left_ref, right_ref):
    field = (
        (left_ref, 0), (left_ref, 1), (low_ref, 0), (low_ref, 1), (high_ref, 1), (right_ref, 0), (right_ref, 1),
    )
    cot = ((left_ref, 2), (low_ref, 2), (mid_ref, 0), (high_ref, 2), (right_ref, 2))
    return field, cot


def pack_kernel(low_ref, high_ref, mid_ref, left_ref, right_ref, up_ref, down_ref):
    field, cot = planes(low_ref, high_ref, mid_ref, left_ref, right_ref)
    for n, (ref, at) in enumerate(field):
        up_ref[2 * n : 2 * n + 2] = ref[at, 6:8]
        down_ref[2 * n : 2 * n + 2] = ref[at, 0:2]
    for n, (ref, at) in enumerate(cot):
        up_ref[14 + n] = ref[at, 7]
        down_ref[14 + n] = ref[at, 0]


def gather_kernel(
    low_ref, high_ref, mid_ref, left_ref, right_ref, up_ref, down_ref, pick_ref,
    field_out, cot_out, hi_ref, lo_ref,
):
    field, cot = planes(low_ref, high_ref, mid_ref, left_ref, right_ref)
    for n, (ref, at) in enumerate(field):
        field_out[n, 0:2] = up_ref[2 * n : 2 * n + 2]
        field_out[n, 2:10] = ref[at]
        field_out[n, 10:12] = down_ref[2 * n : 2 * n + 2]
    for n, (ref, at) in enumerate(cot):
        cot_out[n, 0] = up_ref[14 + n]
        cot_out[n, 1:9] = ref[at]
        cot_out[n, 9] = down_ref[14 + n]

    def faces(pick, rows):
        return lax.dot_general(
            pick, rows, (((1,), (1,)), ((), ())), preferred_element_type=f32
        ).astype(bf16)

    frows = field_out[...].reshape(FIELD_ROWS, 128)
    crows = cot_out[...].reshape(COT_ROWS, 128)
    hi_ref[:, :FIELD_ROWS] = faces(pick_ref[0], frows)
    lo_ref[:, :FIELD_ROWS] = faces(pick_ref[1], frows)
    hi_ref[:, FIELD_ROWS:] = faces(pick_ref[2], crows)
    lo_ref[:, FIELD_ROWS:] = faces(pick_ref[3], crows)


def silu_slope(values):
    logistic = jax.nn.sigmoid(values)
    return logistic * (1.0 + values * (1.0 - logistic))


def conv_kernel(
    field_ref, cot_ref, before_ref, after_ref, place_ref, mask_ref, fwd_ref, bwd_ref, offset_ref,
    grad_ref, sums_ref,
    edge, plane, cols, cot_flat, up, ucols, total,
):
    def placed(faces, place):
        return lax.dot_general(
            faces, place, (((0,), (0,)), ((), ())), preferred_element_type=f32
        )

    edge[:FIELD_ROWS] = (
        placed(before_ref[:, :FIELD_ROWS], place_ref[0]) + placed(after_ref[:, :FIELD_ROWS], place_ref[1])
    ).astype(bf16)
    edge[FIELD_ROWS:] = (
        placed(before_ref[:, FIELD_ROWS:], place_ref[2]) + placed(after_ref[:, FIELD_ROWS:], place_ref[3])
    ).astype(bf16)

    @pl.loop(0, 7)
    def _(x):
        pieces = []
        for y in range(12):
            sides = edge[pl.ds(pl.multiple_of((x * 12 + y) * C, C), C), :]
            pieces += [sides[:, 0:2], field_ref[x, y], sides[:, 2:4]]
        plane[...] = jnp.concatenate(
            pieces + [jnp.zeros((C, PLANE - 12 * PITCH), bf16)], axis=1
        )
        for t in range(9):
            at = (t // 3) * PITCH + t % 3
            cols[x, t * C : (t + 1) * C, :] = plane[:, at : at + OUT]

    total[...] = jnp.zeros_like(total)

    @pl.loop(0, 5)
    def _(x):
        pieces = []
        for y in range(10):
            sides = edge[pl.ds(pl.multiple_of(FIELD_ROWS + (x * 10 + y) * C, C), C), :]
            pieces += [sides[:, 0:1], cot_ref[x, y], sides[:, 1:2], jnp.zeros((C, 2), bf16)]
        pieces.append(jnp.zeros((C, OUT - 10 * PITCH), bf16))
        beside = jnp.concatenate(pieces, axis=1).astype(f32)
        block = cols[pl.ds(x, 3)].reshape(3 * 9 * C, OUT)
        preact = jnp.dot(fwd_ref[...], block, preferred_element_type=f32) + offset_ref[...]
        upstream = (beside * silu_slope(preact)).astype(bf16)
        up[:, :OUT] = upstream
        up[:, OUT:] = jnp.zeros((C, 128), bf16)
        for t in range(9):
            at = (t // 3) * PITCH + t % 3
            ucols[x, t * C : (t + 1) * C, :] = up[:, at : at + GRAD]

        @pl.when((x >= 1) & (x <= 3))
        def _():
            own = upstream.astype(f32) * mask_ref[...]
            total[:, 864:] += jnp.sum(own, axis=1, keepdims=True)
            total[:, :864] += lax.dot_general(
                own.astype(bf16), block, (((1,), (1,)), ((), ())), preferred_element_type=f32
            )

    for s in range(4):
        for l in range(8):
            at = (s * 8 + l) * 8
            if l < 7:
                sums_ref[at : at + 8] = total[8 * s : 8 * s + 8, 128 * l : 128 * l + 128]
            else:
                sums_ref[at : at + 8] = jnp.zeros((8, 128), f32)

    @pl.loop(0, 3)
    def _(x):
        block = ucols[pl.ds(x, 3)].reshape(3 * 9 * C, GRAD)
        grad = jnp.dot(bwd_ref[...], block, preferred_element_type=f32).astype(bf16)
        for y in range(8):
            grad_ref[x, y] = grad[:, y * PITCH : y * PITCH + 128]


def constants():
    perm = np.zeros((256, 256), np.float32)
    for y in range(8):
        for c in range(C):
            perm[y * C + c, c * 8 + y] = 1
    pick = np.zeros((4, 8, 128), np.float32)
    pick[0, 0, 126] = pick[0, 1, 127] = 1
    pick[1, 0, 0] = pick[1, 1, 1] = 1
    pick[2, 0, 127] = 1
    pick[3, 0, 0] = 1
    place = np.zeros((4, 8, 128), np.float32)
    place[0, 0, 0] = place[0, 1, 1] = 1
    place[1, 0, 2] = place[1, 1, 3] = 1
    place[2, 0, 0] = 1
    place[3, 0, 1] = 1
    mask = np.zeros((1, OUT), np.float32)
    for y in range(1, 9):
        mask[0, y * PITCH + 1 : y * PITCH + 129] = 1
    return (
        jnp.asarray(perm, bf16), jnp.asarray(pick, bf16), jnp.asarray(place, bf16), jnp.asarray(mask, f32),
    )


def shifts(axis):
    n = lax.axis_size(axis)
    ahead = [(i, (i + 1) % n) for i in range(n)]
    return ahead, [(j, i) for i, j in ahead]


def modulate(cosmology, lift_weight, lift_bias, style_weight, style_bias, kernel):
    lifted = (
        jnp.dot(cosmology[None, :], lift_weight, precision=lax.Precision.HIGHEST)[0] + lift_bias
    )
    hidden = jax.nn.silu(lifted)
    styles = (
        jnp.dot(hidden[None, :], style_weight, precision=lax.Precision.HIGHEST)[0]
        + style_bias
        + 1.0
    )
    modded = kernel * styles[None, None, :]
    inv_norm = lax.rsqrt(jnp.sum(modded * modded, axis=(0, 2)) + demod_eps)
    scaled = (modded * inv_norm[None, :, None]).astype(bf16)
    return (lifted, hidden, styles, modded, inv_norm, scaled)


def param_backward(
    sums_kernel, sums_offset, cosmology, style_weight, kernel, lifted, hidden, styles, modded, inv_norm
):
    projected = jnp.sum(sums_kernel * modded, axis=(0, 2))
    mod_grad = inv_norm[None, :, None] * (
        sums_kernel - modded * (inv_norm * inv_norm * projected)[None, :, None]
    )
    kernel_raw = mod_grad * styles[None, None, :]
    styles_grad = jnp.sum(mod_grad * kernel, axis=(0, 1))
    hidden_grad = jnp.dot(style_weight, styles_grad[:, None], precision=lax.Precision.HIGHEST)[:, 0]
    lifted_grad = hidden_grad * silu_slope(lifted)
    style_raw = hidden[:, None] * styles_grad[None, :]
    lift_raw = cosmology[:, None] * lifted_grad[None, :]
    members = (kernel_raw, sums_offset, lift_raw, lifted_grad, style_raw, styles_grad)
    square_sum = sum((jnp.sum(member * member) for member in members))
    entries = sum((member.size for member in members))
    factor = jnp.minimum(1.0, lax.rsqrt(square_sum / entries + clip_eps))
    return tuple((factor * member for member in members))


def summed(sums):
    part = jnp.sum(lax.all_to_all(sums.reshape(16, 16, 128), ("gy", "gz"), 0, 0, tiled=True), axis=0)
    spread = jnp.broadcast_to(part[None], (32, 16, 128))
    part = jnp.sum(lax.all_to_all(spread, "gx", 0, 0, tiled=True), axis=0)
    spread = jnp.broadcast_to(part[None], (16, 16, 128))
    return lax.all_to_all(spread, ("gy", "gz"), 0, 0, tiled=True)


def body(
    field, cotangent, cosmology, lift_weight, lift_bias, style_weight, style_bias, kernel, offset
):
    perm, pick, place, mask = constants()
    low, high, mid = call(
        split_kernel, [shape(3, 8, C, 128), shape(3, 8, C, 128), shape(1, 8, C, 128)], 3
    )(field, cotangent, perm)
    ahead, back = shifts("gx")
    left = lax.ppermute(high, "gx", ahead)
    right = lax.ppermute(low, "gx", back)

    taps = jnp.transpose(kernel, (2, 3, 4, 0, 1)).reshape(TAPS, C, C)
    lifted, hidden, styles, modded, inv_norm, scaled = modulate(
        cosmology, lift_weight, lift_bias, style_weight, style_bias, taps
    )
    fwd = jnp.transpose(scaled, (1, 0, 2)).reshape(C, TAPS * C)
    bwd = jnp.transpose(scaled[::-1], (2, 0, 1)).reshape(C, TAPS * C)

    rows = (low, high, mid, left, right)
    up, down = call(pack_kernel, [shape(19, C, 128), shape(19, C, 128)], 5)(*rows)
    ahead, back = shifts("gy")
    up = lax.ppermute(up, "gy", ahead)
    down = lax.ppermute(down, "gy", back)

    field_rows, cot_rows, hi, lo = call(
        gather_kernel,
        [
            shape(7, 12, C, 128), shape(5, 10, C, 128),
            shape(8, FIELD_ROWS + COT_ROWS), shape(8, FIELD_ROWS + COT_ROWS),
        ],
        8,
    )(*rows, up, down, pick)
    ahead, back = shifts("gz")
    before = lax.ppermute(hi, "gz", ahead)
    after = lax.ppermute(lo, "gz", back)

    grad_rows, sums = pl.pallas_call(
        conv_kernel,
        out_shape=[shape(3, 8, C, 128), shape(256, 128, dtype=f32)],
        in_specs=[VMEM] * 9,
        out_specs=[VMEM] * 2,
        scratch_shapes=[
            pltpu.VMEM((FIELD_ROWS + COT_ROWS, 128), bf16),
            pltpu.VMEM((C, PLANE), bf16),
            pltpu.VMEM((7, 9 * C, OUT), bf16),
            pltpu.VMEM((C, OUT), bf16),
            pltpu.VMEM((C, OUT + 128), bf16),
            pltpu.VMEM((5, 9 * C, GRAD), bf16),
            pltpu.VMEM((C, 896), f32),
        ],
        cost_estimate=pl.CostEstimate(flops=700_000_000, bytes_accessed=4 << 20, transcendentals=0),
        compiler_params=pltpu.CompilerParams(vmem_limit_bytes=48 * 1024 * 1024),
    )(field_rows, cot_rows, before, after, place, mask, fwd, bwd, offset[:, None])
    grad_field = jnp.transpose(grad_rows, (2, 0, 1, 3))

    sums = summed(sums).reshape(4, 8, 8, 128).transpose(0, 2, 1, 3).reshape(C, 1024)
    sums_kernel = sums[:, : TAPS * C].reshape(C, TAPS, C).transpose(1, 0, 2)
    sums_offset = sums[:, TAPS * C]
    kernel_out, grad_offset, grad_lift, grad_liftbias, grad_style, grad_stylebias = param_backward(
        sums_kernel, sums_offset, cosmology, style_weight, taps, lifted, hidden, styles, modded, inv_norm
    )
    grad_kernel = jnp.transpose(kernel_out.reshape(3, 3, 3, C, C), (3, 4, 0, 1, 2))
    return (
        grad_field, grad_kernel, grad_offset, grad_lift, grad_liftbias, grad_style, grad_stylebias,
    )


def solution(mesh):
    placed = (P(None, "gx", "gy", "gz"),) * 2 + (P(),) * 7
    return jax.shard_map(
        body,
        mesh=mesh,
        in_specs=placed,
        out_specs=(P(None, "gx", "gy", "gz"),) + (P(),) * 6,
        check_vma=False,
    )
```

time: 646 us -> 125 us (0.19); the launches traced: 636 us -> 125 us
  waiting for transfers between devices: 329 us -> 12.4 us
  local copies, waits for them, and re-layouts: 76 us -> 6.97 us
  blocking collectives: 102 us -> 44.4 us
  matrix products: 37.6 us -> 0.38 us
  starting transfers between devices: 51.4 us -> 35 us
  between operations: 19.2 us -> 4.77 us
  other arithmetic: 21.4 us -> 9.14 us
  Pallas kernels: 0 us -> 11.6 us
    psum x1 -> x0, waiting for transfers between devices: 323 us -> none  [body(): lax.psum((part_kernel, part_offset), ('gx', 'gy', 'gz'))]
    psum x1 -> x0, blocking collectives: 102 us -> none  [body(): lax.psum((part_kernel, part_offset), ('gx', 'gy', 'gz'))]
    all_to_all x0 -> x2, blocking collectives: none -> 44.4 us  [the longest x1 32.8 us: summed(): part = jnp.sum(lax.all_to_all(spread, 'gx', 0, 0, tiled=True), axis=0)]
    transpose x1 -> x0, matrix products: 22.7 us -> none  [weight_conv(): return jnp.transpose(result, (1, 0, 2, 3, 4))]
    ppermute x12 -> x6, starting transfers between devices: 51.3 us -> 29.8 us  [the longest x1 10.8 us: body(): right = lax.ppermute(low, 'gx', back)]
    conv_general_dilated x7 -> x0, local copies, waits for them, and re-layouts: 19.3 us -> none  [conv_local(): lax.conv_general_dilated(operand[None], filters, (1, 1, 1), 'VALID', dime...]
    conv_general_dilated x2 -> x0, matrix products: 13.2 us -> none  [conv_local(): lax.conv_general_dilated(operand[None], filters, (1, 1, 1), 'VALID', dime...]
    pallas_call x0 -> x4, Pallas kernels: none -> 11.6 us  [the longest x1 10.6 us: body(): pl.pallas_call(conv_kernel, out_shape=[shape(3, 8, C, 128), shape(256, 12...]
  transfers between devices with their start and end apart: 13 -> 7, of which waited for: 3 -> 6; matrix products, arithmetic and copies ran while one was open for 9% -> 2% of each run, Pallas kernels for 0% -> 0%
where the time goes in v1:
time: 125 us
  blocking collectives  44.4 us (36%)
  starting transfers between devices  35 us (28%)
  waiting for transfers between devices  12.4 us (10%)
  Pallas kernels  11.6 us (9%)
  other arithmetic  9.14 us (7%)
  local copies, waits for them, and re-layouts  6.97 us (6%)
  between operations  4.77 us (4%)
    all_to_all x1, blocking collectives, summed(): part = jnp.sum(lax.all_to_all(spread, 'gx', 0, 0, tiled=True), axis=0)  32.8 us
    all_to_all x1, blocking collectives, summed(): lax.all_to_all(sums.reshape(16, 16, 128), ('gy', 'gz'), 0, 0, tiled=True)  11.5 us
    ppermute x1, starting transfers between devices, body(): right = lax.ppermute(low, 'gx', back)  10.8 us
    pallas_call x1, Pallas kernels, body(): pl.pallas_call(conv_kernel, out_shape=[shape(3, 8, C, 128), shape(256, 12...  10.6 us
    ppermute x1, starting transfers between devices, body(): left = lax.ppermute(high, 'gx', ahead)  5.65 us
    unnamed x27, local copies, waits for them, and re-layouts  5.54 us
    all_to_all x1, waiting for transfers between devices, summed(): return lax.all_to_all(spread, ('gy', 'gz'), 0, 0, tiled=True)  5.47 us
    all_to_all x1, starting transfers between devices, summed(): return lax.all_to_all(spread, ('gy', 'gz'), 0, 0, tiled=True)  5.2 us
  transfers between devices with their start and end apart: 7, of which 6 were waited for; matrix products, arithmetic and copies ran while one was open for 2% of the time, Pallas kernels for 0%

profile of v1, /device:TPU:1, one launch (start us, length us, event | category | flops | bytes accessed | tf_op | source)
XLA Modules:
  0.0 124.7 jit_solution(13200068396778047756)
XLA Ops:
  0.7 0.9 copy-done.1
  1.6 0.9 copy-done.2
  2.5 0.9 copy-done.3
  3.8 5.6 %collective-permute-start = (bf16[3,8,32,128]{3,2,1,0:T(8,128)(2,1)S(1)}, bf16[3,8,32,128]{3,2,1,0:T(8,128)(2,1)S(1)}, u32[]{:S(2)}, u32[]{:S(2)}) collective-permute-start(bf16[3,8,32,128]{3,2,1,0:T(8,128)(2,1)S(1)} %get-tuple-element.19.high_ref), channel_id=1, source_target_pairs={{0,16},{16,32},{32,48},{48,64},{64,80},{80,96},{96,112},{112,128},... | collective-permute-start | bytes 589832 | tf_op jit(solution)/shard_map/ppermute | solution.py:257
  9.5 10.8 %collective-permute-start.1 = (bf16[3,8,32,128]{3,2,1,0:T(8,128)(2,1)S(1)}, bf16[3,8,32,128]{3,2,1,0:T(8,128)(2,1)S(1)}, u32[]{:S(2)}, u32[]{:S(2)}) collective-permute-start(bf16[3,8,32,128]{3,2,1,0:T(8,128)(2,1)S(1)} %get-tuple-element.18.low_ref), channel_id=1, source_target_pairs={{16,0},{32,16},{48,32},{64,48},{80,64},{96,80},{112,96},{128,112},... | collective-permute-start | bytes 589832 | tf_op jit(solution)/shard_map/ppermute | solution.py:258
  22.1 0.9 collective-permute-done.left_ref
  23.0 0.9 collective-permute-done.1.right_ref
  23.9 3.1 %collective-permute-start.2 = (bf16[19,32,128]{2,1,0:T(8,128)(2,1)S(1)}, bf16[19,32,128]{2,1,0:T(8,128)(2,1)S(1)}, u32[]{:S(2)}, u32[]{:S(2)}) collective-permute-start(bf16[19,32,128]{2,1,0:T(8,128)(2,1)S(1)} %get-tuple-element.21), channel_id=1, source_target_pairs={{0,4},{4,8},{8,12},{12,0},{1,5},{5,9},{9,13},{13,1},{2,6},{6,10},{... | collective-permute-start | bytes 466952 | tf_op jit(solution)/shard_map/ppermute | solution.py:270
  27.1 3.4 %collective-permute-start.3 = (bf16[19,32,128]{2,1,0:T(8,128)(2,1)S(1)}, bf16[19,32,128]{2,1,0:T(8,128)(2,1)S(1)}, u32[]{:S(2)}, u32[]{:S(2)}) collective-permute-start(bf16[19,32,128]{2,1,0:T(8,128)(2,1)S(1)} %get-tuple-element.22), channel_id=1, source_target_pairs={{4,0},{8,4},{12,8},{0,12},{5,1},{9,5},{13,9},{1,13},{6,2},{10,6},{... | collective-permute-start | bytes 466952 | tf_op jit(solution)/shard_map/ppermute | solution.py:271
  31.1 2.2 %collective-permute-done.3.down_ref = bf16[19,32,128]{2,1,0:T(8,128)(2,1)S(1)} collective-permute-done((bf16[19,32,128]{2,1,0:T(8,128)(2,1)S(1)}, bf16[19,32,128]{2,1,0:T(8,128)(2,1)S(1)}, u32[]{:S(2)}, u32[]{:S(2)}) %collective-permute-start.3) | collective-permute-done | bytes 155680 | tf_op jit(solution)/shard_map/ppermute | solution.py:271
  33.3 0.7 shard_map.182
  34.0 4.9 %collective-permute-start.4 = (bf16[8,4288]{1,0:T(8,128)(2,1)S(1)}, bf16[8,4288]{1,0:T(8,128)(2,1)S(1)}, u32[]{:S(2)}, u32[]{:S(2)}) collective-permute-start(bf16[8,4288]{1,0:T(8,128)(2,1)S(1)} %get-tuple-element.25), channel_id=1, source_target_pairs={{0,1},{1,2},{2,3},{3,0},{4,5},{5,6},{6,7},{7,4},{8,9},{9,10},{10,1... | collective-permute-start | bytes 205832 | tf_op jit(solution)/shard_map/ppermute | solution.py:282
  38.9 1.9 %collective-permute-start.5 = (bf16[8,4288]{1,0:T(8,128)(2,1)S(1)}, bf16[8,4288]{1,0:T(8,128)(2,1)S(1)}, u32[]{:S(2)}, u32[]{:S(2)}) collective-permute-start(bf16[8,4288]{1,0:T(8,128)(2,1)S(1)} %get-tuple-element.26), channel_id=1, source_target_pairs={{1,0},{2,1},{3,2},{0,3},{5,4},{6,5},{7,6},{4,7},{9,8},{10,9},{11,1... | collective-permute-start | bytes 205832 | tf_op jit(solution)/shard_map/ppermute | solution.py:283
  42.2 2.3 %collective-permute-done.5.after_ref = bf16[8,4288]{1,0:T(8,128)(2,1)S(1)} collective-permute-done((bf16[8,4288]{1,0:T(8,128)(2,1)S(1)}, bf16[8,4288]{1,0:T(8,128)(2,1)S(1)}, u32[]{:S(2)}, u32[]{:S(2)}) %collective-permute-start.5) | collective-permute-done | bytes 68640 | tf_op jit(solution)/shard_map/ppermute | solution.py:283
  44.6 10.6 %shard_map.183 = (bf16[3,8,32,128]{3,2,1,0:T(8,128)(2,1)S(1)}, f32[256,128]{1,0:T(8,128)S(1)}) custom-call(bf16[7,12,32,128]{3,2,1,0:T(8,128)(2,1)S(1)} %get-tuple-element.23.field_ref, bf16[5,10,32,128]{3,2,1,0:T(8,128)(2,1)S(1)} %get-tuple-element.24.cot_ref, bf16[8,4288]{1,0:T(8,128)(2,1)S(1)} %collective-permute-done.4.before_ref, ...), custom_call_target="tpu_custom_call" | custom-call | flops 700000000 | bytes 4194304 | tf_op jit(solution)/shard_map/pallas_call | solution.py:285
  55.1 11.5 %all_to_all.15 = f32[16,16,128]{2,1,0:T(8,128)S(1)} all-to-all(f32[16,16,128]{2,1,0:T(8,128)S(1)} %bitcast.72), channel_id=1, replica_groups=mesh['gx'=32,'gy'=4,'gz'=4] {'gy','gz'}, dimensions={0} | all-to-all | bytes 262144 | tf_op jit(solution)/shard_map/all_to_all | solution.py:242
  66.7 32.8 %all_to_all.16 = f32[32,16,128]{2,1,0:T(8,128)S(1)} all-to-all(f32[32,16,128]{2,1,0:T(8,128)S(1)} %broadcast_in_dim.7), channel_id=1, replica_groups=mesh['gx'=32,'gy'=4,'gz'=4] {'gx'}, dimensions={0} | all-to-all | bytes 524288 | tf_op jit(solution)/shard_map/all_to_all | solution.py:244
  100.2 5.2 %all-to-all-start.2 = ((f32[16,16,128]{2,1,0:T(8,128)}), f32[16,16,128]{2,1,0:T(8,128)S(1)}, u32[]{:S(2)}, u32[]{:S(2)}) async-start(f32[16,16,128]{2,1,0:T(8,128)} %broadcast_in_dim.8), calls=%async_computation.2 | async-start | bytes 262144 | tf_op jit(solution)/shard_map/all_to_all | solution.py:246
  105.4 0.8 copy.48
  106.2 5.5 %all-to-all-done.2 = f32[16,16,128]{2,1,0:T(8,128)S(1)} async-done(((f32[16,16,128]{2,1,0:T(8,128)}), f32[16,16,128]{2,1,0:T(8,128)S(1)}, u32[]{:S(2)}, u32[]{:S(2)}) %all-to-all-start.2) | async-done | bytes 131104 | tf_op jit(solution)/shard_map/all_to_all | solution.py:246
  112.9 1.0 fusion.2
  114.0 0.7 fusion.7
  122.9 0.7 multiply_reduce_fusion.1
  123.6 1.1 multiply_multiply_fusion
  (55 shorter events, 10.6 us)
Async XLA Ops:
  0.6 20.5 %copy-start = (f32[256,32]{0,1:T(8,128)S(1)}, f32[256,32]{0,1:T(8,128)}, u32[]{:S(2)}) copy-start(f32[256,32]{0,1:T(8,128)} %param.18) | copy-start | bytes 98308
  0.6 0.9 copy-start.1
  1.6 0.9 copy-start.2
  2.5 0.9 copy-start.3
  3.4 18.5 %copy-start.7 = (f32[32,32,3,3,3]{1,0,4,3,2:T(8,128)S(1)}, f32[32,32,3,3,3]{1,0,4,3,2:T(8,128)}, u32[]{:S(2)}) copy-start(f32[32,32,3,3,3]{1,0,4,3,2:T(8,128)} %param.20) | copy-start | bytes 331780
  3.8 16.5 %copy-start.12 = (f32[2,256]{1,0:T(2,128)S(1)}, f32[2,256]{1,0:T(2,128)}, u32[]{:S(2)}) copy-start(f32[2,256]{1,0:T(2,128)} %param.16) | copy-start | bytes 6148
  3.8 16.5 %copy-start.9 = (f32[2]{0:T(128)S(1)}, f32[2]{0:T(128)}, u32[]{:S(2)}) copy-start(f32[2]{0:T(128)} %param.15) | copy-start | bytes 28
  3.8 19.2 %collective-permute-start = (bf16[3,8,32,128]{3,2,1,0:T(8,128)(2,1)S(1)}, bf16[3,8,32,128]{3,2,1,0:T(8,128)(2,1)S(1)}, u32[]{:S(2)}, u32[]{:S(2)}) collective-permute-start(bf16[3,8,32,128]{3,2,1,0:T(8,128)(2,1)S(1)} %get-tuple-element.19.high_ref), channel_id=1, source_target_pairs={{0,16},{16,32},{32,48},{48,64},{64,80},{80,96},{96,112},{112,128},... | collective-permute-start | bytes 589832 | tf_op jit(solution)/shard_map/ppermute | solution.py:257
  9.5 14.5 %collective-permute-start.1 = (bf16[3,8,32,128]{3,2,1,0:T(8,128)(2,1)S(1)}, bf16[3,8,32,128]{3,2,1,0:T(8,128)(2,1)S(1)}, u32[]{:S(2)}, u32[]{:S(2)}) collective-permute-start(bf16[3,8,32,128]{3,2,1,0:T(8,128)(2,1)S(1)} %get-tuple-element.18.low_ref), channel_id=1, source_target_pairs={{16,0},{32,16},{48,32},{64,48},{80,64},{96,80},{112,96},{128,112},... | collective-permute-start | bytes 589832 | tf_op jit(solution)/shard_map/ppermute | solution.py:258
  20.5 0.7 copy-start.8
  21.2 0.7 copy-start.10
  23.9 9.4 %copy-start.4 = (bf16[4,8,128]{2,1,0:T(8,128)(2,1)S(1)}, bf16[4,8,128]{2,1,0:T(8,128)(2,1)}, u32[]{:S(2)}) copy-start(bf16[4,8,128]{2,1,0:T(8,128)(2,1)} %constant.7.clone.pick_ref) | copy-start | bytes 24580
  23.9 7.2 %collective-permute-start.2 = (bf16[19,32,128]{2,1,0:T(8,128)(2,1)S(1)}, bf16[19,32,128]{2,1,0:T(8,128)(2,1)S(1)}, u32[]{:S(2)}, u32[]{:S(2)}) collective-permute-start(bf16[19,32,128]{2,1,0:T(8,128)(2,1)S(1)} %get-tuple-element.21), channel_id=1, source_target_pairs={{0,4},{4,8},{8,12},{12,0},{1,5},{5,9},{9,13},{13,1},{2,6},{6,10},{... | collective-permute-start | bytes 466952 | tf_op jit(solution)/shard_map/ppermute | solution.py:270
  27.1 6.3 %collective-permute-start.3 = (bf16[19,32,128]{2,1,0:T(8,128)(2,1)S(1)}, bf16[19,32,128]{2,1,0:T(8,128)(2,1)S(1)}, u32[]{:S(2)}, u32[]{:S(2)}) collective-permute-start(bf16[19,32,128]{2,1,0:T(8,128)(2,1)S(1)} %get-tuple-element.22), channel_id=1, source_target_pairs={{4,0},{8,4},{12,8},{0,12},{5,1},{9,5},{13,9},{1,13},{6,2},{10,6},{... | collective-permute-start | bytes 466952 | tf_op jit(solution)/shard_map/ppermute | solution.py:271
  34.0 8.2 %collective-permute-start.4 = (bf16[8,4288]{1,0:T(8,128)(2,1)S(1)}, bf16[8,4288]{1,0:T(8,128)(2,1)S(1)}, u32[]{:S(2)}, u32[]{:S(2)}) collective-permute-start(bf16[8,4288]{1,0:T(8,128)(2,1)S(1)} %get-tuple-element.25), channel_id=1, source_target_pairs={{0,1},{1,2},{2,3},{3,0},{4,5},{5,6},{6,7},{7,4},{8,9},{9,10},{10,1... | collective-permute-start | bytes 205832 | tf_op jit(solution)/shard_map/ppermute | solution.py:282
  38.9 5.6 %collective-permute-start.5 = (bf16[8,4288]{1,0:T(8,128)(2,1)S(1)}, bf16[8,4288]{1,0:T(8,128)(2,1)S(1)}, u32[]{:S(2)}, u32[]{:S(2)}) collective-permute-start(bf16[8,4288]{1,0:T(8,128)(2,1)S(1)} %get-tuple-element.26), channel_id=1, source_target_pairs={{1,0},{2,1},{3,2},{0,3},{5,4},{6,5},{7,6},{4,7},{9,8},{10,9},{11,1... | collective-permute-start | bytes 205832 | tf_op jit(solution)/shard_map/ppermute | solution.py:283
  41.5 0.7 copy-start.11
  42.1 2.4 %copy-start.5 = (bf16[4,8,128]{2,1,0:T(8,128)(2,1)S(1)}, bf16[4,8,128]{2,1,0:T(8,128)(2,1)}, u32[]{:S(2)}) copy-start(bf16[4,8,128]{2,1,0:T(8,128)(2,1)} %constant.24.clone.place_ref) | copy-start | bytes 24580
  42.1 2.4 %copy-start.6 = (f32[1,1408]{1,0:T(1,128)S(1)}, f32[1,1408]{1,0:T(1,128)}, u32[]{:S(2)}) copy-start(f32[1,1408]{1,0:T(1,128)} %constant.25.clone.mask_ref) | copy-start | bytes 16900
  100.2 11.4 %all-to-all-start.2 = ((f32[16,16,128]{2,1,0:T(8,128)}), f32[16,16,128]{2,1,0:T(8,128)S(1)}, u32[]{:S(2)}, u32[]{:S(2)}) async-start(f32[16,16,128]{2,1,0:T(8,128)} %broadcast_in_dim.8), calls=%async_computation.2 | async-start | bytes 262144 | tf_op jit(solution)/shard_map/all_to_all | solution.py:246

commit v2 on v1

v2 whole, which is shorter than its diff:
```python
import numpy as np
import jax
import jax.numpy as jnp
from jax import lax
from jax.experimental import pallas as pl
from jax.experimental.pallas import tpu as pltpu
from jax.sharding import Mesh, PartitionSpec as P

demod_eps = 1e-06
clip_eps = 1e-06

C = 32
TAPS = 27
PITCH = 132
PLANE = 14 * 128
OUT = 11 * 128
GRAD = 9 * 128
FIELD_ROWS = 7 * 12 * C
COT_ROWS = 5 * 10 * C
f32 = jnp.float32
bf16 = jnp.bfloat16
VMEM = pl.BlockSpec(memory_space=pltpu.VMEM)


def call(kernel, outs, n_in, flops=0, limit=40):
    return pl.pallas_call(
        kernel,
        out_shape=outs,
        in_specs=[VMEM] * n_in,
        out_specs=[VMEM] * len(outs),
        cost_estimate=pl.CostEstimate(flops=flops, bytes_accessed=1 << 20, transcendentals=0),
        compiler_params=pltpu.CompilerParams(vmem_limit_bytes=limit * 1024 * 1024),
    )


def shape(*dims, dtype=bf16):
    return jax.ShapeDtypeStruct(dims, dtype)


def select(dims, row_axis, lane_axis, lanes):
    row = lax.broadcasted_iota(jnp.int32, dims, row_axis)
    lane = lax.broadcasted_iota(jnp.int32, dims, lane_axis)
    hit = jnp.zeros(dims, f32)
    for n, at in enumerate(lanes):
        if at is not None:
            hit = jnp.where((row == n) & (lane == at), 1.0, hit)
    return hit.astype(bf16)


def split_kernel(field_hbm, cot_hbm, low_ref, high_ref, mid_ref, field_ref, cot_ref, sems):
    fetches = (
        pltpu.make_async_copy(field_hbm, field_ref, sems.at[0]),
        pltpu.make_async_copy(cot_hbm, cot_ref, sems.at[1]),
    )
    for fetch in fetches:
        fetch.start()
    to = lax.broadcasted_iota(jnp.int32, (256, 256), 0)
    of = lax.broadcasted_iota(jnp.int32, (256, 256), 1)
    perm = jnp.where((of & 7) * C + (of >> 3) == to, 1.0, 0.0).astype(bf16)

    def rows(ref, x):
        block = ref[:, x].astype(f32).reshape(C * 8, 128).astype(bf16)
        return jnp.dot(perm, block, preferred_element_type=f32).astype(bf16).reshape(8, C, 128)

    fetches[0].wait()
    f0, f1, f2 = (rows(field_ref, x) for x in range(3))
    low_ref[0], low_ref[1] = f0, f1
    high_ref[0], high_ref[1] = f1, f2
    fetches[1].wait()
    c0, c1, c2 = (rows(cot_ref, x) for x in range(3))
    low_ref[2], high_ref[2], mid_ref[0] = c0, c2, c1


def planes(low_ref, high_ref, mid_ref, left_ref, right_ref):
    field = (
        (left_ref, 0), (left_ref, 1), (low_ref, 0), (low_ref, 1), (high_ref, 1), (right_ref, 0), (right_ref, 1),
    )
    cot = ((left_ref, 2), (low_ref, 2), (mid_ref, 0), (high_ref, 2), (right_ref, 2))
    return field, cot


def pack_kernel(low_ref, high_ref, mid_ref, left_ref, right_ref, up_ref, down_ref):
    field, cot = planes(low_ref, high_ref, mid_ref, left_ref, right_ref)
    for n, (ref, at) in enumerate(field):
        up_ref[2 * n : 2 * n + 2] = ref[at, 6:8]
        down_ref[2 * n : 2 * n + 2] = ref[at, 0:2]
    for n, (ref, at) in enumerate(cot):
        up_ref[14 + n] = ref[at, 7]
        down_ref[14 + n] = ref[at, 0]


def gather_kernel(
    low_ref, high_ref, mid_ref, left_ref, right_ref, up_ref, down_ref, field_out, cot_out, faces_ref
):
    field, cot = planes(low_ref, high_ref, mid_ref, left_ref, right_ref)
    for n, (ref, at) in enumerate(field):
        field_out[n, 0:2] = up_ref[2 * n : 2 * n + 2]
        field_out[n, 2:10] = ref[at]
        field_out[n, 10:12] = down_ref[2 * n : 2 * n + 2]
    for n, (ref, at) in enumerate(cot):
        cot_out[n, 0] = up_ref[14 + n]
        cot_out[n, 1:9] = ref[at]
        cot_out[n, 9] = down_ref[14 + n]

    def faces(lanes, rows):
        pick = select((8, 128), 0, 1, lanes)
        return lax.dot_general(
            pick, rows, (((1,), (1,)), ((), ())), preferred_element_type=f32
        )

    both = faces((126, 127, 0, 1), field_out[...].reshape(FIELD_ROWS, 128))
    beside = faces((None, None, None, None, 127, 0), cot_out[...].reshape(COT_ROWS, 128))
    both = jnp.concatenate([both[:, :COT_ROWS] + beside, both[:, COT_ROWS:]], axis=1).astype(bf16)
    for n in range(4):
        faces_ref[n] = both


def silu_slope(values):
    logistic = jax.nn.sigmoid(values)
    return logistic * (1.0 + values * (1.0 - logistic))


def conv_kernel(
    field_ref, cot_ref, faces_ref, fwd_ref, bwd_ref, offset_ref,
    grad_ref, sums_ref,
    edge, plane, cols, up, ucols, total,
):
    me = lax.axis_index("gz")
    before, after = lax.rem(me + 3, 4), lax.rem(me + 1, 4)

    def placed(lanes_before, lanes_after, count):
        return sum(
            lax.dot_general(
                faces_ref[at, :, :count], select((8, 128), 0, 1, lanes),
                (((0,), (0,)), ((), ())), preferred_element_type=f32,
            )
            for at, lanes in ((before, lanes_before), (after, lanes_after))
        ).astype(bf16)

    none = (None,) * 4
    edge[:FIELD_ROWS] = placed((0, 1), (None, None, 2, 3), FIELD_ROWS)
    edge[FIELD_ROWS:] = placed(none + (0,), none + (None, 1), COT_ROWS)
    lane = lax.broadcasted_iota(jnp.int32, (1, OUT), 1)
    own_lanes = jnp.zeros((1, OUT), f32)
    for y in range(1, 9):
        own_lanes = jnp.where((lane > y * PITCH) & (lane <= y * PITCH + 128), 1.0, own_lanes)

    @pl.loop(0, 7)
    def _(x):
        pieces = []
        for y in range(12):
            sides = edge[pl.ds(pl.multiple_of((x * 12 + y) * C, C), C), :]
            pieces += [sides[:, 0:2], field_ref[x, y], sides[:, 2:4]]
        plane[...] = jnp.concatenate(
            pieces + [jnp.zeros((C, PLANE - 12 * PITCH), bf16)], axis=1
        )
        for t in range(9):
            at = (t // 3) * PITCH + t % 3
            cols[x, t * C : (t + 1) * C, :] = plane[:, at : at + OUT]

    total[...] = jnp.zeros_like(total)

    @pl.loop(0, 5)
    def _(x):
        pieces = []
        for y in range(10):
            sides = edge[pl.ds(pl.multiple_of(FIELD_ROWS + (x * 10 + y) * C, C), C), :]
            pieces += [sides[:, 0:1], cot_ref[x, y], sides[:, 1:2], jnp.zeros((C, 2), bf16)]
        pieces.append(jnp.zeros((C, OUT - 10 * PITCH), bf16))
        beside = jnp.concatenate(pieces, axis=1).astype(f32)
        block = cols[pl.ds(x, 3)].reshape(3 * 9 * C, OUT)
        preact = jnp.dot(fwd_ref[...], block, preferred_element_type=f32) + offset_ref[...]
        upstream = (beside * silu_slope(preact)).astype(bf16)
        up[:, :OUT] = upstream
        up[:, OUT:] = jnp.zeros((C, 128), bf16)
        for t in range(9):
            at = (t // 3) * PITCH + t % 3
            ucols[x, t * C : (t + 1) * C, :] = up[:, at : at + GRAD]

        @pl.when((x >= 1) & (x <= 3))
        def _():
            own = upstream.astype(f32) * own_lanes
            total[:, 864:] += jnp.sum(own, axis=1, keepdims=True)
            total[:, :864] += lax.dot_general(
                own.astype(bf16), block, (((1,), (1,)), ((), ())), preferred_element_type=f32
            )

    for s in range(4):
        for l in range(8):
            at = (s * 8 + l) * 8
            if l < 7:
                sums_ref[at : at + 8] = total[8 * s : 8 * s + 8, 128 * l : 128 * l + 128]
            else:
                sums_ref[at : at + 8] = jnp.zeros((8, 128), f32)

    @pl.loop(0, 3)
    def _(x):
        block = ucols[pl.ds(x, 3)].reshape(3 * 9 * C, GRAD)
        grad = jnp.dot(bwd_ref[...], block, preferred_element_type=f32).astype(bf16)
        for y in range(8):
            grad_ref[x, y] = grad[:, y * PITCH : y * PITCH + 128]


def tail_kernel(
    sums_ref, kernel_ref, modded_ref, styles_ref, inv_ref, lifted_ref, hidden_ref, weight_ref, cosmology_ref,
    kernel_out, offset_out, lift_out, bias_out, style_out, sbias_out,
):
    def total(values):
        return jnp.sum(jnp.sum(values, axis=1, keepdims=True), axis=0, keepdims=True)

    sums = jnp.concatenate(
        [
            jnp.concatenate([sums_ref[(s * 8 + l) * 8 : (s * 8 + l) * 8 + 8] for s in range(4)], axis=0)
            for l in range(7)
        ],
        axis=1,
    )
    kernel, modded, styles, inv = kernel_ref[...], modded_ref[...], styles_ref[...], inv_ref[...]
    eye = jnp.where(
        lax.broadcasted_iota(jnp.int32, (C, C), 0) == lax.broadcasted_iota(jnp.int32, (C, C), 1), 1.0, 0.0
    )
    offset = jnp.sum(sums[:, TAPS * C : TAPS * C + C] * eye, axis=0, keepdims=True)
    projected = jnp.sum(sums * modded, axis=1, keepdims=True)
    mod_grad = inv * (sums - modded * (inv * inv * projected))
    raw = mod_grad * styles
    lanes = jnp.sum(mod_grad * kernel, axis=0, keepdims=True)
    folded = sum(lanes[:, 128 * l : 128 * l + 128] for l in range(7))
    row = sum(folded[:, C * n : C * n + C] for n in range(4))
    column = jnp.sum(row * eye, axis=1, keepdims=True)
    lifted_grad = jnp.sum(weight_ref[...] * column, axis=0, keepdims=True) * silu_slope(lifted_ref[...])
    style_raw = column * hidden_ref[...]
    lift_raw = cosmology_ref[...] * lifted_grad
    squares = sum(total(v * v) for v in (raw, offset, lift_raw, lifted_grad, style_raw, row))
    entries = TAPS * C * C + C + lift_raw.size + lifted_grad.size + style_raw.size + C
    factor = jnp.minimum(1.0, lax.rsqrt(squares / entries + clip_eps))
    raw = raw * factor
    for t in range(TAPS):
        kernel_out[t] = raw[:, C * t : C * t + C]
    offset_out[...] = offset * factor
    lift_out[...] = lift_raw * factor
    bias_out[...] = lifted_grad * factor
    style_out[...] = style_raw * factor
    sbias_out[...] = row * factor


def shifts(axis):
    n = lax.axis_size(axis)
    ahead = [(i, (i + 1) % n) for i in range(n)]
    return ahead, [(j, i) for i, j in ahead]


def modulate(cosmology, lift_weight, lift_bias, style_weight, style_bias, kernel):
    lifted = (
        jnp.dot(cosmology[None, :], lift_weight, precision=lax.Precision.HIGHEST)[0] + lift_bias
    )
    hidden = jax.nn.silu(lifted)
    styles = (
        jnp.dot(hidden[None, :], style_weight, precision=lax.Precision.HIGHEST)[0]
        + style_bias
        + 1.0
    )
    modded = kernel * styles[None, None, :]
    inv_norm = lax.rsqrt(jnp.sum(modded * modded, axis=(0, 2)) + demod_eps)
    scaled = (modded * inv_norm[None, :, None]).astype(bf16)
    return (lifted, hidden, styles, modded, inv_norm, scaled)


def summed(sums):
    flat = ("ghi", "gy", "gz")
    part = jnp.sum(lax.all_to_all(sums.reshape(32, 8, 128), flat, 0, 0, tiled=True), axis=0)
    spread = jnp.broadcast_to(part[None], (16, 8, 128))
    part = jnp.sum(lax.all_to_all(spread, "glong", 0, 0, tiled=True), axis=0)
    spread = jnp.broadcast_to(part[None], (32, 8, 128))
    return lax.all_to_all(spread, flat, 0, 0, tiled=True).reshape(256, 128)


def body(
    field, cotangent, cosmology, lift_weight, lift_bias, style_weight, style_bias, kernel, offset
):
    low, high, mid = pl.pallas_call(
        split_kernel,
        out_shape=[shape(3, 8, C, 128), shape(3, 8, C, 128), shape(1, 8, C, 128)],
        in_specs=[pl.BlockSpec(memory_space=pltpu.HBM)] * 2,
        out_specs=[VMEM] * 3,
        scratch_shapes=[
            pltpu.VMEM((C, 3, 8, 128), bf16), pltpu.VMEM((C, 3, 8, 128), bf16), pltpu.SemaphoreType.DMA((2,)),
        ],
    )(field, cotangent)
    ahead, back = shifts(("glong", "ghi"))
    left = lax.ppermute(high, ("glong", "ghi"), ahead)
    right = lax.ppermute(low, ("glong", "ghi"), back)

    taps = jnp.transpose(kernel, (2, 3, 4, 0, 1)).reshape(TAPS, C, C)
    lifted, hidden, styles, modded, inv_norm, scaled = modulate(
        cosmology, lift_weight, lift_bias, style_weight, style_bias, taps
    )
    fwd = jnp.transpose(scaled, (1, 0, 2)).reshape(C, TAPS * C)
    bwd = jnp.transpose(scaled[::-1], (2, 0, 1)).reshape(C, TAPS * C)

    rows = (low, high, mid, left, right)
    up, down = call(pack_kernel, [shape(19, C, 128), shape(19, C, 128)], 5)(*rows)
    ahead, back = shifts("gy")
    up = lax.ppermute(up, "gy", ahead)
    down = lax.ppermute(down, "gy", back)

    field_rows, cot_rows, faces = call(
        gather_kernel, [shape(7, 12, C, 128), shape(5, 10, C, 128), shape(4, 8, FIELD_ROWS)], 7
    )(*rows, up, down)
    faces = lax.all_to_all(faces, "gz", 0, 0, tiled=True)

    grad_rows, sums = pl.pallas_call(
        conv_kernel,
        out_shape=[shape(3, 8, C, 128), shape(256, 128, dtype=f32)],
        in_specs=[VMEM] * 6,
        out_specs=[VMEM] * 2,
        scratch_shapes=[
            pltpu.VMEM((FIELD_ROWS + COT_ROWS, 128), bf16),
            pltpu.VMEM((C, PLANE), bf16),
            pltpu.VMEM((7, 9 * C, OUT), bf16),
            pltpu.VMEM((C, OUT + 128), bf16),
            pltpu.VMEM((5, 9 * C, GRAD), bf16),
            pltpu.VMEM((C, 896), f32),
        ],
        cost_estimate=pl.CostEstimate(flops=700_000_000, bytes_accessed=4 << 20, transcendentals=0),
        compiler_params=pltpu.CompilerParams(vmem_limit_bytes=48 * 1024 * 1024),
    )(field_rows, cot_rows, faces, fwd, bwd, offset[:, None])
    grad_field = jnp.transpose(grad_rows, (2, 0, 1, 3))

    packed = jnp.pad(jnp.transpose(taps, (1, 0, 2)).reshape(C, TAPS * C), ((0, 0), (0, C)))
    styles_row = jnp.pad(jnp.tile(styles, TAPS), (0, C))[None, :]
    kernel_out, grad_offset, grad_lift, grad_liftbias, grad_style, grad_stylebias = call(
        tail_kernel,
        [
            shape(TAPS, C, C, dtype=f32), shape(1, C, dtype=f32), shape(2, 256, dtype=f32),
            shape(1, 256, dtype=f32), shape(C, 256, dtype=f32), shape(1, C, dtype=f32),
        ],
        9,
    )(
        summed(sums), packed, packed * styles_row, styles_row, inv_norm[:, None], lifted[None, :],
        hidden[None, :], style_weight.T, cosmology[:, None],
    )
    grad_kernel = jnp.transpose(kernel_out.reshape(3, 3, 3, C, C), (3, 4, 0, 1, 2))
    return (
        grad_field, grad_kernel, grad_offset[0], grad_lift, grad_liftbias[0], grad_style.T, grad_stylebias[0],
    )


def solution(mesh):
    cut = Mesh(mesh.devices.reshape(16, 2, 4, 4), ("glong", "ghi", "gy", "gz"))
    grid = P(None, ("glong", "ghi"), "gy", "gz")
    return jax.shard_map(
        body, mesh=cut, in_specs=(grid,) * 2 + (P(),) * 7, out_specs=(grid,) + (P(),) * 6, check_vma=False
    )
```

time: 125 us -> 107 us (0.86)
  blocking collectives: 44.4 us -> 13.3 us
  starting transfers between devices: 35 us -> 45.5 us
  waiting for transfers between devices: 12.4 us -> 21.5 us
  other arithmetic: 9.14 us -> 2.23 us
  between operations: 4.77 us -> 0.89 us
  Pallas kernels: 11.6 us -> 15.3 us
    all_to_all x2 -> x1, blocking collectives: 44.4 us -> 13.3 us  [summed(): lax.all_to_all(sums.reshape(32, 8, 128), flat, 0, 0, tiled=True)]
    all_to_all x1 -> x3, starting transfers between devices: 5.2 us -> 22.5 us  [the longest x1 11.2 us: summed(): part = jnp.sum(lax.all_to_all(spread, 'glong', 0, 0, tiled=True), axis=0)]
    all_to_all x1 -> x3, waiting for transfers between devices: 5.47 us -> 19.8 us  [the longest x1 10.2 us: summed(): part = jnp.sum(lax.all_to_all(spread, 'glong', 0, 0, tiled=True), axis=0)]
    ppermute x4 -> x2, starting transfers between devices: 23.3 us -> 16.5 us  [the longest x1 10.8 us: body(): right = lax.ppermute(low, ('glong', 'ghi'), back)]
    reduce_sum x9 -> x2, other arithmetic: 4.64 us -> 0.05 us  [the longest x1 0.04 us: summed(): jnp.sum(lax.all_to_all(sums.reshape(32, 8, 128), flat, 0, 0, tiled=True),...]
    mul x7 -> x1, other arithmetic: 4.18 us -> 0.02 us  [body(): packed * styles_row]
    ppermute x4 -> x2, waiting for transfers between devices: 4.09 us -> 0.01 us  [the longest x1 0.01 us: body(): left = lax.ppermute(high, ('glong', 'ghi'), ahead)]
    pallas_call x2 -> x3, Pallas kernels: 1.06 us -> 4.74 us  [the longest x1 2.25 us: body(): pl.pallas_call(split_kernel, out_shape=[shape(3, 8, C, 128), shape(3, 8,...]
  transfers between devices with their start and end apart: 7 -> 7, of which waited for: 6 -> 4; matrix products, arithmetic and copies ran while one was open for 2% -> 7% of each run, Pallas kernels for 0% -> 0%
where the time goes in v2:
time: 107 us
  starting transfers between devices  45.5 us (43%)
  waiting for transfers between devices  21.5 us (20%)
  Pallas kernels  15.3 us (14%)
  blocking collectives  13.3 us (12%)
  local copies, waits for them, and re-layouts  6.4 us (6%)
  other arithmetic  2.23 us (2%)
  matrix products  1.58 us (1%)
    all_to_all x1, blocking collectives, summed(): lax.all_to_all(sums.reshape(32, 8, 128), flat, 0, 0, tiled=True)  13.3 us
    all_to_all x1, starting transfers between devices, summed(): part = jnp.sum(lax.all_to_all(spread, 'glong', 0, 0, tiled=True), axis=0)  11.2 us
    ppermute x1, starting transfers between devices, body(): right = lax.ppermute(low, ('glong', 'ghi'), back)  10.8 us
    pallas_call x1, Pallas kernels, body(): pl.pallas_call(conv_kernel, out_shape=[shape(3, 8, C, 128), shape(256, 12...  10.6 us
    all_to_all x1, waiting for transfers between devices, summed(): part = jnp.sum(lax.all_to_all(spread, 'glong', 0, 0, tiled=True), axis=0)  10.2 us
    all_to_all x1, waiting for transfers between devices, summed(): return lax.all_to_all(spread, flat, 0, 0, tiled=True).reshape(256, 128)  7.02 us
    all_to_all x1, starting transfers between devices, summed(): return lax.all_to_all(spread, flat, 0, 0, tiled=True).reshape(256, 128)  5.7 us
    ppermute x1, starting transfers between devices, body(): left = lax.ppermute(high, ('glong', 'ghi'), ahead)  5.66 us
  transfers between devices with their start and end apart: 7, of which 4 were waited for; matrix products, arithmetic and copies ran while one was open for 7% of the time, Pallas kernels for 0%

profile of v2, /device:TPU:1, one launch (start us, length us, event | category | flops | bytes accessed | tf_op | source)
XLA Modules:
  0.0 106.8 jit_solution(12472595030684891187)
XLA Ops:
  0.7 2.3 %shard_map.144 = (bf16[3,8,32,128]{3,2,1,0:T(8,128)(2,1)}, bf16[3,8,32,128]{3,2,1,0:T(8,128)(2,1)}, bf16[1,8,32,128]{3,2,1,0:T(8,128)(2,1)}) custom-call(bf16[32,3,8,128]{3,2,1,0:T(8,128)(2,1)} %field_hbm.1, bf16[32,3,8,128]{3,2,1,0:T(8,128)(2,1)} %cot_hbm.1), custom_call_target="tpu_custom_call" | custom-call | tf_op jit(solution)/shard_map/pallas_call | solution.py:280
  2.9 5.7 %collective-permute-start = (bf16[3,8,32,128]{3,2,1,0:T(8,128)(2,1)}, bf16[3,8,32,128]{3,2,1,0:T(8,128)(2,1)S(1)}, u32[]{:S(2)}, u32[]{:S(2)}) collective-permute-start(bf16[3,8,32,128]{3,2,1,0:T(8,128)(2,1)} %get-tuple-element.24.high_ref), channel_id=1, source_target_pairs={{0,16},{16,32},{32,48},{48,64},{64,80},{80,96},{96,112},{112,128},... | collective-permute-start | bytes 589832 | tf_op jit(solution)/shard_map/ppermute | solution.py:290
  8.6 10.8 %collective-permute-start.1 = (bf16[3,8,32,128]{3,2,1,0:T(8,128)(2,1)}, bf16[3,8,32,128]{3,2,1,0:T(8,128)(2,1)S(1)}, u32[]{:S(2)}, u32[]{:S(2)}) collective-permute-start(bf16[3,8,32,128]{3,2,1,0:T(8,128)(2,1)} %get-tuple-element.23.low_ref), channel_id=1, source_target_pairs={{16,0},{32,16},{48,32},{64,48},{80,64},{96,80},{112,96},{128,112},... | collective-permute-start | bytes 589832 | tf_op jit(solution)/shard_map/ppermute | solution.py:291
  19.5 0.8 fusion.4
  20.2 0.7 divide_multiply_fusion
  20.9 0.8 fusion.1
  21.7 1.2 %fusion.3 = f32[32]{0:T(128)S(1)} fusion(f32[32,32,3,3,3]{1,0,4,3,2:T(8,128)} %param.16, f32[32]{0:T(128)S(1)} %fusion.1), kind=kLoop, calls=%fused_computation.7 | loop fusion | flops 82912 | bytes 110848 | tf_op jit(solution)/shard_map/reduce_sum | solution.py:263
  24.0 3.1 %collective-permute-start.2 = (bf16[19,32,128]{2,1,0:T(8,128)(2,1)S(1)}, bf16[19,32,128]{2,1,0:T(8,128)(2,1)S(1)}, u32[]{:S(2)}, u32[]{:S(2)}) collective-permute-start(bf16[19,32,128]{2,1,0:T(8,128)(2,1)S(1)} %get-tuple-element.26), channel_id=1, source_target_pairs={{0,4},{4,8},{8,12},{12,0},{1,5},{5,9},{9,13},{13,1},{2,6},{6,10},{... | collective-permute-start | bytes 466952 | tf_op jit(solution)/shard_map/ppermute | solution.py:303
  27.1 3.4 %collective-permute-start.3 = (bf16[19,32,128]{2,1,0:T(8,128)(2,1)S(1)}, bf16[19,32,128]{2,1,0:T(8,128)(2,1)S(1)}, u32[]{:S(2)}, u32[]{:S(2)}) collective-permute-start(bf16[19,32,128]{2,1,0:T(8,128)(2,1)S(1)} %get-tuple-element.27), channel_id=1, source_target_pairs={{4,0},{8,4},{12,8},{0,12},{5,1},{9,5},{13,9},{1,13},{6,2},{10,6},{... | collective-permute-start | bytes 466952 | tf_op jit(solution)/shard_map/ppermute | solution.py:304
  31.5 1.7 %collective-permute-done.3.down_ref = bf16[19,32,128]{2,1,0:T(8,128)(2,1)S(1)} collective-permute-done((bf16[19,32,128]{2,1,0:T(8,128)(2,1)S(1)}, bf16[19,32,128]{2,1,0:T(8,128)(2,1)S(1)}, u32[]{:S(2)}, u32[]{:S(2)}) %collective-permute-start.3) | collective-permute-done | bytes 155680 | tf_op jit(solution)/shard_map/ppermute | solution.py:304
  33.2 1.1 %shard_map.146 = (bf16[7,12,32,128]{3,2,1,0:T(8,128)(2,1)S(1)}, bf16[5,10,32,128]{3,2,1,0:T(8,128)(2,1)S(1)}, bf16[4,8,2688]{2,1,0:T(8,128)(2,1)}) custom-call(bf16[3,8,32,128]{3,2,1,0:T(8,128)(2,1)S(1)} %copy-done.1, bf16[3,8,32,128]{3,2,1,0:T(8,128)(2,1)S(1)} %copy-done.2, bf16[1,8,32,128]{3,2,1,0:T(8,128)(2,1)S(1)} %copy-done.3, ...), custom_call_target="tpu_custom_call" | custom-call | bytes 1048576 | tf_op jit(solution)/shard_map/pallas_call | solution.py:306
  34.3 5.6 %all-to-all-start = ((bf16[4,8,2688]{2,1,0:T(8,128)(2,1)}), bf16[4,8,2688]{2,1,0:T(8,128)(2,1)S(1)}, u32[]{:S(2)}, u32[]{:S(2)}) async-start(bf16[4,8,2688]{2,1,0:T(8,128)(2,1)} %get-tuple-element.30), calls=%async_computation | async-start | bytes 344064 | tf_op jit(solution)/shard_map/all_to_all | solution.py:309
  40.5 0.6 copy-done.6
  41.3 2.6 %all-to-all-done.faces_ref = bf16[4,8,2688]{2,1,0:T(8,128)(2,1)S(1)} async-done(((bf16[4,8,2688]{2,1,0:T(8,128)(2,1)}), bf16[4,8,2688]{2,1,0:T(8,128)(2,1)S(1)}, u32[]{:S(2)}, u32[]{:S(2)}) %all-to-all-start) | async-done | bytes 172064 | tf_op jit(solution)/shard_map/all_to_all | solution.py:309
  43.9 10.6 %shard_map.147 = (bf16[3,8,32,128]{3,2,1,0:T(8,128)(2,1)S(1)}, f32[256,128]{1,0:T(8,128)S(1)}) custom-call(bf16[7,12,32,128]{3,2,1,0:T(8,128)(2,1)S(1)} %get-tuple-element.28.field_ref, bf16[5,10,32,128]{3,2,1,0:T(8,128)(2,1)S(1)} %get-tuple-element.29.cot_ref, bf16[4,8,2688]{2,1,0:T(8,128)(2,1)S(1)} %all-to-all-done.faces_ref, ...), custom_call_target="tpu_custom_call" | custom-call | flops 700000000 | bytes 4194304 | tf_op jit(solution)/shard_map/pallas_call | solution.py:311
  54.4 13.3 %all_to_all.20 = f32[32,8,128]{2,1,0:T(8,128)S(1)} all-to-all(f32[32,8,128]{2,1,0:T(8,128)S(1)} %bitcast.48), channel_id=1, replica_groups=mesh['glong'=16,'ghi'=2,'gy'=4,'gz'=4] {'ghi','gy','gz'}, dimensions={0} | all-to-all | bytes 262144 | tf_op jit(solution)/shard_map/all_to_all | solution.py:270
  68.4 11.2 %all-to-all-start.2 = ((f32[16,8,128]{2,1,0:T(8,128)}), f32[16,8,128]{2,1,0:T(8,128)S(1)}, u32[]{:S(2)}, u32[]{:S(2)}) async-start(f32[16,8,128]{2,1,0:T(8,128)} %broadcast_in_dim.15), calls=%async_computation.2 | async-start | bytes 131072 | tf_op jit(solution)/shard_map/all_to_all | solution.py:272
  80.3 0.7 copy-done.7
  81.1 10.2 %all-to-all-done.2 = f32[16,8,128]{2,1,0:T(8,128)S(1)} async-done(((f32[16,8,128]{2,1,0:T(8,128)}), f32[16,8,128]{2,1,0:T(8,128)S(1)}, u32[]{:S(2)}, u32[]{:S(2)}) %all-to-all-start.2) | async-done | bytes 65568 | tf_op jit(solution)/shard_map/all_to_all | solution.py:272
  91.2 0.7 broadcast_in_dim.16
  91.9 5.7 %all-to-all-start.3 = ((f32[32,8,128]{2,1,0:T(8,128)}), f32[32,8,128]{2,1,0:T(8,128)S(1)}, u32[]{:S(2)}, u32[]{:S(2)}) async-start(f32[32,8,128]{2,1,0:T(8,128)} %broadcast_in_dim.16), calls=%async_computation.3 | async-start | bytes 262144 | tf_op jit(solution)/shard_map/all_to_all | solution.py:274
  97.7 0.8 copy.36
  98.4 7.0 %all-to-all-done.3 = f32[32,8,128]{2,1,0:T(8,128)S(1)} async-done(((f32[32,8,128]{2,1,0:T(8,128)}), f32[32,8,128]{2,1,0:T(8,128)S(1)}, u32[]{:S(2)}, u32[]{:S(2)}) %all-to-all-start.3) | async-done | bytes 131104 | tf_op jit(solution)/shard_map/all_to_all | solution.py:274
  105.4 1.4 %shard_map.148 = (f32[27,32,32]{2,1,0:T(8,128)}, f32[1,32]{1,0:T(1,128)}, f32[2,256]{1,0:T(2,128)}, f32[1,256]{1,0:T(1,128)}, f32[32,256]{1,0:T(8,128)}, /*index=5*/f32[1,32]{1,0:T(1,128)}) custom-call(f32[256,128]{1,0:T(8,128)S(1)} %bitcast.45, f32[32,896]{1,0:T(8,128)S(1)} %get-tuple-element.63.kernel_ref, f32[32,896]{1,0:T(8,128)S(1)} %get-tuple-element.62.modded_ref, ...), custom_call_target="tpu_custom_call" | custom-call | bytes 1048576 | tf_op jit(solution)/shard_map/pallas_call | solution.py:331
  (39 shorter events, 4.0 us)
Async XLA Ops:
  0.6 18.8 %copy-start = (f32[2,256]{1,0:T(2,128)S(1)}, f32[2,256]{1,0:T(2,128)}, u32[]{:S(2)}) copy-start(f32[2,256]{1,0:T(2,128)} %param.12) | copy-start | bytes 6148
  0.6 20.3 %copy-start.4 = (f32[256,32]{0,1:T(8,128)S(1)}, f32[256,32]{0,1:T(8,128)}, u32[]{:S(2)}) copy-start(f32[256,32]{0,1:T(8,128)} %param.14) | copy-start | bytes 98308
  0.7 22.3 %copy-start.5 = (f32[32,32,3,3,3]{1,0,4,3,2:T(8,128)S(1)}, f32[32,32,3,3,3]{1,0,4,3,2:T(8,128)}, u32[]{:S(2)}) copy-start(f32[32,32,3,3,3]{1,0,4,3,2:T(8,128)} %param.16) | copy-start | bytes 331780
  2.9 20.5 %collective-permute-start = (bf16[3,8,32,128]{3,2,1,0:T(8,128)(2,1)}, bf16[3,8,32,128]{3,2,1,0:T(8,128)(2,1)S(1)}, u32[]{:S(2)}, u32[]{:S(2)}) collective-permute-start(bf16[3,8,32,128]{3,2,1,0:T(8,128)(2,1)} %get-tuple-element.24.high_ref), channel_id=1, source_target_pairs={{0,16},{16,32},{32,48},{48,64},{64,80},{80,96},{96,112},{112,128},... | collective-permute-start | bytes 589832 | tf_op jit(solution)/shard_map/ppermute | solution.py:290
  8.6 14.9 %collective-permute-start.1 = (bf16[3,8,32,128]{3,2,1,0:T(8,128)(2,1)}, bf16[3,8,32,128]{3,2,1,0:T(8,128)(2,1)S(1)}, u32[]{:S(2)}, u32[]{:S(2)}) collective-permute-start(bf16[3,8,32,128]{3,2,1,0:T(8,128)(2,1)} %get-tuple-element.23.low_ref), channel_id=1, source_target_pairs={{16,0},{32,16},{48,32},{64,48},{80,64},{96,80},{112,96},{128,112},... | collective-permute-start | bytes 589832 | tf_op jit(solution)/shard_map/ppermute | solution.py:291
  23.0 0.9 copy-start.1
  23.0 1.0 copy-start.2
  23.0 1.0 copy-start.3
  24.0 7.5 %collective-permute-start.2 = (bf16[19,32,128]{2,1,0:T(8,128)(2,1)S(1)}, bf16[19,32,128]{2,1,0:T(8,128)(2,1)S(1)}, u32[]{:S(2)}, u32[]{:S(2)}) collective-permute-start(bf16[19,32,128]{2,1,0:T(8,128)(2,1)S(1)} %get-tuple-element.26), channel_id=1, source_target_pairs={{0,4},{4,8},{8,12},{12,0},{1,5},{5,9},{9,13},{13,1},{2,6},{6,10},{... | collective-permute-start | bytes 466952 | tf_op jit(solution)/shard_map/ppermute | solution.py:303
  27.1 6.1 %collective-permute-start.3 = (bf16[19,32,128]{2,1,0:T(8,128)(2,1)S(1)}, bf16[19,32,128]{2,1,0:T(8,128)(2,1)S(1)}, u32[]{:S(2)}, u32[]{:S(2)}) collective-permute-start(bf16[19,32,128]{2,1,0:T(8,128)(2,1)S(1)} %get-tuple-element.27), channel_id=1, source_target_pairs={{4,0},{8,4},{12,8},{0,12},{5,1},{9,5},{13,9},{1,13},{6,2},{10,6},{... | collective-permute-start | bytes 466952 | tf_op jit(solution)/shard_map/ppermute | solution.py:304
  34.3 9.5 %all-to-all-start = ((bf16[4,8,2688]{2,1,0:T(8,128)(2,1)}), bf16[4,8,2688]{2,1,0:T(8,128)(2,1)S(1)}, u32[]{:S(2)}, u32[]{:S(2)}) async-start(bf16[4,8,2688]{2,1,0:T(8,128)(2,1)} %get-tuple-element.30), calls=%async_computation | async-start | bytes 344064 | tf_op jit(solution)/shard_map/all_to_all | solution.py:309
  40.5 0.7 copy-start.6
  68.4 22.8 %all-to-all-start.2 = ((f32[16,8,128]{2,1,0:T(8,128)}), f32[16,8,128]{2,1,0:T(8,128)S(1)}, u32[]{:S(2)}, u32[]{:S(2)}) async-start(f32[16,8,128]{2,1,0:T(8,128)} %broadcast_in_dim.15), calls=%async_computation.2 | async-start | bytes 131072 | tf_op jit(solution)/shard_map/all_to_all | solution.py:272
  80.3 0.7 copy-start.7
  91.9 13.5 %all-to-all-start.3 = ((f32[32,8,128]{2,1,0:T(8,128)}), f32[32,8,128]{2,1,0:T(8,128)S(1)}, u32[]{:S(2)}, u32[]{:S(2)}) async-start(f32[32,8,128]{2,1,0:T(8,128)} %broadcast_in_dim.16), calls=%async_computation.3 | async-start | bytes 262144 | tf_op jit(solution)/shard_map/all_to_all | solution.py:274

commit v3 on v2

--- a/solution.py
+++ b/solution.py
@@ -11,23 +11,23 @@
 
 C = 32
 TAPS = 27
-PITCH = 132
-PLANE = 14 * 128
-OUT = 11 * 128
-GRAD = 9 * 128
-FIELD_ROWS = 7 * 12 * C
-COT_ROWS = 5 * 10 * C
+EDGE = 6
+FIELD_LANES = 12 * 8 * C
+COT_LANES = 10 * 8 * C
+OUT = 10 * 128
+OWN = 8 * 128
 f32 = jnp.float32
 bf16 = jnp.bfloat16
 VMEM = pl.BlockSpec(memory_space=pltpu.VMEM)
 
 
-def call(kernel, outs, n_in, flops=0, limit=40):
+def call(kernel, outs, n_in, flops=0, limit=24, scratch=()):
     return pl.pallas_call(
         kernel,
         out_shape=outs,
         in_specs=[VMEM] * n_in,
         out_specs=[VMEM] * len(outs),
+        scratch_shapes=list(scratch),
         cost_estimate=pl.CostEstimate(flops=flops, bytes_accessed=1 << 20, transcendentals=0),
         compiler_params=pltpu.CompilerParams(vmem_limit_bytes=limit * 1024 * 1024),
     )
@@ -94,13 +94,19 @@
 ):
     field, cot = planes(low_ref, high_ref, mid_ref, left_ref, right_ref)
     for n, (ref, at) in enumerate(field):
-        field_out[n, 0:2] = up_ref[2 * n : 2 * n + 2]
-        field_out[n, 2:10] = ref[at]
-        field_out[n, 10:12] = down_ref[2 * n : 2 * n + 2]
+        for y in range(12):
+            if y < 2:
+                row = up_ref[2 * n + y]
+            elif y < 10:
+                row = ref[at, y - 2]
+            else:
+                row = down_ref[2 * n + y - 10]
+            field_out[y, n] = row
+    field_out[:, 7:] = jnp.zeros((12, 1, C, 128), bf16)
     for n, (ref, at) in enumerate(cot):
-        cot_out[n, 0] = up_ref[14 + n]
-        cot_out[n, 1:9] = ref[at]
-        cot_out[n, 9] = down_ref[14 + n]
+        for y in range(10):
+            cot_out[y, n] = up_ref[14 + n] if y == 0 else down_ref[14 + n] if y == 9 else ref[at, y - 1]
+    cot_out[:, 5:] = jnp.zeros((10, 3, C, 128), bf16)
 
     def faces(lanes, rows):
         pick = select((8, 128), 0, 1, lanes)
@@ -108,9 +114,9 @@
             pick, rows, (((1,), (1,)), ((), ())), preferred_element_type=f32
         )
 
-    both = faces((126, 127, 0, 1), field_out[...].reshape(FIELD_ROWS, 128))
-    beside = faces((None, None, None, None, 127, 0), cot_out[...].reshape(COT_ROWS, 128))
-    both = jnp.concatenate([both[:, :COT_ROWS] + beside, both[:, COT_ROWS:]], axis=1).astype(bf16)
+    both = faces((126, 127, 0, 1), field_out[...].reshape(FIELD_LANES, 128))
+    beside = faces((None, None, None, None, 127, 0), cot_out[...].reshape(COT_LANES, 128))
+    both = jnp.concatenate([both[:, :COT_LANES] + beside, both[:, COT_LANES:]], axis=1).astype(bf16)
     for n in range(4):
         faces_ref[n] = both
 
@@ -121,68 +127,77 @@
 
 
 def conv_kernel(
-    field_ref, cot_ref, faces_ref, fwd_ref, bwd_ref, offset_ref,
-    grad_ref, sums_ref,
-    edge, plane, cols, up, ucols, total,
+    field_ref, cot_ref, faces_ref, fwd_ref, offset_ref, sums_ref, up_ref, rim_ref, halo, shifted, edge, total
 ):
     me = lax.axis_index("gz")
     before, after = lax.rem(me + 3, 4), lax.rem(me + 1, 4)
 
-    def placed(lanes_before, lanes_after, count):
-        return sum(
-            lax.dot_general(
-                faces_ref[at, :, :count], select((8, 128), 0, 1, lanes),
-                (((0,), (0,)), ((), ())), preferred_element_type=f32,
-            )
-            for at, lanes in ((before, lanes_before), (after, lanes_after))
-        ).astype(bf16)
-
-    none = (None,) * 4
-    edge[:FIELD_ROWS] = placed((0, 1), (None, None, 2, 3), FIELD_ROWS)
-    edge[FIELD_ROWS:] = placed(none + (0,), none + (None, 1), COT_ROWS)
-    lane = lax.broadcasted_iota(jnp.int32, (1, OUT), 1)
-    own_lanes = jnp.zeros((1, OUT), f32)
-    for y in range(1, 9):
-        own_lanes = jnp.where((lane > y * PITCH) & (lane <= y * PITCH + 128), 1.0, own_lanes)
+    def across(rows, place):
+        return lax.dot_general(rows, place, (((0,), (0,)), ((), ())), preferred_element_type=f32)
+
+    halo[...] = (
+        across(faces_ref[before], select((8, 128), 0, 1, (None, 0)))
+        + across(faces_ref[after], select((8, 128), 0, 1, (None, None, 127)))
+    ).astype(bf16)
+    lane = lax.broadcasted_iota(jnp.int32, (C, 128), 1)
 
     @pl.loop(0, 7)
     def _(x):
-        pieces = []
         for y in range(12):
-            sides = edge[pl.ds(pl.multiple_of((x * 12 + y) * C, C), C), :]
-            pieces += [sides[:, 0:2], field_ref[x, y], sides[:, 2:4]]
-        plane[...] = jnp.concatenate(
-            pieces + [jnp.zeros((C, PLANE - 12 * PITCH), bf16)], axis=1
-        )
-        for t in range(9):
-            at = (t // 3) * PITCH + t % 3
-            cols[x, t * C : (t + 1) * C, :] = plane[:, at : at + OUT]
+            row = field_ref[y, x]
+            ends = halo[pl.ds(pl.multiple_of((y * 8 + x) * C, C), C), :]
+            at = slice(y * 128, y * 128 + 128)
+            shifted[0, x, :, at] = jnp.where(lane == 0, ends, pltpu.roll(row, 1, 1))
+            shifted[1, x, :, at] = row
+            shifted[2, x, :, at] = jnp.where(lane == 127, ends, pltpu.roll(row, 127, 1))
+
+    def spread(at, count, moves):
+        rows = jnp.concatenate(
+            [faces_ref[at, :, y * 256 : y * 256 + 256].astype(f32) for y in range(count)], axis=0
+        ).astype(bf16)
+        row = lax.broadcasted_iota(jnp.int32, (count * 8, 128), 0)
+        to = lax.broadcasted_iota(jnp.int32, (count * 8, 128), 1)
+        place = jnp.zeros((count * 8, 128), f32)
+        for k, n in moves:
+            place = jnp.where(((row & 7) == k) & (to == (row >> 3) * EDGE + n), 1.0, place)
+        return across(rows, place.astype(bf16))
+
+    rim = spread(before, 12, ((0, 0), (1, 1))) + spread(me, 12, ((2, 2), (1, 3))) + spread(after, 12, ((2, 4), (3, 5)))
+    for t in range(9):
+        shift = (t // 3) * EDGE + t % 3
+        edge[t] = (pltpu.roll(rim, 128 - shift, 1) if shift else rim).astype(bf16)
+    rim_cot = spread(before, 10, ((4, 0),)) + spread(after, 10, ((5, 3),))
+    block = jnp.concatenate(
+        [
+            jnp.concatenate([edge[t, (x + a) * C : (x + a) * C + C] for a in range(3) for t in range(9)], axis=0)
+            for x in range(5)
+        ],
+        axis=1,
+    )
+    preact = jnp.dot(fwd_ref[...], block, preferred_element_type=f32) + offset_ref[...]
+    slope = silu_slope(preact)
+    for x in range(5):
+        rim_ref[x] = (rim_cot[x * C : x * C + C] * slope[:, x * 128 : x * 128 + 128]).astype(bf16)
 
     total[...] = jnp.zeros_like(total)
 
     @pl.loop(0, 5)
     def _(x):
-        pieces = []
-        for y in range(10):
-            sides = edge[pl.ds(pl.multiple_of(FIELD_ROWS + (x * 10 + y) * C, C), C), :]
-            pieces += [sides[:, 0:1], cot_ref[x, y], sides[:, 1:2], jnp.zeros((C, 2), bf16)]
-        pieces.append(jnp.zeros((C, OUT - 10 * PITCH), bf16))
-        beside = jnp.concatenate(pieces, axis=1).astype(f32)
-        block = cols[pl.ds(x, 3)].reshape(3 * 9 * C, OUT)
+        beside = jnp.concatenate([cot_ref[y, x] for y in range(10)], axis=1).astype(f32)
+        block = jnp.concatenate(
+            [shifted[c, x + a, :, b * 128 : b * 128 + OUT] for a in range(3) for b in range(3) for c in range(3)],
+            axis=0,
+        )
         preact = jnp.dot(fwd_ref[...], block, preferred_element_type=f32) + offset_ref[...]
         upstream = (beside * silu_slope(preact)).astype(bf16)
-        up[:, :OUT] = upstream
-        up[:, OUT:] = jnp.zeros((C, 128), bf16)
-        for t in range(9):
-            at = (t // 3) * PITCH + t % 3
-            ucols[x, t * C : (t + 1) * C, :] = up[:, at : at + GRAD]
+        up_ref[x] = upstream
 
         @pl.when((x >= 1) & (x <= 3))
         def _():
-            own = upstream.astype(f32) * own_lanes
-            total[:, 864:] += jnp.sum(own, axis=1, keepdims=True)
+            own = upstream[:, 128 : 128 + OWN]
+            total[:, 864:] += jnp.sum(own.astype(f32), axis=1, keepdims=True)
             total[:, :864] += lax.dot_general(
-                own.astype(bf16), block, (((1,), (1,)), ((), ())), preferred_element_type=f32
+                own, block[:, 128 : 128 + OWN], (((1,), (1,)), ((), ())), preferred_element_type=f32
             )
 
     for s in range(4):
@@ -193,12 +208,30 @@
             else:
                 sums_ref[at : at + 8] = jnp.zeros((8, 128), f32)
 
+
+def grad_kernel_body(up_ref, rim_ref, bwd_ref, grad_ref, shifted):
+    lane = lax.broadcasted_iota(jnp.int32, (C, 128), 1)
+
+    @pl.loop(0, 5)
+    def _(x):
+        rim = rim_ref[x].astype(f32)
+        for y in range(10):
+            at = slice(y * 128, y * 128 + 128)
+            row = up_ref[x, :, at].astype(f32)
+            low, high = rim[:, y * EDGE : y * EDGE + 1], rim[:, y * EDGE + 3 : y * EDGE + 4]
+            shifted[0, x, :, at] = jnp.where(lane == 0, low, pltpu.roll(row, 1, 1)).astype(bf16)
+            shifted[1, x, :, at] = up_ref[x, :, at]
+            shifted[2, x, :, at] = jnp.where(lane == 127, high, pltpu.roll(row, 127, 1)).astype(bf16)
+
     @pl.loop(0, 3)
     def _(x):
-        block = ucols[pl.ds(x, 3)].reshape(3 * 9 * C, GRAD)
+        block = jnp.concatenate(
+            [shifted[c, x + a, :, b * 128 : b * 128 + OWN] for a in range(3) for b in range(3) for c in range(3)],
+            axis=0,
+        )
         grad = jnp.dot(bwd_ref[...], block, preferred_element_type=f32).astype(bf16)
         for y in range(8):
-            grad_ref[x, y] = grad[:, y * PITCH : y * PITCH + 128]
+            grad_ref[x, y] = grad[:, y * 128 : y * 128 + 128]
 
 
 def tail_kernel(
@@ -304,26 +337,29 @@
     down = lax.ppermute(down, "gy", back)
 
     field_rows, cot_rows, faces = call(
-        gather_kernel, [shape(7, 12, C, 128), shape(5, 10, C, 128), shape(4, 8, FIELD_ROWS)], 7
+        gather_kernel, [shape(12, 8, C, 128), shape(10, 8, C, 128), shape(4, 8, FIELD_LANES)], 7
     )(*rows, up, down)
     faces = lax.all_to_all(faces, "gz", 0, 0, tiled=True)
 
-    grad_rows, sums = pl.pallas_call(
+    sums, upstream, rim = call(
         conv_kernel,
-        out_shape=[shape(3, 8, C, 128), shape(256, 128, dtype=f32)],
-        in_specs=[VMEM] * 6,
-        out_specs=[VMEM] * 2,
-        scratch_shapes=[
-            pltpu.VMEM((FIELD_ROWS + COT_ROWS, 128), bf16),
-            pltpu.VMEM((C, PLANE), bf16),
-            pltpu.VMEM((7, 9 * C, OUT), bf16),
-            pltpu.VMEM((C, OUT + 128), bf16),
-            pltpu.VMEM((5, 9 * C, GRAD), bf16),
+        [shape(256, 128, dtype=f32), shape(5, C, OUT), shape(5, C, 128)],
+        5,
+        flops=540_000_000,
+        scratch=[
+            pltpu.VMEM((FIELD_LANES, 128), bf16),
+            pltpu.VMEM((3, 7, C, 12 * 128), bf16),
+            pltpu.VMEM((9, 8 * C, 128), bf16),
             pltpu.VMEM((C, 896), f32),
         ],
-        cost_estimate=pl.CostEstimate(flops=700_000_000, bytes_accessed=4 << 20, transcendentals=0),
-        compiler_params=pltpu.CompilerParams(vmem_limit_bytes=48 * 1024 * 1024),
-    )(field_rows, cot_rows, faces, fwd, bwd, offset[:, None])
+    )(field_rows, cot_rows, faces, fwd, offset[:, None])
+    (grad_rows,) = call(
+        grad_kernel_body,
+        [shape(3, 8, C, 128)],
+        3,
+        flops=170_000_000,
+        scratch=[pltpu.VMEM((3, 5, C, OUT), bf16)],
+    )(upstream, rim, bwd)
     grad_field = jnp.transpose(grad_rows, (2, 0, 1, 3))
 
     packed = jnp.pad(jnp.transpose(taps, (1, 0, 2)).reshape(C, TAPS * C), ((0, 0), (0, C)))

time: 107 us -> 104 us (0.972)
  other arithmetic: 2.23 us -> 0.51 us
  local copies, waits for them, and re-layouts: 6.4 us -> 8.05 us
  Pallas kernels: 15.3 us -> 13.9 us
  matrix products: 1.58 us -> 0.26 us
    all_to_all x1, waiting for transfers between devices: 7.02 us -> 4.05 us  [summed(): return lax.all_to_all(spread, flat, 0, 0, tiled=True).reshape(256, 128)]
    pallas_call x2 -> x3, Pallas kernels: 11.7 us -> 10.3 us  [the longest x1 6.77 us: body(): call(conv_kernel, [shape(256, 128, dtype=f32), shape(5, C, OUT), shape(5,...]
    reshape x2, local copies, waits for them, and re-layouts: 0.73 us -> 1.81 us  [body(): taps = jnp.transpose(kernel, (2, 3, 4, 0, 1)).reshape(TAPS, C, C)]
    unnamed x17 -> x21, local copies, waits for them, and re-layouts: 2.58 us -> 3.15 us
  transfers between devices with their start and end apart: 7 -> 7, of which waited for: 4 -> 6; matrix products, arithmetic and copies ran while one was open for 7% -> 5% of each run, Pallas kernels for 0% -> 2%
where the time goes in v3:
time: 104 us; the launch traced here: 103 us
  starting transfers between devices  45.6 us (44%)
  waiting for transfers between devices  21.1 us (20%)
  Pallas kernels  13.9 us (13%)
  blocking collectives  13.1 us (13%)
  local copies, waits for them, and re-layouts  8.05 us (8%)
    all_to_all x1, blocking collectives, summed(): lax.all_to_all(sums.reshape(32, 8, 128), flat, 0, 0, tiled=True)  13.1 us
    all_to_all x1, starting transfers between devices, summed(): part = jnp.sum(lax.all_to_all(spread, 'glong', 0, 0, tiled=True), axis=0)  11.2 us
    all_to_all x1, waiting for transfers between devices, summed(): part = jnp.sum(lax.all_to_all(spread, 'glong', 0, 0, tiled=True), axis=0)  10.9 us
    ppermute x1, starting transfers between devices, body(): right = lax.ppermute(low, ('glong', 'ghi'), back)  10.8 us
    pallas_call x1, Pallas kernels, body(): call(conv_kernel, [shape(256, 128, dtype=f32), shape(5, C, OUT), shape(5,...  6.77 us
    all_to_all x1, starting transfers between devices, summed(): return lax.all_to_all(spread, flat, 0, 0, tiled=True).reshape(256, 128)  5.7 us
    all_to_all x1, starting transfers between devices, body(): faces = lax.all_to_all(faces, 'gz', 0, 0, tiled=True)  5.68 us
    ppermute x1, starting transfers between devices, body(): left = lax.ppermute(high, ('glong', 'ghi'), ahead)  5.65 us
  transfers between devices with their start and end apart: 7, of which 6 were waited for; matrix products, arithmetic and copies ran while one was open for 5% of the time, Pallas kernels for 2%

profile of v3, /device:TPU:1, one launch (start us, length us, event | category | flops | bytes accessed | tf_op | source)
XLA Modules:
  0.0 103.4 jit_solution(16611594264363780304)
XLA Ops:
  0.7 2.2 %shard_map.144 = (bf16[3,8,32,128]{3,2,1,0:T(8,128)(2,1)}, bf16[3,8,32,128]{3,2,1,0:T(8,128)(2,1)}, bf16[1,8,32,128]{3,2,1,0:T(8,128)(2,1)}) custom-call(bf16[32,3,8,128]{3,2,1,0:T(8,128)(2,1)} %field_hbm.1, bf16[32,3,8,128]{3,2,1,0:T(8,128)(2,1)} %cot_hbm.1), custom_call_target="tpu_custom_call" | custom-call | tf_op jit(solution)/shard_map/pallas_call | solution.py:313
  2.9 5.6 %collective-permute-start = (bf16[3,8,32,128]{3,2,1,0:T(8,128)(2,1)}, bf16[3,8,32,128]{3,2,1,0:T(8,128)(2,1)S(1)}, u32[]{:S(2)}, u32[]{:S(2)}) collective-permute-start(bf16[3,8,32,128]{3,2,1,0:T(8,128)(2,1)} %get-tuple-element.25.high_ref), channel_id=1, source_target_pairs={{0,16},{16,32},{32,48},{48,64},{64,80},{80,96},{96,112},{112,128},... | collective-permute-start | bytes 589832 | tf_op jit(solution)/shard_map/ppermute | solution.py:323
  8.5 10.8 %collective-permute-start.1 = (bf16[3,8,32,128]{3,2,1,0:T(8,128)(2,1)}, bf16[3,8,32,128]{3,2,1,0:T(8,128)(2,1)S(1)}, u32[]{:S(2)}, u32[]{:S(2)}) collective-permute-start(bf16[3,8,32,128]{3,2,1,0:T(8,128)(2,1)} %get-tuple-element.24.low_ref), channel_id=1, source_target_pairs={{16,0},{32,16},{48,32},{64,48},{80,64},{96,80},{112,96},{128,112},... | collective-permute-start | bytes 589832 | tf_op jit(solution)/shard_map/ppermute | solution.py:324
  19.6 0.7 copy-done.6
  20.3 0.7 copy-done.7
  21.1 1.5 %copy.30 = f32[27,32,32]{1,0,2:T(8,128)S(1)} copy(f32[27,32,32]{2,1,0:T(8,128)} %bitcast.52) | data formatting | bytes 221184 | tf_op jit(solution)/shard_map/reshape | solution.py:326
  23.7 3.1 %collective-permute-start.2 = (bf16[19,32,128]{2,1,0:T(8,128)(2,1)S(1)}, bf16[19,32,128]{2,1,0:T(8,128)(2,1)S(1)}, u32[]{:S(2)}, u32[]{:S(2)}) collective-permute-start(bf16[19,32,128]{2,1,0:T(8,128)(2,1)S(1)} %get-tuple-element.27), channel_id=1, source_target_pairs={{0,4},{4,8},{8,12},{12,0},{1,5},{5,9},{9,13},{13,1},{2,6},{6,10},{... | collective-permute-start | bytes 466952 | tf_op jit(solution)/shard_map/ppermute | solution.py:336
  26.8 3.4 %collective-permute-start.3 = (bf16[19,32,128]{2,1,0:T(8,128)(2,1)S(1)}, bf16[19,32,128]{2,1,0:T(8,128)(2,1)S(1)}, u32[]{:S(2)}, u32[]{:S(2)}) collective-permute-start(bf16[19,32,128]{2,1,0:T(8,128)(2,1)S(1)} %get-tuple-element.28), channel_id=1, source_target_pairs={{4,0},{8,4},{12,8},{0,12},{5,1},{9,5},{13,9},{1,13},{6,2},{10,6},{... | collective-permute-start | bytes 466952 | tf_op jit(solution)/shard_map/ppermute | solution.py:337
  30.2 0.7 collective-permute-done.2.up_ref
  30.9 2.2 %collective-permute-done.3.down_ref = bf16[19,32,128]{2,1,0:T(8,128)(2,1)S(1)} collective-permute-done((bf16[19,32,128]{2,1,0:T(8,128)(2,1)S(1)}, bf16[19,32,128]{2,1,0:T(8,128)(2,1)S(1)}, u32[]{:S(2)}, u32[]{:S(2)}) %collective-permute-start.3) | collective-permute-done | bytes 155680 | tf_op jit(solution)/shard_map/ppermute | solution.py:337
  33.1 1.2 %shard_map.146 = (bf16[12,8,32,128]{3,2,1,0:T(8,128)(2,1)S(1)}, bf16[10,8,32,128]{3,2,1,0:T(8,128)(2,1)S(1)}, bf16[4,8,3072]{2,1,0:T(8,128)(2,1)}) custom-call(bf16[3,8,32,128]{3,2,1,0:T(8,128)(2,1)S(1)} %copy-done.1, bf16[3,8,32,128]{3,2,1,0:T(8,128)(2,1)S(1)} %copy-done.2, bf16[1,8,32,128]{3,2,1,0:T(8,128)(2,1)S(1)} %copy-done.3, ...), custom_call_target="tpu_custom_call" | custom-call | bytes 1048576 | tf_op jit(solution)/shard_map/pallas_call | solution.py:339
  34.3 5.7 %all-to-all-start = ((bf16[4,8,3072]{2,1,0:T(8,128)(2,1)}), bf16[4,8,3072]{2,1,0:T(8,128)(2,1)S(1)}, u32[]{:S(2)}, u32[]{:S(2)}) async-start(bf16[4,8,3072]{2,1,0:T(8,128)(2,1)} %get-tuple-element.31), calls=%async_computation | async-start | bytes 393216 | tf_op jit(solution)/shard_map/all_to_all | solution.py:342
  41.0 0.6 copy-done.8
  41.7 2.8 %all-to-all-done.faces_ref = bf16[4,8,3072]{2,1,0:T(8,128)(2,1)S(1)} async-done(((bf16[4,8,3072]{2,1,0:T(8,128)(2,1)}), bf16[4,8,3072]{2,1,0:T(8,128)(2,1)S(1)}, u32[]{:S(2)}, u32[]{:S(2)}) %all-to-all-start) | async-done | bytes 196640 | tf_op jit(solution)/shard_map/all_to_all | solution.py:342
  44.5 6.8 %shard_map.147 = (f32[256,128]{1,0:T(8,128)S(1)}, bf16[5,32,1280]{2,1,0:T(8,128)(2,1)S(1)}, bf16[5,32,128]{2,1,0:T(8,128)(2,1)S(1)}) custom-call(bf16[12,8,32,128]{3,2,1,0:T(8,128)(2,1)S(1)} %get-tuple-element.29.field_ref, bf16[10,8,32,128]{3,2,1,0:T(8,128)(2,1)S(1)} %get-tuple-element.30.cot_ref, bf16[4,8,3072]{2,1,0:T(8,128)(2,1)S(1)} %all-to-all-done.faces_ref, ...), custom_call_target="tpu_custom_call" | custom-call | flops 540000000 | bytes 1048576 | tf_op jit(solution)/shard_map/pallas_call | solution.py:344
  51.3 13.1 %all_to_all.20 = f32[32,8,128]{2,1,0:T(8,128)S(1)} all-to-all(f32[32,8,128]{2,1,0:T(8,128)S(1)} %bitcast.48), channel_id=1, replica_groups=mesh['glong'=16,'ghi'=2,'gy'=4,'gz'=4] {'ghi','gy','gz'}, dimensions={0} | all-to-all | bytes 262144 | tf_op jit(solution)/shard_map/all_to_all | solution.py:303
  65.0 11.2 %all-to-all-start.2 = ((f32[16,8,128]{2,1,0:T(8,128)}), f32[16,8,128]{2,1,0:T(8,128)S(1)}, u32[]{:S(2)}, u32[]{:S(2)}) async-start(f32[16,8,128]{2,1,0:T(8,128)} %broadcast_in_dim.15), calls=%async_computation.2 | async-start | bytes 131072 | tf_op jit(solution)/shard_map/all_to_all | solution.py:305
  76.9 10.9 %all-to-all-done.2 = f32[16,8,128]{2,1,0:T(8,128)S(1)} async-done(((f32[16,8,128]{2,1,0:T(8,128)}), f32[16,8,128]{2,1,0:T(8,128)S(1)}, u32[]{:S(2)}, u32[]{:S(2)}) %all-to-all-start.2) | async-done | bytes 65568 | tf_op jit(solution)/shard_map/all_to_all | solution.py:305
  87.8 0.7 broadcast_in_dim.16
  88.5 5.7 %all-to-all-start.3 = ((f32[32,8,128]{2,1,0:T(8,128)}), f32[32,8,128]{2,1,0:T(8,128)S(1)}, u32[]{:S(2)}, u32[]{:S(2)}) async-start(f32[32,8,128]{2,1,0:T(8,128)} %broadcast_in_dim.16), calls=%async_computation.3 | async-start | bytes 262144 | tf_op jit(solution)/shard_map/all_to_all | solution.py:307
  94.9 2.3 %shard_map.148 = bf16[3,8,32,128]{3,2,1,0:T(8,128)(2,1)S(1)} custom-call(bf16[5,32,1280]{2,1,0:T(8,128)(2,1)S(1)} %get-tuple-element.32.up_ref, bf16[5,32,128]{2,1,0:T(8,128)(2,1)S(1)} %get-tuple-element.33.rim_ref, bf16[32,864]{1,0:T(8,128)(2,1)S(1)} %reshape.67.bwd_ref), custom_call_target="tpu_custom_call" | custom-call | flops 170000000 | bytes 1048576 | tf_op jit(solution)/shard_map/pallas_call | solution.py:356
  97.2 0.8 copy.36
  98.0 4.1 %all-to-all-done.3 = f32[32,8,128]{2,1,0:T(8,128)S(1)} async-done(((f32[32,8,128]{2,1,0:T(8,128)}), f32[32,8,128]{2,1,0:T(8,128)S(1)}, u32[]{:S(2)}, u32[]{:S(2)}) %all-to-all-start.3) | async-done | bytes 131104 | tf_op jit(solution)/shard_map/all_to_all | solution.py:307
  102.0 1.4 %shard_map.149 = (f32[27,32,32]{2,1,0:T(8,128)}, f32[1,32]{1,0:T(1,128)}, f32[2,256]{1,0:T(2,128)}, f32[1,256]{1,0:T(1,128)}, f32[32,256]{1,0:T(8,128)}, /*index=5*/f32[1,32]{1,0:T(1,128)}) custom-call(f32[256,128]{1,0:T(8,128)S(1)} %bitcast.46, f32[32,896]{1,0:T(8,128)S(1)} %get-tuple-element.65.kernel_ref, f32[32,896]{1,0:T(8,128)S(1)} %get-tuple-element.64.modded_ref, ...), custom_call_target="tpu_custom_call" | custom-call | bytes 1048576 | tf_op jit(solution)/shard_map/pallas_call | solution.py:367
  (44 shorter events, 4.3 us)
Async XLA Ops:
  0.6 18.8 %copy-start = (f32[2,256]{1,0:T(2,128)S(1)}, f32[2,256]{1,0:T(2,128)}, u32[]{:S(2)}) copy-start(f32[2,256]{1,0:T(2,128)} %param.12) | copy-start | bytes 6148
  0.6 19.6 %copy-start.4 = (f32[256,32]{0,1:T(8,128)S(1)}, f32[256,32]{0,1:T(8,128)}, u32[]{:S(2)}) copy-start(f32[256,32]{0,1:T(8,128)} %param.14) | copy-start | bytes 98308
  2.9 16.5 %copy-start.9 = (f32[2]{0:T(128)S(1)}, f32[2]{0:T(128)}, u32[]{:S(2)}) copy-start(f32[2]{0:T(128)} %param.11) | copy-start | bytes 28
  2.9 19.9 %collective-permute-start = (bf16[3,8,32,128]{3,2,1,0:T(8,128)(2,1)}, bf16[3,8,32,128]{3,2,1,0:T(8,128)(2,1)S(1)}, u32[]{:S(2)}, u32[]{:S(2)}) collective-permute-start(bf16[3,8,32,128]{3,2,1,0:T(8,128)(2,1)} %get-tuple-element.25.high_ref), channel_id=1, source_target_pairs={{0,16},{16,32},{32,48},{48,64},{64,80},{80,96},{96,112},{112,128},... | collective-permute-start | bytes 589832 | tf_op jit(solution)/shard_map/ppermute | solution.py:323
  8.5 14.8 %collective-permute-start.1 = (bf16[3,8,32,128]{3,2,1,0:T(8,128)(2,1)}, bf16[3,8,32,128]{3,2,1,0:T(8,128)(2,1)S(1)}, u32[]{:S(2)}, u32[]{:S(2)}) collective-permute-start(bf16[3,8,32,128]{3,2,1,0:T(8,128)(2,1)} %get-tuple-element.24.low_ref), channel_id=1, source_target_pairs={{16,0},{32,16},{48,32},{64,48},{80,64},{96,80},{112,96},{128,112},... | collective-permute-start | bytes 589832 | tf_op jit(solution)/shard_map/ppermute | solution.py:324
  19.6 0.7 copy-start.6
  20.2 0.7 copy-start.7
  21.0 1.6 %copy-start.5 = (f32[32,32,3,3,3]{1,0,4,3,2:T(8,128)S(1)}, f32[32,32,3,3,3]{1,0,4,3,2:T(8,128)}, u32[]{:S(2)}) copy-start(f32[32,32,3,3,3]{1,0,4,3,2:T(8,128)} %param.16) | copy-start | bytes 331780
  21.0 2.3 %copy-start.3 = (bf16[1,8,32,128]{3,2,1,0:T(8,128)(2,1)S(1)}, bf16[1,8,32,128]{3,2,1,0:T(8,128)(2,1)}, u32[]{:S(2)}) copy-start(bf16[1,8,32,128]{3,2,1,0:T(8,128)(2,1)} %get-tuple-element.26.mid_ref) | copy-start | bytes 196612
  22.6 0.9 copy-start.1
  22.6 1.0 copy-start.2
  23.7 7.2 %collective-permute-start.2 = (bf16[19,32,128]{2,1,0:T(8,128)(2,1)S(1)}, bf16[19,32,128]{2,1,0:T(8,128)(2,1)S(1)}, u32[]{:S(2)}, u32[]{:S(2)}) collective-permute-start(bf16[19,32,128]{2,1,0:T(8,128)(2,1)S(1)} %get-tuple-element.27), channel_id=1, source_target_pairs={{0,4},{4,8},{8,12},{12,0},{1,5},{5,9},{9,13},{13,1},{2,6},{6,10},{... | collective-permute-start | bytes 466952 | tf_op jit(solution)/shard_map/ppermute | solution.py:336
  26.8 6.3 %collective-permute-start.3 = (bf16[19,32,128]{2,1,0:T(8,128)(2,1)S(1)}, bf16[19,32,128]{2,1,0:T(8,128)(2,1)S(1)}, u32[]{:S(2)}, u32[]{:S(2)}) collective-permute-start(bf16[19,32,128]{2,1,0:T(8,128)(2,1)S(1)} %get-tuple-element.28), channel_id=1, source_target_pairs={{4,0},{8,4},{12,8},{0,12},{5,1},{9,5},{13,9},{1,13},{6,2},{10,6},{... | collective-permute-start | bytes 466952 | tf_op jit(solution)/shard_map/ppermute | solution.py:337
  34.3 10.1 %all-to-all-start = ((bf16[4,8,3072]{2,1,0:T(8,128)(2,1)}), bf16[4,8,3072]{2,1,0:T(8,128)(2,1)S(1)}, u32[]{:S(2)}, u32[]{:S(2)}) async-start(bf16[4,8,3072]{2,1,0:T(8,128)(2,1)} %get-tuple-element.31), calls=%async_computation | async-start | bytes 393216 | tf_op jit(solution)/shard_map/all_to_all | solution.py:342
  41.0 0.7 copy-start.8
  65.0 22.8 %all-to-all-start.2 = ((f32[16,8,128]{2,1,0:T(8,128)}), f32[16,8,128]{2,1,0:T(8,128)S(1)}, u32[]{:S(2)}, u32[]{:S(2)}) async-start(f32[16,8,128]{2,1,0:T(8,128)} %broadcast_in_dim.15), calls=%async_computation.2 | async-start | bytes 131072 | tf_op jit(solution)/shard_map/all_to_all | solution.py:305
  88.5 13.5 %all-to-all-start.3 = ((f32[32,8,128]{2,1,0:T(8,128)}), f32[32,8,128]{2,1,0:T(8,128)S(1)}, u32[]{:S(2)}, u32[]{:S(2)}) async-start(f32[32,8,128]{2,1,0:T(8,128)} %broadcast_in_dim.16), calls=%async_computation.3 | async-start | bytes 262144 | tf_op jit(solution)/shard_map/all_to_all | solution.py:307

commit v4 on v3

--- a/solution.py
+++ b/solution.py
@@ -79,7 +79,7 @@
     return field, cot
 
 
-def pack_kernel(low_ref, high_ref, mid_ref, left_ref, right_ref, up_ref, down_ref):
+def pack_kernel(low_ref, high_ref, mid_ref, left_ref, right_ref, _, up_ref, down_ref):
     field, cot = planes(low_ref, high_ref, mid_ref, left_ref, right_ref)
     for n, (ref, at) in enumerate(field):
         up_ref[2 * n : 2 * n + 2] = ref[at, 6:8]
@@ -126,8 +126,16 @@
     return logistic * (1.0 + values * (1.0 - logistic))
 
 
+def row_taps(ref, x, width):
+    return jnp.concatenate(
+        [ref[c, x, :, b * 128 : b * 128 + width] for b in range(3) for c in range(3)], axis=0
+    )
+
+
 def conv_kernel(
-    field_ref, cot_ref, faces_ref, fwd_ref, offset_ref, sums_ref, up_ref, rim_ref, halo, shifted, edge, total
+    field_ref, cot_ref, faces_ref, fwd_ref, offset_ref,
+    sums_ref, up_ref, rim_ref,
+    halo, shifted, edge, acc, own, total,
 ):
     me = lax.axis_index("gz")
     before, after = lax.rem(me + 3, 4), lax.rem(me + 1, 4)
@@ -135,11 +143,13 @@
     def across(rows, place):
         return lax.dot_general(rows, place, (((0,), (0,)), ((), ())), preferred_element_type=f32)
 
-    halo[...] = (
-        across(faces_ref[before], select((8, 128), 0, 1, (None, 0)))
-        + across(faces_ref[after], select((8, 128), 0, 1, (None, None, 127)))
+    sides = [faces_ref[at].astype(f32) for at in (before, me, after)]
+    halo[...] = across(
+        jnp.concatenate([sides[0], sides[2]], axis=0).astype(bf16),
+        select((16, 128), 0, 1, (None, 0) + (None,) * 8 + (127,)),
     ).astype(bf16)
     lane = lax.broadcasted_iota(jnp.int32, (C, 128), 1)
+    acc[...] = jnp.zeros_like(acc)
 
     @pl.loop(0, 7)
     def _(x):
@@ -150,88 +160,145 @@
             shifted[0, x, :, at] = jnp.where(lane == 0, ends, pltpu.roll(row, 1, 1))
             shifted[1, x, :, at] = row
             shifted[2, x, :, at] = jnp.where(lane == 127, ends, pltpu.roll(row, 127, 1))
-
-    def spread(at, count, moves):
+        part = jnp.dot(fwd_ref[...], row_taps(shifted, x, OUT), preferred_element_type=f32)
+        for a in range(3):
+            acc[x + 2 - a] += part[a * C : a * C + C]
+
+    def spread(count, moves):
         rows = jnp.concatenate(
-            [faces_ref[at, :, y * 256 : y * 256 + 256].astype(f32) for y in range(count)], axis=0
+            [side[:, y * 256 : y * 256 + 256] for side in sides for y in range(count)], axis=0
         ).astype(bf16)
-        row = lax.broadcasted_iota(jnp.int32, (count * 8, 128), 0)
-        to = lax.broadcasted_iota(jnp.int32, (count * 8, 128), 1)
-        place = jnp.zeros((count * 8, 128), f32)
-        for k, n in moves:
-            place = jnp.where(((row & 7) == k) & (to == (row >> 3) * EDGE + n), 1.0, place)
+        row = lax.broadcasted_iota(jnp.int32, (count * 24, 128), 0)
+        to = lax.broadcasted_iota(jnp.int32, (count * 24, 128), 1)
+        place = jnp.zeros((count * 24, 128), f32)
+        for n, (side, k, m) in enumerate(moves):
+            y = (row >> 3) - side * count
+            hit = ((row & 7) == k) & (to == y * EDGE + m) & (y >= 0) & (y < count)
+            place = jnp.where(hit, 1.0, place)
         return across(rows, place.astype(bf16))
 
-    rim = spread(before, 12, ((0, 0), (1, 1))) + spread(me, 12, ((2, 2), (1, 3))) + spread(after, 12, ((2, 4), (3, 5)))
+    rim = spread(12, ((0, 0, 0), (0, 1, 1), (1, 2, 2), (1, 1, 3), (2, 2, 4), (2, 3, 5)))
     for t in range(9):
         shift = (t // 3) * EDGE + t % 3
         edge[t] = (pltpu.roll(rim, 128 - shift, 1) if shift else rim).astype(bf16)
-    rim_cot = spread(before, 10, ((4, 0),)) + spread(after, 10, ((5, 3),))
+    rim_cot = spread(10, ((0, 4, 0), (2, 5, 3)))
     block = jnp.concatenate(
-        [
-            jnp.concatenate([edge[t, (x + a) * C : (x + a) * C + C] for a in range(3) for t in range(9)], axis=0)
-            for x in range(5)
-        ],
-        axis=1,
-    )
-    preact = jnp.dot(fwd_ref[...], block, preferred_element_type=f32) + offset_ref[...]
-    slope = silu_slope(preact)
+        [jnp.concatenate([edge[t, x * C : x * C + C] for t in range(9)], axis=0) for x in range(7)], axis=1
+    )
+    part = jnp.dot(fwd_ref[...], block, preferred_element_type=f32)
+    offset = offset_ref[...]
     for x in range(5):
-        rim_ref[x] = (rim_cot[x * C : x * C + C] * slope[:, x * 128 : x * 128 + 128]).astype(bf16)
-
+        preact = offset + sum(
+            part[a * C : a * C + C, (x + a) * 128 : (x + a) * 128 + 128] for a in range(3)
+        )
+        rim_ref[x] = (rim_cot[x * C : x * C + C] * silu_slope(preact)).astype(bf16)
+
+    own[...] = jnp.zeros_like(own)
     total[...] = jnp.zeros_like(total)
 
     @pl.loop(0, 5)
     def _(x):
         beside = jnp.concatenate([cot_ref[y, x] for y in range(10)], axis=1).astype(f32)
-        block = jnp.concatenate(
-            [shifted[c, x + a, :, b * 128 : b * 128 + OUT] for a in range(3) for b in range(3) for c in range(3)],
-            axis=0,
-        )
-        preact = jnp.dot(fwd_ref[...], block, preferred_element_type=f32) + offset_ref[...]
-        upstream = (beside * silu_slope(preact)).astype(bf16)
+        upstream = (beside * silu_slope(acc[x + 2] + offset)).astype(bf16)
         up_ref[x] = upstream
 
         @pl.when((x >= 1) & (x <= 3))
         def _():
-            own = upstream[:, 128 : 128 + OWN]
-            total[:, 864:] += jnp.sum(own.astype(f32), axis=1, keepdims=True)
-            total[:, :864] += lax.dot_general(
-                own, block[:, 128 : 128 + OWN], (((1,), (1,)), ((), ())), preferred_element_type=f32
-            )
-
+            own[x + 1] = upstream[:, 128 : 128 + OWN]
+
+    @pl.loop(1, 6)
+    def _(x):
+        left = jnp.concatenate([own[x + 1 - a] for a in range(3)], axis=0)
+        right = jnp.concatenate(
+            [shifted[c, x, :, b * 128 + 128 : b * 128 + 128 + OWN] for b in range(3) for c in range(3)], axis=0
+        )
+        total[...] += lax.dot_general(left, right, (((1,), (1,)), ((), ())), preferred_element_type=f32)
+
+    offsets = sum(jnp.sum(own[x].astype(f32), axis=1, keepdims=True) for x in range(2, 5))
+    packed = jnp.concatenate(
+        [total[a * C : a * C + C] for a in range(3)] + [jnp.broadcast_to(offsets, (C, C))], axis=1
+    )
     for s in range(4):
         for l in range(8):
             at = (s * 8 + l) * 8
             if l < 7:
-                sums_ref[at : at + 8] = total[8 * s : 8 * s + 8, 128 * l : 128 * l + 128]
+                sums_ref[at : at + 8] = packed[8 * s : 8 * s + 8, 128 * l : 128 * l + 128]
             else:
                 sums_ref[at : at + 8] = jnp.zeros((8, 128), f32)
 
 
-def grad_kernel_body(up_ref, rim_ref, bwd_ref, grad_ref, shifted):
+def grad_kernel_body(up_ref, rim_ref, bwd_ref, grad_ref, shifted, acc):
     lane = lax.broadcasted_iota(jnp.int32, (C, 128), 1)
+    acc[...] = jnp.zeros_like(acc)
 
     @pl.loop(0, 5)
     def _(x):
         rim = rim_ref[x].astype(f32)
         for y in range(10):
             at = slice(y * 128, y * 128 + 128)
-            row = up_ref[x, :, at].astype(f32)
-            low, high = rim[:, y * EDGE : y * EDGE + 1], rim[:, y * EDGE + 3 : y * EDGE + 4]
-            shifted[0, x, :, at] = jnp.where(lane == 0, low, pltpu.roll(row, 1, 1)).astype(bf16)
-            shifted[1, x, :, at] = up_ref[x, :, at]
-            shifted[2, x, :, at] = jnp.where(lane == 127, high, pltpu.roll(row, 127, 1)).astype(bf16)
-
-    @pl.loop(0, 3)
-    def _(x):
-        block = jnp.concatenate(
-            [shifted[c, x + a, :, b * 128 : b * 128 + OWN] for a in range(3) for b in range(3) for c in range(3)],
-            axis=0,
-        )
-        grad = jnp.dot(bwd_ref[...], block, preferred_element_type=f32).astype(bf16)
-        for y in range(8):
-            grad_ref[x, y] = grad[:, y * 128 : y * 128 + 128]
+            row = up_ref[x, :, at]
+            low = jnp.broadcast_to(rim[:, y * EDGE : y * EDGE + 1], (C, 128)).astype(bf16)
+            high = jnp.broadcast_to(rim[:, y * EDGE + 3 : y * EDGE + 4], (C, 128)).astype(bf16)
+            shifted[0, 0, :, at] = jnp.where(lane == 0, low, pltpu.roll(row, 1, 1))
+            shifted[1, 0, :, at] = row
+            shifted[2, 0, :, at] = jnp.where(lane == 127, high, pltpu.roll(row, 127, 1))
+        part = jnp.dot(bwd_ref[...], row_taps(shifted, 0, OWN), preferred_element_type=f32)
+        for a in range(3):
+            acc[x + 2 - a] += part[a * C : a * C + C]
+
+    to = lax.broadcasted_iota(jnp.int32, (256, 256), 0)
+    of = lax.broadcasted_iota(jnp.int32, (256, 256), 1)
+    perm = jnp.where((to & 7) * C + (to >> 3) == of, 1.0, 0.0).astype(bf16)
+    for x in range(3):
+        rows = jnp.concatenate(
+            [acc[x + 2, :, y * 128 : y * 128 + 128] for y in range(8)], axis=0
+        ).astype(bf16)
+        moved = jnp.dot(perm, rows, preferred_element_type=f32)
+        grad_ref[:, x] = moved.reshape(C, 8, 128).astype(bf16)
+
+
+def identity():
+    return jnp.where(
+        lax.broadcasted_iota(jnp.int32, (C, C), 0) == lax.broadcasted_iota(jnp.int32, (C, C), 1), 1.0, 0.0
+    )
+
+
+def modulate_kernel(
+    cosmology_ref, lift_ref, bias_ref, weight_ref, sbias_ref, taps_ref, offset_ref,
+    fwd_ref, bwd_ref, kernel_ref, modded_ref, styles_ref, inv_ref, lifted_ref, hidden_ref, params_ref, column_ref,
+):
+    first, second = cosmology_ref[:, 0:1], cosmology_ref[:, 1:2]
+    lifted = first * lift_ref[0:1] + second * lift_ref[1:2] + bias_ref[...]
+    hidden = lifted * jax.nn.sigmoid(lifted)
+    eye = identity()
+    column = jnp.sum(weight_ref[...] * hidden, axis=1, keepdims=True)
+    styles = jnp.sum(column * eye, axis=0, keepdims=True) + sbias_ref[...] + 1.0
+    kernel = jnp.concatenate([taps_ref[t] for t in range(TAPS)] + [jnp.zeros((C, C), f32)], axis=1)
+    styles = jnp.concatenate([styles] * TAPS + [jnp.zeros((1, C), f32)], axis=1)
+    modded = kernel * styles
+    inv = lax.rsqrt(jnp.sum(modded * modded, axis=1, keepdims=True) + demod_eps)
+    scaled = (modded * inv).astype(bf16)
+    for a in range(3):
+        fwd_ref[a * C : a * C + C] = scaled[:, a * 288 : a * 288 + 288]
+    turned = scaled.astype(f32).T
+    for a in range(3):
+        bwd_ref[a * C : a * C + C] = jnp.concatenate(
+            [turned[(26 - a * 9 - t) * C : (27 - a * 9 - t) * C] for t in range(9)], axis=1
+        ).astype(bf16)
+    kernel_ref[...] = kernel
+    modded_ref[...] = modded
+    styles_ref[...] = styles
+    inv_ref[...] = inv
+    lifted_ref[...] = lifted
+    hidden_ref[...] = hidden
+    params_ref[...] = jnp.concatenate([first, second], axis=0)
+    column_ref[...] = jnp.sum(offset_ref[...] * eye, axis=1, keepdims=True)
+
+
+def total_kernel(parts_ref, spread_ref):
+    part = jnp.sum(parts_ref[...], axis=0)
+    for n in range(spread_ref.shape[0]):
+        spread_ref[n] = part
 
 
 def tail_kernel(
@@ -249,9 +316,7 @@
         axis=1,
     )
     kernel, modded, styles, inv = kernel_ref[...], modded_ref[...], styles_ref[...], inv_ref[...]
-    eye = jnp.where(
-        lax.broadcasted_iota(jnp.int32, (C, C), 0) == lax.broadcasted_iota(jnp.int32, (C, C), 1), 1.0, 0.0
-    )
+    eye = identity()
     offset = jnp.sum(sums[:, TAPS * C : TAPS * C + C] * eye, axis=0, keepdims=True)
     projected = jnp.sum(sums * modded, axis=1, keepdims=True)
     mod_grad = inv * (sums - modded * (inv * inv * projected))
@@ -282,28 +347,12 @@
     return ahead, [(j, i) for i, j in ahead]
 
 
-def modulate(cosmology, lift_weight, lift_bias, style_weight, style_bias, kernel):
-    lifted = (
-        jnp.dot(cosmology[None, :], lift_weight, precision=lax.Precision.HIGHEST)[0] + lift_bias
-    )
-    hidden = jax.nn.silu(lifted)
-    styles = (
-        jnp.dot(hidden[None, :], style_weight, precision=lax.Precision.HIGHEST)[0]
-        + style_bias
-        + 1.0
-    )
-    modded = kernel * styles[None, None, :]
-    inv_norm = lax.rsqrt(jnp.sum(modded * modded, axis=(0, 2)) + demod_eps)
-    scaled = (modded * inv_norm[None, :, None]).astype(bf16)
-    return (lifted, hidden, styles, modded, inv_norm, scaled)
-
-
 def summed(sums):
     flat = ("ghi", "gy", "gz")
-    part = jnp.sum(lax.all_to_all(sums.reshape(32, 8, 128), flat, 0, 0, tiled=True), axis=0)
-    spread = jnp.broadcast_to(part[None], (16, 8, 128))
-    part = jnp.sum(lax.all_to_all(spread, "glong", 0, 0, tiled=True), axis=0)
-    spread = jnp.broadcast_to(part[None], (32, 8, 128))
+    parts = lax.all_to_all(sums.reshape(32, 8, 128), flat, 0, 0, tiled=True)
+    (spread,) = call(total_kernel, [shape(16, 8, 128, dtype=f32)], 1, limit=4)(parts)
+    parts = lax.all_to_all(spread, "glong", 0, 0, tiled=True)
+    (spread,) = call(total_kernel, [shape(32, 8, 128, dtype=f32)], 1, limit=4)(parts)
     return lax.all_to_all(spread, flat, 0, 0, tiled=True).reshape(256, 128)
 
 
@@ -318,20 +367,29 @@
         scratch_shapes=[
             pltpu.VMEM((C, 3, 8, 128), bf16), pltpu.VMEM((C, 3, 8, 128), bf16), pltpu.SemaphoreType.DMA((2,)),
         ],
-    )(field, cotangent)
+        compiler_params=pltpu.CompilerParams(vmem_limit_bytes=4 * 1024 * 1024),
+    )(*(pltpu.with_memory_space_constraint(block, pltpu.HBM) for block in (field, cotangent)))
     ahead, back = shifts(("glong", "ghi"))
     left = lax.ppermute(high, ("glong", "ghi"), ahead)
     right = lax.ppermute(low, ("glong", "ghi"), back)
 
     taps = jnp.transpose(kernel, (2, 3, 4, 0, 1)).reshape(TAPS, C, C)
-    lifted, hidden, styles, modded, inv_norm, scaled = modulate(
-        cosmology, lift_weight, lift_bias, style_weight, style_bias, taps
-    )
-    fwd = jnp.transpose(scaled, (1, 0, 2)).reshape(C, TAPS * C)
-    bwd = jnp.transpose(scaled[::-1], (2, 0, 1)).reshape(C, TAPS * C)
+    fwd, bwd, packed, modded, styles, inv_norm, lifted, hidden, params, column = call(
+        modulate_kernel,
+        [
+            shape(3 * C, 9 * C), shape(3 * C, 9 * C), shape(C, 896, dtype=f32), shape(C, 896, dtype=f32),
+            shape(1, 896, dtype=f32), shape(C, 1, dtype=f32), shape(1, 256, dtype=f32), shape(1, 256, dtype=f32),
+            shape(2, 1, dtype=f32), shape(C, 1, dtype=f32),
+        ],
+        7,
+        limit=8,
+    )(
+        cosmology[None, :], lift_weight, lift_bias[None, :], style_weight.T, style_bias[None, :], taps,
+        offset[None, :],
+    )
 
     rows = (low, high, mid, left, right)
-    up, down = call(pack_kernel, [shape(19, C, 128), shape(19, C, 128)], 5)(*rows)
+    up, down = call(pack_kernel, [shape(19, C, 128), shape(19, C, 128)], 6, limit=8)(*rows, column)
     ahead, back = shifts("gy")
     up = lax.ppermute(up, "gy", ahead)
     down = lax.ppermute(down, "gy", back)
@@ -350,20 +408,19 @@
             pltpu.VMEM((FIELD_LANES, 128), bf16),
             pltpu.VMEM((3, 7, C, 12 * 128), bf16),
             pltpu.VMEM((9, 8 * C, 128), bf16),
-            pltpu.VMEM((C, 896), f32),
+            pltpu.VMEM((9, C, OUT), f32),
+            pltpu.VMEM((7, C, OWN), bf16),
+            pltpu.VMEM((3 * C, 9 * C), f32),
         ],
-    )(field_rows, cot_rows, faces, fwd, offset[:, None])
-    (grad_rows,) = call(
+    )(field_rows, cot_rows, faces, fwd, column)
+    (grad_field,) = call(
         grad_kernel_body,
-        [shape(3, 8, C, 128)],
+        [shape(C, 3, 8, 128)],
         3,
         flops=170_000_000,
-        scratch=[pltpu.VMEM((3, 5, C, OUT), bf16)],
+        scratch=[pltpu.VMEM((3, 1, C, OUT), bf16), pltpu.VMEM((7, C, OWN), f32)],
     )(upstream, rim, bwd)
-    grad_field = jnp.transpose(grad_rows, (2, 0, 1, 3))
-
-    packed = jnp.pad(jnp.transpose(taps, (1, 0, 2)).reshape(C, TAPS * C), ((0, 0), (0, C)))
-    styles_row = jnp.pad(jnp.tile(styles, TAPS), (0, C))[None, :]
+
     kernel_out, grad_offset, grad_lift, grad_liftbias, grad_style, grad_stylebias = call(
         tail_kernel,
         [
@@ -371,9 +428,9 @@
             shape(1, 256, dtype=f32), shape(C, 256, dtype=f32), shape(1, C, dtype=f32),
         ],
         9,
+        limit=8,
     )(
-        summed(sums), packed, packed * styles_row, styles_row, inv_norm[:, None], lifted[None, :],
-        hidden[None, :], style_weight.T, cosmology[:, None],
+        summed(sums), packed, modded, styles, inv_norm, lifted, hidden, style_weight.T, params,
     )
     grad_kernel = jnp.transpose(kernel_out.reshape(3, 3, 3, C, C), (3, 4, 0, 1, 2))
     return (

time: 104 us -> 101 us (0.971)
  blocking collectives: 13.1 us -> 41.2 us
  starting transfers between devices: 45.6 us -> 28.7 us
  waiting for transfers between devices: 21.1 us -> 14.3 us
  local copies, waits for them, and re-layouts: 8.05 us -> 1.7 us
    all_to_all x1 -> x3, blocking collectives: 13.1 us -> 41.2 us  [the longest x1 18.6 us: summed(): parts = lax.all_to_all(spread, 'glong', 0, 0, tiled=True)]
    all_to_all x2 -> x0, starting transfers between devices: 16.9 us -> none  [the longest x1 11.2 us: summed(): part = jnp.sum(lax.all_to_all(spread, 'glong', 0, 0, tiled=True), axis=0)]
    all_to_all x2 -> x0, waiting for transfers between devices: 13.7 us -> none  [the longest x1 10.9 us: summed(): part = jnp.sum(lax.all_to_all(spread, 'glong', 0, 0, tiled=True), axis=0)]
    ppermute x1, waiting for transfers between devices: 0.01 us -> 6.66 us  [body(): left = lax.ppermute(high, ('glong', 'ghi'), ahead)]
    ppermute x1, starting transfers between devices: 10.8 us -> 14.6 us  [body(): right = lax.ppermute(low, ('glong', 'ghi'), back)]
    ppermute x1, starting transfers between devices: 5.65 us -> 1.92 us  [body(): left = lax.ppermute(high, ('glong', 'ghi'), ahead)]
    reshape x5 -> x0, local copies, waits for them, and re-layouts: 2.48 us -> none  [the longest x2 1.81 us: body(): taps = jnp.transpose(kernel, (2, 3, 4, 0, 1)).reshape(TAPS, C, C)]
    pallas_call x2 -> x5, Pallas kernels: 2.32 us -> 4.43 us  [the longest x1 3.09 us: body(): call(grad_kernel_body, [shape(C, 3, 8, 128)], 3, flops=170000000, scratch...]
  transfers between devices with their start and end apart: 7 -> 5, of which waited for: 6 -> 4; matrix products, arithmetic and copies ran while one was open for 5% -> 0% of each run, Pallas kernels for 2% -> 4%
where the time goes in v4:
time: 101 us
  blocking collectives  41.2 us (41%)
  starting transfers between devices  28.7 us (28%)
  waiting for transfers between devices  14.3 us (14%)
  Pallas kernels  14 us (14%)
  local copies, waits for them, and re-layouts  1.7 us (2%)
    all_to_all x1, blocking collectives, summed(): parts = lax.all_to_all(spread, 'glong', 0, 0, tiled=True)  18.6 us
    ppermute x1, starting transfers between devices, body(): right = lax.ppermute(low, ('glong', 'ghi'), back)  14.6 us
    all_to_all x1, blocking collectives, summed(): parts = lax.all_to_all(sums.reshape(32, 8, 128), flat, 0, 0, tiled=True)  12.6 us
    all_to_all x1, blocking collectives, body(): faces = lax.all_to_all(faces, 'gz', 0, 0, tiled=True)  9.97 us
    ppermute x1, waiting for transfers between devices, body(): left = lax.ppermute(high, ('glong', 'ghi'), ahead)  6.66 us
    pallas_call x1, Pallas kernels, body(): call(conv_kernel, [shape(256, 128, dtype=f32), shape(5, C, OUT), shape(5,...  6.21 us
    all_to_all x1, starting transfers between devices, summed(): return lax.all_to_all(spread, flat, 0, 0, tiled=True).reshape(256, 128)  5.7 us
    all_to_all x1, waiting for transfers between devices, summed(): return lax.all_to_all(spread, flat, 0, 0, tiled=True).reshape(256, 128)  4.71 us
  transfers between devices with their start and end apart: 5, of which 4 were waited for; matrix products, arithmetic and copies ran while one was open for 0% of the time, Pallas kernels for 4%

profile of v4, /device:TPU:1, one launch (start us, length us, event | category | flops | bytes accessed | tf_op | source)
XLA Modules:
  0.0 100.6 jit_solution(13755706580282791525)
XLA Ops:
  0.6 1.5 %shard_map.144 = (bf16[3,8,32,128]{3,2,1,0:T(8,128)(2,1)S(1)}, bf16[3,8,32,128]{3,2,1,0:T(8,128)(2,1)S(1)}, bf16[1,8,32,128]{3,2,1,0:T(8,128)(2,1)S(1)}) custom-call(bf16[32,3,8,128]{3,2,1,0:T(8,128)(2,1)} %field_hbm.1, bf16[32,3,8,128]{3,2,1,0:T(8,128)(2,1)} %cot_hbm.1), custom_call_target="tpu_custom_call" | custom-call | tf_op jit(solution)/shard_map/pallas_call | solution.py:362
  2.2 14.6 %collective-permute-start.1 = (bf16[3,8,32,128]{3,2,1,0:T(8,128)(2,1)S(1)}, bf16[3,8,32,128]{3,2,1,0:T(8,128)(2,1)S(1)}, u32[]{:S(2)}, u32[]{:S(2)}) collective-permute-start(bf16[3,8,32,128]{3,2,1,0:T(8,128)(2,1)S(1)} %get-tuple-element.34.low_ref), channel_id=1, source_target_pairs={{16,0},{32,16},{48,32},{64,48},{80,64},{96,80},{112,96},{128,112},... | collective-permute-start | bytes 589832 | tf_op jit(solution)/shard_map/ppermute | solution.py:374
  16.8 1.9 %collective-permute-start = (bf16[3,8,32,128]{3,2,1,0:T(8,128)(2,1)S(1)}, bf16[3,8,32,128]{3,2,1,0:T(8,128)(2,1)S(1)}, u32[]{:S(2)}, u32[]{:S(2)}) collective-permute-start(bf16[3,8,32,128]{3,2,1,0:T(8,128)(2,1)S(1)} %get-tuple-element.35.high_ref), channel_id=1, source_target_pairs={{0,16},{16,32},{32,48},{48,64},{64,80},{80,96},{96,112},{112,128},... | collective-permute-start | bytes 589832 | tf_op jit(solution)/shard_map/ppermute | solution.py:373
  18.8 0.6 copy-done.5
  19.3 0.0 copy-done.6
  19.4 0.0 copy-done.2
  19.4 0.0 copy-done.3
  19.4 1.0 %copy-done = f32[32,32,3,3,3]{1,0,4,3,2:T(8,128)S(1)} copy-done((f32[32,32,3,3,3]{1,0,4,3,2:T(8,128)S(1)}, f32[32,32,3,3,3]{1,0,4,3,2:T(8,128)}, u32[]{:S(2)}) %copy-start) | copy-done | bytes 110616
  20.4 0.6 shard_map.145
  21.1 6.7 %collective-permute-done.left_ref = bf16[3,8,32,128]{3,2,1,0:T(8,128)(2,1)S(1)} collective-permute-done((bf16[3,8,32,128]{3,2,1,0:T(8,128)(2,1)S(1)}, bf16[3,8,32,128]{3,2,1,0:T(8,128)(2,1)S(1)}, u32[]{:S(2)}, u32[]{:S(2)}) %collective-permute-start) | collective-permute-done | bytes 196640 | tf_op jit(solution)/shard_map/ppermute | solution.py:373
  27.7 3.1 %collective-permute-start.2 = (bf16[19,32,128]{2,1,0:T(8,128)(2,1)S(1)}, bf16[19,32,128]{2,1,0:T(8,128)(2,1)S(1)}, u32[]{:S(2)}, u32[]{:S(2)}) collective-permute-start(bf16[19,32,128]{2,1,0:T(8,128)(2,1)S(1)} %get-tuple-element.38), channel_id=1, source_target_pairs={{0,4},{4,8},{8,12},{12,0},{1,5},{5,9},{9,13},{13,1},{2,6},{6,10},{... | collective-permute-start | bytes 466952 | tf_op jit(solution)/shard_map/ppermute | solution.py:394
  30.9 3.4 %collective-permute-start.3 = (bf16[19,32,128]{2,1,0:T(8,128)(2,1)S(1)}, bf16[19,32,128]{2,1,0:T(8,128)(2,1)S(1)}, u32[]{:S(2)}, u32[]{:S(2)}) collective-permute-start(bf16[19,32,128]{2,1,0:T(8,128)(2,1)S(1)} %get-tuple-element.39), channel_id=1, source_target_pairs={{4,0},{8,4},{12,8},{0,12},{5,1},{9,5},{13,9},{1,13},{6,2},{10,6},{... | collective-permute-start | bytes 466952 | tf_op jit(solution)/shard_map/ppermute | solution.py:395
  34.2 0.7 collective-permute-done.2.up_ref
  34.9 2.2 %collective-permute-done.3.down_ref = bf16[19,32,128]{2,1,0:T(8,128)(2,1)S(1)} collective-permute-done((bf16[19,32,128]{2,1,0:T(8,128)(2,1)S(1)}, bf16[19,32,128]{2,1,0:T(8,128)(2,1)S(1)}, u32[]{:S(2)}, u32[]{:S(2)}) %collective-permute-start.3) | collective-permute-done | bytes 155680 | tf_op jit(solution)/shard_map/ppermute | solution.py:395
  37.1 0.5 shard_map.147
  37.6 10.0 %all_to_all.20.faces_ref = bf16[4,8,3072]{2,1,0:T(8,128)(2,1)S(1)} all-to-all(bf16[4,8,3072]{2,1,0:T(8,128)(2,1)S(1)} %get-tuple-element.42), channel_id=1, replica_groups=mesh['glong'=16,'ghi'=2,'gy'=4,'gz'=4] {'gz'}, dimensions={0} | all-to-all | bytes 393216 | tf_op jit(solution)/shard_map/all_to_all | solution.py:400
  47.6 6.2 %shard_map.148 = (f32[256,128]{1,0:T(8,128)S(1)}, bf16[5,32,1280]{2,1,0:T(8,128)(2,1)S(1)}, bf16[5,32,128]{2,1,0:T(8,128)(2,1)S(1)}) custom-call(bf16[12,8,32,128]{3,2,1,0:T(8,128)(2,1)S(1)} %get-tuple-element.40.field_ref, bf16[10,8,32,128]{3,2,1,0:T(8,128)(2,1)S(1)} %get-tuple-element.41.cot_ref, bf16[4,8,3072]{2,1,0:T(8,128)(2,1)S(1)} %all_to_all.20.faces_ref, ...), custom_call_target="tpu_custom_call" | custom-call | flops 540000000 | bytes 1048576 | tf_op jit(solution)/shard_map/pallas_call | solution.py:402
  53.8 12.6 %all_to_all.21.parts_ref = f32[32,8,128]{2,1,0:T(8,128)S(1)} all-to-all(f32[32,8,128]{2,1,0:T(8,128)S(1)} %bitcast.21), channel_id=1, replica_groups=mesh['glong'=16,'ghi'=2,'gy'=4,'gz'=4] {'ghi','gy','gz'}, dimensions={0} | all-to-all | bytes 262144 | tf_op jit(solution)/shard_map/all_to_all | solution.py:352
  66.5 18.6 %all_to_all.22.parts_ref = f32[16,8,128]{2,1,0:T(8,128)S(1)} all-to-all(f32[16,8,128]{2,1,0:T(8,128)S(1)} %shard_map.150), channel_id=1, replica_groups=mesh['glong'=16,'ghi'=2,'gy'=4,'gz'=4] {'glong'}, dimensions={0} | all-to-all | bytes 131072 | tf_op jit(solution)/shard_map/all_to_all | solution.py:354
  85.1 0.7 shard_map.151
  85.8 5.7 %all-to-all-start.3 = ((f32[32,8,128]{2,1,0:T(8,128)}), f32[32,8,128]{2,1,0:T(8,128)S(1)}, u32[]{:S(2)}, u32[]{:S(2)}) async-start(f32[32,8,128]{2,1,0:T(8,128)} %shard_map.151), calls=%async_computation.3 | async-start | bytes 262144 | tf_op jit(solution)/shard_map/all_to_all | solution.py:356
  91.5 3.1 %shard_map.149 = bf16[32,3,8,128]{3,2,1,0:T(8,128)(2,1)} custom-call(bf16[5,32,1280]{2,1,0:T(8,128)(2,1)S(1)} %get-tuple-element.44.up_ref, bf16[5,32,128]{2,1,0:T(8,128)(2,1)S(1)} %get-tuple-element.45.rim_ref, bf16[96,288]{1,0:T(8,128)(2,1)S(1)} %get-tuple-element.46.bwd_ref), custom_call_target="tpu_custom_call" | custom-call | flops 170000000 | bytes 1048576 | tf_op jit(solution)/shard_map/pallas_call | solution.py:416
  94.6 4.7 %all-to-all-done.3 = f32[32,8,128]{2,1,0:T(8,128)S(1)} async-done(((f32[32,8,128]{2,1,0:T(8,128)}), f32[32,8,128]{2,1,0:T(8,128)S(1)}, u32[]{:S(2)}, u32[]{:S(2)}) %all-to-all-start.3) | async-done | bytes 131104 | tf_op jit(solution)/shard_map/all_to_all | solution.py:356
  99.3 1.4 %shard_map.152 = (f32[27,32,32]{2,1,0:T(8,128)}, f32[1,32]{1,0:T(1,128)}, f32[2,256]{1,0:T(2,128)}, f32[1,256]{1,0:T(1,128)}, f32[32,256]{1,0:T(8,128)}, /*index=5*/f32[1,32]{1,0:T(1,128)}) custom-call(f32[256,128]{1,0:T(8,128)S(1)} %bitcast.17, f32[32,896]{1,0:T(8,128)S(1)} %get-tuple-element.48.kernel_ref, f32[32,896]{1,0:T(8,128)S(1)} %get-tuple-element.49.modded_ref, ...), custom_call_target="tpu_custom_call" | custom-call | bytes 1048576 | tf_op jit(solution)/shard_map/pallas_call | solution.py:424
  (12 shorter events, 0.1 us)
Async XLA Ops:
  0.6 18.1 %copy-start.1 = (f32[256,32]{0,1:T(8,128)S(1)}, f32[256,32]{0,1:T(8,128)}, u32[]{:S(2)}) copy-start(f32[256,32]{0,1:T(8,128)} %param.14) | copy-start | bytes 98308
  2.2 18.9 %collective-permute-start.1 = (bf16[3,8,32,128]{3,2,1,0:T(8,128)(2,1)S(1)}, bf16[3,8,32,128]{3,2,1,0:T(8,128)(2,1)S(1)}, u32[]{:S(2)}, u32[]{:S(2)}) collective-permute-start(bf16[3,8,32,128]{3,2,1,0:T(8,128)(2,1)S(1)} %get-tuple-element.34.low_ref), channel_id=1, source_target_pairs={{16,0},{32,16},{48,32},{64,48},{80,64},{96,80},{112,96},{128,112},... | collective-permute-start | bytes 589832 | tf_op jit(solution)/shard_map/ppermute | solution.py:374
  16.8 11.0 %collective-permute-start = (bf16[3,8,32,128]{3,2,1,0:T(8,128)(2,1)S(1)}, bf16[3,8,32,128]{3,2,1,0:T(8,128)(2,1)S(1)}, u32[]{:S(2)}, u32[]{:S(2)}) collective-permute-start(bf16[3,8,32,128]{3,2,1,0:T(8,128)(2,1)S(1)} %get-tuple-element.35.high_ref), channel_id=1, source_target_pairs={{0,16},{16,32},{32,48},{48,64},{64,80},{80,96},{96,112},{112,128},... | collective-permute-start | bytes 589832 | tf_op jit(solution)/shard_map/ppermute | solution.py:373
  18.7 0.7 copy-start.5
  18.7 0.7 copy-start.6
  18.7 0.7 copy-start.2
  18.7 0.7 copy-start.3
  18.7 0.7 copy-start.4
  19.4 1.0 %copy-start = (f32[32,32,3,3,3]{1,0,4,3,2:T(8,128)S(1)}, f32[32,32,3,3,3]{1,0,4,3,2:T(8,128)}, u32[]{:S(2)}) copy-start(f32[32,32,3,3,3]{1,0,4,3,2:T(8,128)} %param.16) | copy-start | bytes 331780
  27.7 7.2 %collective-permute-start.2 = (bf16[19,32,128]{2,1,0:T(8,128)(2,1)S(1)}, bf16[19,32,128]{2,1,0:T(8,128)(2,1)S(1)}, u32[]{:S(2)}, u32[]{:S(2)}) collective-permute-start(bf16[19,32,128]{2,1,0:T(8,128)(2,1)S(1)} %get-tuple-element.38), channel_id=1, source_target_pairs={{0,4},{4,8},{8,12},{12,0},{1,5},{5,9},{9,13},{13,1},{2,6},{6,10},{... | collective-permute-start | bytes 466952 | tf_op jit(solution)/shard_map/ppermute | solution.py:394
  30.9 6.3 %collective-permute-start.3 = (bf16[19,32,128]{2,1,0:T(8,128)(2,1)S(1)}, bf16[19,32,128]{2,1,0:T(8,128)(2,1)S(1)}, u32[]{:S(2)}, u32[]{:S(2)}) collective-permute-start(bf16[19,32,128]{2,1,0:T(8,128)(2,1)S(1)} %get-tuple-element.39), channel_id=1, source_target_pairs={{4,0},{8,4},{12,8},{0,12},{5,1},{9,5},{13,9},{1,13},{6,2},{10,6},{... | collective-permute-start | bytes 466952 | tf_op jit(solution)/shard_map/ppermute | solution.py:395
  85.8 13.5 %all-to-all-start.3 = ((f32[32,8,128]{2,1,0:T(8,128)}), f32[32,8,128]{2,1,0:T(8,128)S(1)}, u32[]{:S(2)}, u32[]{:S(2)}) async-start(f32[32,8,128]{2,1,0:T(8,128)} %shard_map.151), calls=%async_computation.3 | async-start | bytes 262144 | tf_op jit(solution)/shard_map/all_to_all | solution.py:356

commit v5 on v4

--- a/solution.py
+++ b/solution.py
@@ -135,7 +135,7 @@
 def conv_kernel(
     field_ref, cot_ref, faces_ref, fwd_ref, offset_ref,
     sums_ref, up_ref, rim_ref,
-    halo, shifted, edge, acc, own, total,
+    halo, shifted, edge, acc,
 ):
     me = lax.axis_index("gz")
     before, after = lax.rem(me + 3, 4), lax.rem(me + 1, 4)
@@ -149,20 +149,21 @@
         select((16, 128), 0, 1, (None, 0) + (None,) * 8 + (127,)),
     ).astype(bf16)
     lane = lax.broadcasted_iota(jnp.int32, (C, 128), 1)
-    acc[...] = jnp.zeros_like(acc)
-
-    @pl.loop(0, 7)
-    def _(x):
+    for x in range(7):
         for y in range(12):
             row = field_ref[y, x]
-            ends = halo[pl.ds(pl.multiple_of((y * 8 + x) * C, C), C), :]
+            ends = halo[(y * 8 + x) * C : (y * 8 + x) * C + C, :]
             at = slice(y * 128, y * 128 + 128)
             shifted[0, x, :, at] = jnp.where(lane == 0, ends, pltpu.roll(row, 1, 1))
             shifted[1, x, :, at] = row
             shifted[2, x, :, at] = jnp.where(lane == 127, ends, pltpu.roll(row, 127, 1))
         part = jnp.dot(fwd_ref[...], row_taps(shifted, x, OUT), preferred_element_type=f32)
         for a in range(3):
-            acc[x + 2 - a] += part[a * C : a * C + C]
+            if 0 <= x - a < 5:
+                if a == 0:
+                    acc[x] = part[:C]
+                else:
+                    acc[x - a] += part[a * C : a * C + C]
 
     def spread(count, moves):
         rows = jnp.concatenate(
@@ -193,28 +194,32 @@
         )
         rim_ref[x] = (rim_cot[x * C : x * C + C] * silu_slope(preact)).astype(bf16)
 
-    own[...] = jnp.zeros_like(own)
-    total[...] = jnp.zeros_like(total)
-
-    @pl.loop(0, 5)
-    def _(x):
+    ups = []
+    for x in range(5):
         beside = jnp.concatenate([cot_ref[y, x] for y in range(10)], axis=1).astype(f32)
-        upstream = (beside * silu_slope(acc[x + 2] + offset)).astype(bf16)
+        upstream = (beside * silu_slope(acc[x] + offset)).astype(bf16)
         up_ref[x] = upstream
-
-        @pl.when((x >= 1) & (x <= 3))
-        def _():
-            own[x + 1] = upstream[:, 128 : 128 + OWN]
-
-    @pl.loop(1, 6)
-    def _(x):
-        left = jnp.concatenate([own[x + 1 - a] for a in range(3)], axis=0)
-        right = jnp.concatenate(
-            [shifted[c, x, :, b * 128 + 128 : b * 128 + 128 + OWN] for b in range(3) for c in range(3)], axis=0
-        )
-        total[...] += lax.dot_general(left, right, (((1,), (1,)), ((), ())), preferred_element_type=f32)
-
-    offsets = sum(jnp.sum(own[x].astype(f32), axis=1, keepdims=True) for x in range(2, 5))
+        ups.append(upstream[:, 128 : 128 + OWN] if 1 <= x <= 3 else jnp.zeros((C, OWN), bf16))
+
+    left = jnp.concatenate(
+        [
+            jnp.concatenate([ups[x - a] if 0 <= x - a < 5 else ups[0] for a in range(3)], axis=0)
+            for x in range(1, 6)
+        ],
+        axis=1,
+    )
+    right = jnp.concatenate(
+        [
+            jnp.concatenate(
+                [shifted[c, x, :, b * 128 + 128 : b * 128 + 128 + OWN] for b in range(3) for c in range(3)], axis=0
+            )
+            for x in range(1, 6)
+        ],
+        axis=1,
+    )
+    total = lax.dot_general(left, right, (((1,), (1,)), ((), ())), preferred_element_type=f32)
+
+    offsets = sum(jnp.sum(ups[x].astype(f32), axis=1, keepdims=True) for x in range(1, 4))
     packed = jnp.concatenate(
         [total[a * C : a * C + C] for a in range(3)] + [jnp.broadcast_to(offsets, (C, C))], axis=1
     )
@@ -229,29 +234,30 @@
 
 def grad_kernel_body(up_ref, rim_ref, bwd_ref, grad_ref, shifted, acc):
     lane = lax.broadcasted_iota(jnp.int32, (C, 128), 1)
-    acc[...] = jnp.zeros_like(acc)
-
-    @pl.loop(0, 5)
-    def _(x):
+    for x in range(5):
         rim = rim_ref[x].astype(f32)
         for y in range(10):
             at = slice(y * 128, y * 128 + 128)
             row = up_ref[x, :, at]
             low = jnp.broadcast_to(rim[:, y * EDGE : y * EDGE + 1], (C, 128)).astype(bf16)
             high = jnp.broadcast_to(rim[:, y * EDGE + 3 : y * EDGE + 4], (C, 128)).astype(bf16)
-            shifted[0, 0, :, at] = jnp.where(lane == 0, low, pltpu.roll(row, 1, 1))
-            shifted[1, 0, :, at] = row
-            shifted[2, 0, :, at] = jnp.where(lane == 127, high, pltpu.roll(row, 127, 1))
-        part = jnp.dot(bwd_ref[...], row_taps(shifted, 0, OWN), preferred_element_type=f32)
+            shifted[0, x, :, at] = jnp.where(lane == 0, low, pltpu.roll(row, 1, 1))
+            shifted[1, x, :, at] = row
+            shifted[2, x, :, at] = jnp.where(lane == 127, high, pltpu.roll(row, 127, 1))
+        part = jnp.dot(bwd_ref[...], row_taps(shifted, x, OWN), preferred_element_type=f32)
         for a in range(3):
-            acc[x + 2 - a] += part[a * C : a * C + C]
+            if 0 <= x - a < 3:
+                if a == 0:
+                    acc[x] = part[:C]
+                else:
+                    acc[x - a] += part[a * C : a * C + C]
 
     to = lax.broadcasted_iota(jnp.int32, (256, 256), 0)
     of = lax.broadcasted_iota(jnp.int32, (256, 256), 1)
     perm = jnp.where((to & 7) * C + (to >> 3) == of, 1.0, 0.0).astype(bf16)
     for x in range(3):
         rows = jnp.concatenate(
-            [acc[x + 2, :, y * 128 : y * 128 + 128] for y in range(8)], axis=0
+            [acc[x, :, y * 128 : y * 128 + 128] for y in range(8)], axis=0
         ).astype(bf16)
         moved = jnp.dot(perm, rows, preferred_element_type=f32)
         grad_ref[:, x] = moved.reshape(C, 8, 128).astype(bf16)
@@ -408,9 +414,7 @@
             pltpu.VMEM((FIELD_LANES, 128), bf16),
             pltpu.VMEM((3, 7, C, 12 * 128), bf16),
             pltpu.VMEM((9, 8 * C, 128), bf16),
-            pltpu.VMEM((9, C, OUT), f32),
-            pltpu.VMEM((7, C, OWN), bf16),
-            pltpu.VMEM((3 * C, 9 * C), f32),
+            pltpu.VMEM((5, C, OUT), f32),
         ],
     )(field_rows, cot_rows, faces, fwd, column)
     (grad_field,) = call(
@@ -418,7 +422,7 @@
         [shape(C, 3, 8, 128)],
         3,
         flops=170_000_000,
-        scratch=[pltpu.VMEM((3, 1, C, OUT), bf16), pltpu.VMEM((7, C, OWN), f32)],
+        scratch=[pltpu.VMEM((3, 5, C, OUT), bf16), pltpu.VMEM((3, C, OWN), f32)],
     )(upstream, rim, bwd)
 
     kernel_out, grad_offset, grad_lift, grad_liftbias, grad_style, grad_stylebias = call(

time: 101 us -> 98.3 us (0.973)
  Pallas kernels: 14 us -> 9.98 us
  waiting for transfers between devices: 14.3 us -> 15.5 us
    pallas_call x1, Pallas kernels: 6.21 us -> 3.42 us  [body(): call(conv_kernel, [shape(256, 128, dtype=f32), shape(5, C, OUT), shape(5,...]
    all_to_all x1, waiting for transfers between devices: 4.71 us -> 5.97 us  [summed(): return lax.all_to_all(spread, flat, 0, 0, tiled=True).reshape(256, 128)]
    pallas_call x1, Pallas kernels: 3.09 us -> 1.83 us  [body(): call(grad_kernel_body, [shape(C, 3, 8, 128)], 3, flops=170000000, scratch...]
  transfers between devices with their start and end apart: 5 -> 5, of which waited for: 4 -> 4; matrix products, arithmetic and copies ran while one was open for 0% -> 0% of each run, Pallas kernels for 4% -> 2%
where the time goes in v5:
time: 98.3 us; the launch traced here: 97.8 us
  blocking collectives  41.2 us (42%)
  starting transfers between devices  28.7 us (29%)
  waiting for transfers between devices  15.5 us (16%)
  Pallas kernels  9.98 us (10%)
  local copies, waits for them, and re-layouts  1.7 us (2%)
    all_to_all x1, blocking collectives, summed(): parts = lax.all_to_all(spread, 'glong', 0, 0, tiled=True)  18.6 us
    ppermute x1, starting transfers between devices, body(): right = lax.ppermute(low, ('glong', 'ghi'), back)  14.6 us
    all_to_all x1, blocking collectives, summed(): parts = lax.all_to_all(sums.reshape(32, 8, 128), flat, 0, 0, tiled=True)  12.6 us
    all_to_all x1, blocking collectives, body(): faces = lax.all_to_all(faces, 'gz', 0, 0, tiled=True)  9.97 us
    ppermute x1, waiting for transfers between devices, body(): left = lax.ppermute(high, ('glong', 'ghi'), ahead)  6.66 us
    all_to_all x1, waiting for transfers between devices, summed(): return lax.all_to_all(spread, flat, 0, 0, tiled=True).reshape(256, 128)  5.97 us
    all_to_all x1, starting transfers between devices, summed(): return lax.all_to_all(spread, flat, 0, 0, tiled=True).reshape(256, 128)  5.7 us
    pallas_call x1, Pallas kernels, body(): call(conv_kernel, [shape(256, 128, dtype=f32), shape(5, C, OUT), shape(5,...  3.42 us
  transfers between devices with their start and end apart: 5, of which 4 were waited for; matrix products, arithmetic and copies ran while one was open for 0% of the time, Pallas kernels for 2%

profile of v5, /device:TPU:1, one launch (start us, length us, event | category | flops | bytes accessed | tf_op | source)
XLA Modules:
  0.0 97.8 jit_solution(11819001121243380651)
XLA Ops:
  0.6 1.5 %shard_map.144 = (bf16[3,8,32,128]{3,2,1,0:T(8,128)(2,1)S(1)}, bf16[3,8,32,128]{3,2,1,0:T(8,128)(2,1)S(1)}, bf16[1,8,32,128]{3,2,1,0:T(8,128)(2,1)S(1)}) custom-call(bf16[32,3,8,128]{3,2,1,0:T(8,128)(2,1)} %field_hbm.1, bf16[32,3,8,128]{3,2,1,0:T(8,128)(2,1)} %cot_hbm.1), custom_call_target="tpu_custom_call" | custom-call | tf_op jit(solution)/shard_map/pallas_call | solution.py:368
  2.2 14.6 %collective-permute-start.1 = (bf16[3,8,32,128]{3,2,1,0:T(8,128)(2,1)S(1)}, bf16[3,8,32,128]{3,2,1,0:T(8,128)(2,1)S(1)}, u32[]{:S(2)}, u32[]{:S(2)}) collective-permute-start(bf16[3,8,32,128]{3,2,1,0:T(8,128)(2,1)S(1)} %get-tuple-element.34.low_ref), channel_id=1, source_target_pairs={{16,0},{32,16},{48,32},{64,48},{80,64},{96,80},{112,96},{128,112},... | collective-permute-start | bytes 589832 | tf_op jit(solution)/shard_map/ppermute | solution.py:380
  16.8 1.9 %collective-permute-start = (bf16[3,8,32,128]{3,2,1,0:T(8,128)(2,1)S(1)}, bf16[3,8,32,128]{3,2,1,0:T(8,128)(2,1)S(1)}, u32[]{:S(2)}, u32[]{:S(2)}) collective-permute-start(bf16[3,8,32,128]{3,2,1,0:T(8,128)(2,1)S(1)} %get-tuple-element.35.high_ref), channel_id=1, source_target_pairs={{0,16},{16,32},{32,48},{48,64},{64,80},{80,96},{96,112},{112,128},... | collective-permute-start | bytes 589832 | tf_op jit(solution)/shard_map/ppermute | solution.py:379
  18.8 0.6 copy-done.5
  19.3 0.0 copy-done.6
  19.4 0.0 copy-done.2
  19.4 0.0 copy-done.3
  19.4 1.0 %copy-done = f32[32,32,3,3,3]{1,0,4,3,2:T(8,128)S(1)} copy-done((f32[32,32,3,3,3]{1,0,4,3,2:T(8,128)S(1)}, f32[32,32,3,3,3]{1,0,4,3,2:T(8,128)}, u32[]{:S(2)}) %copy-start) | copy-done | bytes 110616
  20.4 0.6 shard_map.145
  21.1 6.7 %collective-permute-done.left_ref = bf16[3,8,32,128]{3,2,1,0:T(8,128)(2,1)S(1)} collective-permute-done((bf16[3,8,32,128]{3,2,1,0:T(8,128)(2,1)S(1)}, bf16[3,8,32,128]{3,2,1,0:T(8,128)(2,1)S(1)}, u32[]{:S(2)}, u32[]{:S(2)}) %collective-permute-start) | collective-permute-done | bytes 196640 | tf_op jit(solution)/shard_map/ppermute | solution.py:379
  27.7 3.1 %collective-permute-start.2 = (bf16[19,32,128]{2,1,0:T(8,128)(2,1)S(1)}, bf16[19,32,128]{2,1,0:T(8,128)(2,1)S(1)}, u32[]{:S(2)}, u32[]{:S(2)}) collective-permute-start(bf16[19,32,128]{2,1,0:T(8,128)(2,1)S(1)} %get-tuple-element.38), channel_id=1, source_target_pairs={{0,4},{4,8},{8,12},{12,0},{1,5},{5,9},{9,13},{13,1},{2,6},{6,10},{... | collective-permute-start | bytes 466952 | tf_op jit(solution)/shard_map/ppermute | solution.py:400
  30.9 3.4 %collective-permute-start.3 = (bf16[19,32,128]{2,1,0:T(8,128)(2,1)S(1)}, bf16[19,32,128]{2,1,0:T(8,128)(2,1)S(1)}, u32[]{:S(2)}, u32[]{:S(2)}) collective-permute-start(bf16[19,32,128]{2,1,0:T(8,128)(2,1)S(1)} %get-tuple-element.39), channel_id=1, source_target_pairs={{4,0},{8,4},{12,8},{0,12},{5,1},{9,5},{13,9},{1,13},{6,2},{10,6},{... | collective-permute-start | bytes 466952 | tf_op jit(solution)/shard_map/ppermute | solution.py:401
  34.2 0.7 collective-permute-done.2.up_ref
  34.9 2.2 %collective-permute-done.3.down_ref = bf16[19,32,128]{2,1,0:T(8,128)(2,1)S(1)} collective-permute-done((bf16[19,32,128]{2,1,0:T(8,128)(2,1)S(1)}, bf16[19,32,128]{2,1,0:T(8,128)(2,1)S(1)}, u32[]{:S(2)}, u32[]{:S(2)}) %collective-permute-start.3) | collective-permute-done | bytes 155680 | tf_op jit(solution)/shard_map/ppermute | solution.py:401
  37.1 0.5 shard_map.147
  37.6 10.0 %all_to_all.20.faces_ref = bf16[4,8,3072]{2,1,0:T(8,128)(2,1)S(1)} all-to-all(bf16[4,8,3072]{2,1,0:T(8,128)(2,1)S(1)} %get-tuple-element.42), channel_id=1, replica_groups=mesh['glong'=16,'ghi'=2,'gy'=4,'gz'=4] {'gz'}, dimensions={0} | all-to-all | bytes 393216 | tf_op jit(solution)/shard_map/all_to_all | solution.py:406
  47.6 3.4 %shard_map.148 = (f32[256,128]{1,0:T(8,128)S(1)}, bf16[5,32,1280]{2,1,0:T(8,128)(2,1)S(1)}, bf16[5,32,128]{2,1,0:T(8,128)(2,1)S(1)}) custom-call(bf16[12,8,32,128]{3,2,1,0:T(8,128)(2,1)S(1)} %get-tuple-element.40.field_ref, bf16[10,8,32,128]{3,2,1,0:T(8,128)(2,1)S(1)} %get-tuple-element.41.cot_ref, bf16[4,8,3072]{2,1,0:T(8,128)(2,1)S(1)} %all_to_all.20.faces_ref, ...), custom_call_target="tpu_custom_call" | custom-call | flops 540000000 | bytes 1048576 | tf_op jit(solution)/shard_map/pallas_call | solution.py:408
  51.0 12.6 %all_to_all.21.parts_ref = f32[32,8,128]{2,1,0:T(8,128)S(1)} all-to-all(f32[32,8,128]{2,1,0:T(8,128)S(1)} %bitcast.21), channel_id=1, replica_groups=mesh['glong'=16,'ghi'=2,'gy'=4,'gz'=4] {'ghi','gy','gz'}, dimensions={0} | all-to-all | bytes 262144 | tf_op jit(solution)/shard_map/all_to_all | solution.py:358
  63.7 18.6 %all_to_all.22.parts_ref = f32[16,8,128]{2,1,0:T(8,128)S(1)} all-to-all(f32[16,8,128]{2,1,0:T(8,128)S(1)} %shard_map.150), channel_id=1, replica_groups=mesh['glong'=16,'ghi'=2,'gy'=4,'gz'=4] {'glong'}, dimensions={0} | all-to-all | bytes 131072 | tf_op jit(solution)/shard_map/all_to_all | solution.py:360
  82.3 0.7 shard_map.151
  83.0 5.7 %all-to-all-start.3 = ((f32[32,8,128]{2,1,0:T(8,128)}), f32[32,8,128]{2,1,0:T(8,128)S(1)}, u32[]{:S(2)}, u32[]{:S(2)}) async-start(f32[32,8,128]{2,1,0:T(8,128)} %shard_map.151), calls=%async_computation.3 | async-start | bytes 262144 | tf_op jit(solution)/shard_map/all_to_all | solution.py:362
  88.7 1.8 %shard_map.149 = bf16[32,3,8,128]{3,2,1,0:T(8,128)(2,1)} custom-call(bf16[5,32,1280]{2,1,0:T(8,128)(2,1)S(1)} %get-tuple-element.44.up_ref, bf16[5,32,128]{2,1,0:T(8,128)(2,1)S(1)} %get-tuple-element.45.rim_ref, bf16[96,288]{1,0:T(8,128)(2,1)S(1)} %get-tuple-element.46.bwd_ref), custom_call_target="tpu_custom_call" | custom-call | flops 170000000 | bytes 1048576 | tf_op jit(solution)/shard_map/pallas_call | solution.py:420
  90.5 6.0 %all-to-all-done.3 = f32[32,8,128]{2,1,0:T(8,128)S(1)} async-done(((f32[32,8,128]{2,1,0:T(8,128)}), f32[32,8,128]{2,1,0:T(8,128)S(1)}, u32[]{:S(2)}, u32[]{:S(2)}) %all-to-all-start.3) | async-done | bytes 131104 | tf_op jit(solution)/shard_map/all_to_all | solution.py:362
  96.5 1.4 %shard_map.152 = (f32[27,32,32]{2,1,0:T(8,128)}, f32[1,32]{1,0:T(1,128)}, f32[2,256]{1,0:T(2,128)}, f32[1,256]{1,0:T(1,128)}, f32[32,256]{1,0:T(8,128)}, /*index=5*/f32[1,32]{1,0:T(1,128)}) custom-call(f32[256,128]{1,0:T(8,128)S(1)} %bitcast.17, f32[32,896]{1,0:T(8,128)S(1)} %get-tuple-element.48.kernel_ref, f32[32,896]{1,0:T(8,128)S(1)} %get-tuple-element.49.modded_ref, ...), custom_call_target="tpu_custom_call" | custom-call | bytes 1048576 | tf_op jit(solution)/shard_map/pallas_call | solution.py:428
  (12 shorter events, 0.1 us)
Async XLA Ops:
  0.6 18.1 %copy-start.1 = (f32[256,32]{0,1:T(8,128)S(1)}, f32[256,32]{0,1:T(8,128)}, u32[]{:S(2)}) copy-start(f32[256,32]{0,1:T(8,128)} %param.14) | copy-start | bytes 98308
  2.2 18.9 %collective-permute-start.1 = (bf16[3,8,32,128]{3,2,1,0:T(8,128)(2,1)S(1)}, bf16[3,8,32,128]{3,2,1,0:T(8,128)(2,1)S(1)}, u32[]{:S(2)}, u32[]{:S(2)}) collective-permute-start(bf16[3,8,32,128]{3,2,1,0:T(8,128)(2,1)S(1)} %get-tuple-element.34.low_ref), channel_id=1, source_target_pairs={{16,0},{32,16},{48,32},{64,48},{80,64},{96,80},{112,96},{128,112},... | collective-permute-start | bytes 589832 | tf_op jit(solution)/shard_map/ppermute | solution.py:380
  16.8 11.0 %collective-permute-start = (bf16[3,8,32,128]{3,2,1,0:T(8,128)(2,1)S(1)}, bf16[3,8,32,128]{3,2,1,0:T(8,128)(2,1)S(1)}, u32[]{:S(2)}, u32[]{:S(2)}) collective-permute-start(bf16[3,8,32,128]{3,2,1,0:T(8,128)(2,1)S(1)} %get-tuple-element.35.high_ref), channel_id=1, source_target_pairs={{0,16},{16,32},{32,48},{48,64},{64,80},{80,96},{96,112},{112,128},... | collective-permute-start | bytes 589832 | tf_op jit(solution)/shard_map/ppermute | solution.py:379
  18.7 0.7 copy-start.5
  18.7 0.7 copy-start.6
  18.7 0.7 copy-start.2
  18.7 0.7 copy-start.3
  18.7 0.7 copy-start.4
  19.4 1.0 %copy-start = (f32[32,32,3,3,3]{1,0,4,3,2:T(8,128)S(1)}, f32[32,32,3,3,3]{1,0,4,3,2:T(8,128)}, u32[]{:S(2)}) copy-start(f32[32,32,3,3,3]{1,0,4,3,2:T(8,128)} %param.16) | copy-start | bytes 331780
  27.7 7.2 %collective-permute-start.2 = (bf16[19,32,128]{2,1,0:T(8,128)(2,1)S(1)}, bf16[19,32,128]{2,1,0:T(8,128)(2,1)S(1)}, u32[]{:S(2)}, u32[]{:S(2)}) collective-permute-start(bf16[19,32,128]{2,1,0:T(8,128)(2,1)S(1)} %get-tuple-element.38), channel_id=1, source_target_pairs={{0,4},{4,8},{8,12},{12,0},{1,5},{5,9},{9,13},{13,1},{2,6},{6,10},{... | collective-permute-start | bytes 466952 | tf_op jit(solution)/shard_map/ppermute | solution.py:400
  30.9 6.3 %collective-permute-start.3 = (bf16[19,32,128]{2,1,0:T(8,128)(2,1)S(1)}, bf16[19,32,128]{2,1,0:T(8,128)(2,1)S(1)}, u32[]{:S(2)}, u32[]{:S(2)}) collective-permute-start(bf16[19,32,128]{2,1,0:T(8,128)(2,1)S(1)} %get-tuple-element.39), channel_id=1, source_target_pairs={{4,0},{8,4},{12,8},{0,12},{5,1},{9,5},{13,9},{1,13},{6,2},{10,6},{... | collective-permute-start | bytes 466952 | tf_op jit(solution)/shard_map/ppermute | solution.py:401
  83.0 13.5 %all-to-all-start.3 = ((f32[32,8,128]{2,1,0:T(8,128)}), f32[32,8,128]{2,1,0:T(8,128)S(1)}, u32[]{:S(2)}, u32[]{:S(2)}) async-start(f32[32,8,128]{2,1,0:T(8,128)} %shard_map.151), calls=%async_computation.3 | async-start | bytes 262144 | tf_op jit(solution)/shard_map/all_to_all | solution.py:362

commit v6 on v5

--- a/solution.py
+++ b/solution.py
@@ -114,11 +114,21 @@
             pick, rows, (((1,), (1,)), ((), ())), preferred_element_type=f32
         )
 
-    both = faces((126, 127, 0, 1), field_out[...].reshape(FIELD_LANES, 128))
-    beside = faces((None, None, None, None, 127, 0), cot_out[...].reshape(COT_LANES, 128))
-    both = jnp.concatenate([both[:, :COT_LANES] + beside, both[:, COT_LANES:]], axis=1).astype(bf16)
-    for n in range(4):
-        faces_ref[n] = both
+    both = faces((126, 127, None, 0, 1, None), field_out[...].reshape(FIELD_LANES, 128))
+    beside = faces((None, None, 127, None, None, 0), cot_out[...].reshape(COT_LANES, 128))
+    both = jnp.concatenate([both[:, :COT_LANES] + beside, both[:, COT_LANES:]], axis=1)
+
+    def chunk(first):
+        return jnp.concatenate(
+            [both[first : first + 4, y * 256 : y * 256 + 256] for y in range(12)], axis=0
+        ).astype(bf16)
+
+    me = lax.axis_index("gz")
+    high = chunk(0)
+    faces_ref[me] = high
+    faces_ref[lax.rem(me + 1, 4)] = high
+    faces_ref[lax.rem(me + 2, 4)] = jnp.zeros_like(high)
+    faces_ref[lax.rem(me + 3, 4)] = chunk(3)
 
 
 def silu_slope(values):
@@ -143,17 +153,32 @@
     def across(rows, place):
         return lax.dot_general(rows, place, (((0,), (0,)), ((), ())), preferred_element_type=f32)
 
-    sides = [faces_ref[at].astype(f32) for at in (before, me, after)]
-    halo[...] = across(
-        jnp.concatenate([sides[0], sides[2]], axis=0).astype(bf16),
-        select((16, 128), 0, 1, (None, 0) + (None,) * 8 + (127,)),
-    ).astype(bf16)
+    sides = jnp.concatenate([faces_ref[at] for at in (before, me, after)], axis=0)
+    row = lax.broadcasted_iota(jnp.int32, (144, 128), 0)
+    to = lax.broadcasted_iota(jnp.int32, (144, 128), 1)
+
+    def spread(moves):
+        place = jnp.zeros((144, 128), f32)
+        for side, k, m in moves:
+            y = (row >> 2) - side * 12
+            hit = ((row & 3) == k) & (to == y * EDGE + m) & (y >= 0) & (y < 12)
+            place = jnp.where(hit, 1.0, place)
+        return across(sides, place.astype(bf16))
+
+    rim = spread(((0, 0, 0), (0, 1, 1), (1, 3, 2), (1, 1, 3), (2, 0, 4), (2, 1, 5)))
+    rim_cot = spread(((0, 2, 0), (2, 2, 3)))
+
+    row = lax.broadcasted_iota(jnp.int32, (128, 12 * 128), 0)
+    to = lax.broadcasted_iota(jnp.int32, (128, 12 * 128), 1)
+    at = (to >> 7) * EDGE
+    place = jnp.where(((to & 127) == 0) & (row == at + 1) | ((to & 127) == 127) & (row == at + 4), 1.0, 0.0)
+    halo[...] = jnp.dot(rim.astype(bf16), place.astype(bf16), preferred_element_type=f32).astype(bf16)
     lane = lax.broadcasted_iota(jnp.int32, (C, 128), 1)
     for x in range(7):
         for y in range(12):
             row = field_ref[y, x]
-            ends = halo[(y * 8 + x) * C : (y * 8 + x) * C + C, :]
             at = slice(y * 128, y * 128 + 128)
+            ends = halo[x * C : x * C + C, at]
             shifted[0, x, :, at] = jnp.where(lane == 0, ends, pltpu.roll(row, 1, 1))
             shifted[1, x, :, at] = row
             shifted[2, x, :, at] = jnp.where(lane == 127, ends, pltpu.roll(row, 127, 1))
@@ -165,24 +190,9 @@
                 else:
                     acc[x - a] += part[a * C : a * C + C]
 
-    def spread(count, moves):
-        rows = jnp.concatenate(
-            [side[:, y * 256 : y * 256 + 256] for side in sides for y in range(count)], axis=0
-        ).astype(bf16)
-        row = lax.broadcasted_iota(jnp.int32, (count * 24, 128), 0)
-        to = lax.broadcasted_iota(jnp.int32, (count * 24, 128), 1)
-        place = jnp.zeros((count * 24, 128), f32)
-        for n, (side, k, m) in enumerate(moves):
-            y = (row >> 3) - side * count
-            hit = ((row & 7) == k) & (to == y * EDGE + m) & (y >= 0) & (y < count)
-            place = jnp.where(hit, 1.0, place)
-        return across(rows, place.astype(bf16))
-
-    rim = spread(12, ((0, 0, 0), (0, 1, 1), (1, 2, 2), (1, 1, 3), (2, 2, 4), (2, 3, 5)))
     for t in range(9):
         shift = (t // 3) * EDGE + t % 3
         edge[t] = (pltpu.roll(rim, 128 - shift, 1) if shift else rim).astype(bf16)
-    rim_cot = spread(10, ((0, 4, 0), (2, 5, 3)))
     block = jnp.concatenate(
         [jnp.concatenate([edge[t, x * C : x * C + C] for t in range(9)], axis=0) for x in range(7)], axis=1
     )
@@ -401,7 +411,7 @@
     down = lax.ppermute(down, "gy", back)
 
     field_rows, cot_rows, faces = call(
-        gather_kernel, [shape(12, 8, C, 128), shape(10, 8, C, 128), shape(4, 8, FIELD_LANES)], 7
+        gather_kernel, [shape(12, 8, C, 128), shape(10, 8, C, 128), shape(4, 48, 256)], 7
     )(*rows, up, down)
     faces = lax.all_to_all(faces, "gz", 0, 0, tiled=True)
 
@@ -411,7 +421,7 @@
         5,
         flops=540_000_000,
         scratch=[
-            pltpu.VMEM((FIELD_LANES, 128), bf16),
+            pltpu.VMEM((8 * C, 12 * 128), bf16),
             pltpu.VMEM((3, 7, C, 12 * 128), bf16),
             pltpu.VMEM((9, 8 * C, 128), bf16),
             pltpu.VMEM((5, C, OUT), f32),

time: 98.3 us -> 97.4 us (level)
  blocking collectives: 41.2 us -> 40.1 us
    all_to_all x1, blocking collectives: 9.97 us -> 8.72 us  [body(): faces = lax.all_to_all(faces, 'gz', 0, 0, tiled=True)]
  transfers between devices with their start and end apart: 5 -> 5, of which waited for: 4 -> 4; matrix products, arithmetic and copies ran while one was open for 0% -> 0% of each run, Pallas kernels for 2% -> 3%
where the time goes in v6:
time: 97.4 us; the launch traced here: 96.9 us
  blocking collectives  40.1 us (41%)
  starting transfers between devices  28.7 us (29%)
  waiting for transfers between devices  15.5 us (16%)
  Pallas kernels  10.1 us (10%)
  local copies, waits for them, and re-layouts  1.7 us (2%)
    all_to_all x1, blocking collectives, summed(): parts = lax.all_to_all(spread, 'glong', 0, 0, tiled=True)  18.6 us
    ppermute x1, starting transfers between devices, body(): right = lax.ppermute(low, ('glong', 'ghi'), back)  14.6 us
    all_to_all x1, blocking collectives, summed(): parts = lax.all_to_all(sums.reshape(32, 8, 128), flat, 0, 0, tiled=True)  12.8 us
    all_to_all x1, blocking collectives, body(): faces = lax.all_to_all(faces, 'gz', 0, 0, tiled=True)  8.72 us
    ppermute x1, waiting for transfers between devices, body(): left = lax.ppermute(high, ('glong', 'ghi'), ahead)  6.66 us
    all_to_all x1, waiting for transfers between devices, summed(): return lax.all_to_all(spread, flat, 0, 0, tiled=True).reshape(256, 128)  5.97 us
    all_to_all x1, starting transfers between devices, summed(): return lax.all_to_all(spread, flat, 0, 0, tiled=True).reshape(256, 128)  5.7 us
    pallas_call x1, Pallas kernels, body(): call(conv_kernel, [shape(256, 128, dtype=f32), shape(5, C, OUT), shape(5,...  3.52 us
  transfers between devices with their start and end apart: 5, of which 4 were waited for; matrix products, arithmetic and copies ran while one was open for 0% of the time, Pallas kernels for 3%

profile of v6, /device:TPU:1, one launch (start us, length us, event | category | flops | bytes accessed | tf_op | source)
XLA Modules:
  0.0 96.9 jit_solution(5532665396915846471)
XLA Ops:
  0.6 1.5 %shard_map.144 = (bf16[3,8,32,128]{3,2,1,0:T(8,128)(2,1)S(1)}, bf16[3,8,32,128]{3,2,1,0:T(8,128)(2,1)S(1)}, bf16[1,8,32,128]{3,2,1,0:T(8,128)(2,1)S(1)}) custom-call(bf16[32,3,8,128]{3,2,1,0:T(8,128)(2,1)} %field_hbm.1, bf16[32,3,8,128]{3,2,1,0:T(8,128)(2,1)} %cot_hbm.1), custom_call_target="tpu_custom_call" | custom-call | tf_op jit(solution)/shard_map/pallas_call | solution.py:378
  2.2 14.6 %collective-permute-start.1 = (bf16[3,8,32,128]{3,2,1,0:T(8,128)(2,1)S(1)}, bf16[3,8,32,128]{3,2,1,0:T(8,128)(2,1)S(1)}, u32[]{:S(2)}, u32[]{:S(2)}) collective-permute-start(bf16[3,8,32,128]{3,2,1,0:T(8,128)(2,1)S(1)} %get-tuple-element.34.low_ref), channel_id=1, source_target_pairs={{16,0},{32,16},{48,32},{64,48},{80,64},{96,80},{112,96},{128,112},... | collective-permute-start | bytes 589832 | tf_op jit(solution)/shard_map/ppermute | solution.py:390
  16.8 1.9 %collective-permute-start = (bf16[3,8,32,128]{3,2,1,0:T(8,128)(2,1)S(1)}, bf16[3,8,32,128]{3,2,1,0:T(8,128)(2,1)S(1)}, u32[]{:S(2)}, u32[]{:S(2)}) collective-permute-start(bf16[3,8,32,128]{3,2,1,0:T(8,128)(2,1)S(1)} %get-tuple-element.35.high_ref), channel_id=1, source_target_pairs={{0,16},{16,32},{32,48},{48,64},{64,80},{80,96},{96,112},{112,128},... | collective-permute-start | bytes 589832 | tf_op jit(solution)/shard_map/ppermute | solution.py:389
  18.8 0.6 copy-done.5
  19.3 0.0 copy-done.6
  19.4 0.0 copy-done.2
  19.4 0.0 copy-done.3
  19.4 1.0 %copy-done = f32[32,32,3,3,3]{1,0,4,3,2:T(8,128)S(1)} copy-done((f32[32,32,3,3,3]{1,0,4,3,2:T(8,128)S(1)}, f32[32,32,3,3,3]{1,0,4,3,2:T(8,128)}, u32[]{:S(2)}) %copy-start) | copy-done | bytes 110616
  20.4 0.6 shard_map.145
  21.1 6.7 %collective-permute-done.left_ref = bf16[3,8,32,128]{3,2,1,0:T(8,128)(2,1)S(1)} collective-permute-done((bf16[3,8,32,128]{3,2,1,0:T(8,128)(2,1)S(1)}, bf16[3,8,32,128]{3,2,1,0:T(8,128)(2,1)S(1)}, u32[]{:S(2)}, u32[]{:S(2)}) %collective-permute-start) | collective-permute-done | bytes 196640 | tf_op jit(solution)/shard_map/ppermute | solution.py:389
  27.7 3.1 %collective-permute-start.2 = (bf16[19,32,128]{2,1,0:T(8,128)(2,1)S(1)}, bf16[19,32,128]{2,1,0:T(8,128)(2,1)S(1)}, u32[]{:S(2)}, u32[]{:S(2)}) collective-permute-start(bf16[19,32,128]{2,1,0:T(8,128)(2,1)S(1)} %get-tuple-element.38), channel_id=1, source_target_pairs={{0,4},{4,8},{8,12},{12,0},{1,5},{5,9},{9,13},{13,1},{2,6},{6,10},{... | collective-permute-start | bytes 466952 | tf_op jit(solution)/shard_map/ppermute | solution.py:410
  30.9 3.4 %collective-permute-start.3 = (bf16[19,32,128]{2,1,0:T(8,128)(2,1)S(1)}, bf16[19,32,128]{2,1,0:T(8,128)(2,1)S(1)}, u32[]{:S(2)}, u32[]{:S(2)}) collective-permute-start(bf16[19,32,128]{2,1,0:T(8,128)(2,1)S(1)} %get-tuple-element.39), channel_id=1, source_target_pairs={{4,0},{8,4},{12,8},{0,12},{5,1},{9,5},{13,9},{1,13},{6,2},{10,6},{... | collective-permute-start | bytes 466952 | tf_op jit(solution)/shard_map/ppermute | solution.py:411
  34.2 0.7 collective-permute-done.2.up_ref
  34.9 2.2 %collective-permute-done.3.down_ref = bf16[19,32,128]{2,1,0:T(8,128)(2,1)S(1)} collective-permute-done((bf16[19,32,128]{2,1,0:T(8,128)(2,1)S(1)}, bf16[19,32,128]{2,1,0:T(8,128)(2,1)S(1)}, u32[]{:S(2)}, u32[]{:S(2)}) %collective-permute-start.3) | collective-permute-done | bytes 155680 | tf_op jit(solution)/shard_map/ppermute | solution.py:411
  37.1 0.5 shard_map.147
  37.7 8.7 %all_to_all.20.faces_ref = bf16[4,48,256]{2,1,0:T(8,128)(2,1)S(1)} all-to-all(bf16[4,48,256]{2,1,0:T(8,128)(2,1)S(1)} %get-tuple-element.42), channel_id=1, replica_groups=mesh['glong'=16,'ghi'=2,'gy'=4,'gz'=4] {'gz'}, dimensions={0} | all-to-all | bytes 196608 | tf_op jit(solution)/shard_map/all_to_all | solution.py:416
  46.4 3.5 %shard_map.148 = (f32[256,128]{1,0:T(8,128)S(1)}, bf16[5,32,1280]{2,1,0:T(8,128)(2,1)S(1)}, bf16[5,32,128]{2,1,0:T(8,128)(2,1)S(1)}) custom-call(bf16[12,8,32,128]{3,2,1,0:T(8,128)(2,1)S(1)} %get-tuple-element.40.field_ref, bf16[10,8,32,128]{3,2,1,0:T(8,128)(2,1)S(1)} %get-tuple-element.41.cot_ref, bf16[4,48,256]{2,1,0:T(8,128)(2,1)S(1)} %all_to_all.20.faces_ref, ...), custom_call_target="tpu_custom_call" | custom-call | flops 540000000 | bytes 1048576 | tf_op jit(solution)/shard_map/pallas_call | solution.py:418
  49.9 12.8 %all_to_all.21.parts_ref = f32[32,8,128]{2,1,0:T(8,128)S(1)} all-to-all(f32[32,8,128]{2,1,0:T(8,128)S(1)} %bitcast.21), channel_id=1, replica_groups=mesh['glong'=16,'ghi'=2,'gy'=4,'gz'=4] {'ghi','gy','gz'}, dimensions={0} | all-to-all | bytes 262144 | tf_op jit(solution)/shard_map/all_to_all | solution.py:368
  62.8 18.6 %all_to_all.22.parts_ref = f32[16,8,128]{2,1,0:T(8,128)S(1)} all-to-all(f32[16,8,128]{2,1,0:T(8,128)S(1)} %shard_map.150), channel_id=1, replica_groups=mesh['glong'=16,'ghi'=2,'gy'=4,'gz'=4] {'glong'}, dimensions={0} | all-to-all | bytes 131072 | tf_op jit(solution)/shard_map/all_to_all | solution.py:370
  81.3 0.7 shard_map.151
  82.0 5.7 %all-to-all-start.3 = ((f32[32,8,128]{2,1,0:T(8,128)}), f32[32,8,128]{2,1,0:T(8,128)S(1)}, u32[]{:S(2)}, u32[]{:S(2)}) async-start(f32[32,8,128]{2,1,0:T(8,128)} %shard_map.151), calls=%async_computation.3 | async-start | bytes 262144 | tf_op jit(solution)/shard_map/all_to_all | solution.py:372
  87.7 1.8 %shard_map.149 = bf16[32,3,8,128]{3,2,1,0:T(8,128)(2,1)} custom-call(bf16[5,32,1280]{2,1,0:T(8,128)(2,1)S(1)} %get-tuple-element.44.up_ref, bf16[5,32,128]{2,1,0:T(8,128)(2,1)S(1)} %get-tuple-element.45.rim_ref, bf16[96,288]{1,0:T(8,128)(2,1)S(1)} %get-tuple-element.46.bwd_ref), custom_call_target="tpu_custom_call" | custom-call | flops 170000000 | bytes 1048576 | tf_op jit(solution)/shard_map/pallas_call | solution.py:430
  89.6 6.0 %all-to-all-done.3 = f32[32,8,128]{2,1,0:T(8,128)S(1)} async-done(((f32[32,8,128]{2,1,0:T(8,128)}), f32[32,8,128]{2,1,0:T(8,128)S(1)}, u32[]{:S(2)}, u32[]{:S(2)}) %all-to-all-start.3) | async-done | bytes 131104 | tf_op jit(solution)/shard_map/all_to_all | solution.py:372
  95.5 1.4 %shard_map.152 = (f32[27,32,32]{2,1,0:T(8,128)}, f32[1,32]{1,0:T(1,128)}, f32[2,256]{1,0:T(2,128)}, f32[1,256]{1,0:T(1,128)}, f32[32,256]{1,0:T(8,128)}, /*index=5*/f32[1,32]{1,0:T(1,128)}) custom-call(f32[256,128]{1,0:T(8,128)S(1)} %bitcast.17, f32[32,896]{1,0:T(8,128)S(1)} %get-tuple-element.48.kernel_ref, f32[32,896]{1,0:T(8,128)S(1)} %get-tuple-element.49.modded_ref, ...), custom_call_target="tpu_custom_call" | custom-call | bytes 1048576 | tf_op jit(solution)/shard_map/pallas_call | solution.py:438
  (12 shorter events, 0.1 us)
Async XLA Ops:
  0.6 18.1 %copy-start.1 = (f32[256,32]{0,1:T(8,128)S(1)}, f32[256,32]{0,1:T(8,128)}, u32[]{:S(2)}) copy-start(f32[256,32]{0,1:T(8,128)} %param.14) | copy-start | bytes 98308
  2.2 18.9 %collective-permute-start.1 = (bf16[3,8,32,128]{3,2,1,0:T(8,128)(2,1)S(1)}, bf16[3,8,32,128]{3,2,1,0:T(8,128)(2,1)S(1)}, u32[]{:S(2)}, u32[]{:S(2)}) collective-permute-start(bf16[3,8,32,128]{3,2,1,0:T(8,128)(2,1)S(1)} %get-tuple-element.34.low_ref), channel_id=1, source_target_pairs={{16,0},{32,16},{48,32},{64,48},{80,64},{96,80},{112,96},{128,112},... | collective-permute-start | bytes 589832 | tf_op jit(solution)/shard_map/ppermute | solution.py:390
  16.8 11.0 %collective-permute-start = (bf16[3,8,32,128]{3,2,1,0:T(8,128)(2,1)S(1)}, bf16[3,8,32,128]{3,2,1,0:T(8,128)(2,1)S(1)}, u32[]{:S(2)}, u32[]{:S(2)}) collective-permute-start(bf16[3,8,32,128]{3,2,1,0:T(8,128)(2,1)S(1)} %get-tuple-element.35.high_ref), channel_id=1, source_target_pairs={{0,16},{16,32},{32,48},{48,64},{64,80},{80,96},{96,112},{112,128},... | collective-permute-start | bytes 589832 | tf_op jit(solution)/shard_map/ppermute | solution.py:389
  18.7 0.7 copy-start.5
  18.7 0.7 copy-start.6
  18.7 0.7 copy-start.2
  18.7 0.7 copy-start.3
  18.7 0.7 copy-start.4
  19.4 1.0 %copy-start = (f32[32,32,3,3,3]{1,0,4,3,2:T(8,128)S(1)}, f32[32,32,3,3,3]{1,0,4,3,2:T(8,128)}, u32[]{:S(2)}) copy-start(f32[32,32,3,3,3]{1,0,4,3,2:T(8,128)} %param.16) | copy-start | bytes 331780
  27.7 7.2 %collective-permute-start.2 = (bf16[19,32,128]{2,1,0:T(8,128)(2,1)S(1)}, bf16[19,32,128]{2,1,0:T(8,128)(2,1)S(1)}, u32[]{:S(2)}, u32[]{:S(2)}) collective-permute-start(bf16[19,32,128]{2,1,0:T(8,128)(2,1)S(1)} %get-tuple-element.38), channel_id=1, source_target_pairs={{0,4},{4,8},{8,12},{12,0},{1,5},{5,9},{9,13},{13,1},{2,6},{6,10},{... | collective-permute-start | bytes 466952 | tf_op jit(solution)/shard_map/ppermute | solution.py:410
  30.9 6.3 %collective-permute-start.3 = (bf16[19,32,128]{2,1,0:T(8,128)(2,1)S(1)}, bf16[19,32,128]{2,1,0:T(8,128)(2,1)S(1)}, u32[]{:S(2)}, u32[]{:S(2)}) collective-permute-start(bf16[19,32,128]{2,1,0:T(8,128)(2,1)S(1)} %get-tuple-element.39), channel_id=1, source_target_pairs={{4,0},{8,4},{12,8},{0,12},{5,1},{9,5},{13,9},{1,13},{6,2},{10,6},{... | collective-permute-start | bytes 466952 | tf_op jit(solution)/shard_map/ppermute | solution.py:411
  82.0 13.5 %all-to-all-start.3 = ((f32[32,8,128]{2,1,0:T(8,128)}), f32[32,8,128]{2,1,0:T(8,128)S(1)}, u32[]{:S(2)}, u32[]{:S(2)}) async-start(f32[32,8,128]{2,1,0:T(8,128)} %shard_map.151), calls=%async_computation.3 | async-start | bytes 262144 | tf_op jit(solution)/shard_map/all_to_all | solution.py:372

commit v7 on v6

--- a/solution.py
+++ b/solution.py
@@ -143,7 +143,7 @@
 
 
 def conv_kernel(
-    field_ref, cot_ref, faces_ref, fwd_ref, offset_ref,
+    field_ref, cot_ref, faces_ref, fwd_ref, offset_ref, place_ref,
     sums_ref, up_ref, rim_ref,
     halo, shifted, edge, acc,
 ):
@@ -154,25 +154,9 @@
         return lax.dot_general(rows, place, (((0,), (0,)), ((), ())), preferred_element_type=f32)
 
     sides = jnp.concatenate([faces_ref[at] for at in (before, me, after)], axis=0)
-    row = lax.broadcasted_iota(jnp.int32, (144, 128), 0)
-    to = lax.broadcasted_iota(jnp.int32, (144, 128), 1)
-
-    def spread(moves):
-        place = jnp.zeros((144, 128), f32)
-        for side, k, m in moves:
-            y = (row >> 2) - side * 12
-            hit = ((row & 3) == k) & (to == y * EDGE + m) & (y >= 0) & (y < 12)
-            place = jnp.where(hit, 1.0, place)
-        return across(sides, place.astype(bf16))
-
-    rim = spread(((0, 0, 0), (0, 1, 1), (1, 3, 2), (1, 1, 3), (2, 0, 4), (2, 1, 5)))
-    rim_cot = spread(((0, 2, 0), (2, 2, 3)))
-
-    row = lax.broadcasted_iota(jnp.int32, (128, 12 * 128), 0)
-    to = lax.broadcasted_iota(jnp.int32, (128, 12 * 128), 1)
-    at = (to >> 7) * EDGE
-    place = jnp.where(((to & 127) == 0) & (row == at + 1) | ((to & 127) == 127) & (row == at + 4), 1.0, 0.0)
-    halo[...] = jnp.dot(rim.astype(bf16), place.astype(bf16), preferred_element_type=f32).astype(bf16)
+    spread = across(sides, place_ref[...])
+    rim, rim_cot = spread[:, :128], spread[:, 128:256]
+    halo[...] = spread[:, 256:].astype(bf16)
     lane = lax.broadcasted_iota(jnp.int32, (C, 128), 1)
     for x in range(7):
         for y in range(12):
@@ -242,7 +226,8 @@
                 sums_ref[at : at + 8] = jnp.zeros((8, 128), f32)
 
 
-def grad_kernel_body(up_ref, rim_ref, bwd_ref, grad_ref, shifted, acc):
+def grad_kernel_body(up_ref, rim_ref, bwd_ref, grad_ref, done_ref, shifted, acc):
+    done_ref[...] = jnp.zeros_like(done_ref)
     lane = lax.broadcasted_iota(jnp.int32, (C, 128), 1)
     for x in range(5):
         rim = rim_ref[x].astype(f32)
@@ -279,10 +264,31 @@
     )
 
 
+def fill_places(place_ref):
+    row = lax.broadcasted_iota(jnp.int32, (144, 128), 0)
+    to = lax.broadcasted_iota(jnp.int32, (144, 128), 1)
+    y, k = row >> 2, row & 3
+
+    def place(moves):
+        hit = jnp.zeros((144, 128), f32)
+        for side, face, lane in moves:
+            inside = (y >= side * 12) & (y < side * 12 + 12)
+            hit = jnp.where(inside & (k == face) & (to == (y - side * 12) * EDGE + lane), 1.0, hit)
+        return hit.astype(bf16)
+
+    place_ref[:, :128] = place(((0, 0, 0), (0, 1, 1), (1, 3, 2), (1, 1, 3), (2, 0, 4), (2, 1, 5)))
+    place_ref[:, 128:256] = place(((0, 2, 0), (2, 2, 3)))
+    for n in range(12):
+        ends = (to == 0) & (row == n * 4 + 1) | (to == 127) & (row == (24 + n) * 4)
+        place_ref[:, 256 + n * 128 : 384 + n * 128] = jnp.where(ends, 1.0, 0.0).astype(bf16)
+
+
 def modulate_kernel(
     cosmology_ref, lift_ref, bias_ref, weight_ref, sbias_ref, taps_ref, offset_ref,
     fwd_ref, bwd_ref, kernel_ref, modded_ref, styles_ref, inv_ref, lifted_ref, hidden_ref, params_ref, column_ref,
+    place_ref,
 ):
+    fill_places(place_ref)
     first, second = cosmology_ref[:, 0:1], cosmology_ref[:, 1:2]
     lifted = first * lift_ref[0:1] + second * lift_ref[1:2] + bias_ref[...]
     hidden = lifted * jax.nn.sigmoid(lifted)
@@ -311,7 +317,8 @@
     column_ref[...] = jnp.sum(offset_ref[...] * eye, axis=1, keepdims=True)
 
 
-def total_kernel(parts_ref, spread_ref):
+def total_kernel(parts_ref, *rest):
+    spread_ref = rest[-1]
     part = jnp.sum(parts_ref[...], axis=0)
     for n in range(spread_ref.shape[0]):
         spread_ref[n] = part
@@ -363,12 +370,12 @@
     return ahead, [(j, i) for i, j in ahead]
 
 
-def summed(sums):
+def summed(sums, first):
     flat = ("ghi", "gy", "gz")
     parts = lax.all_to_all(sums.reshape(32, 8, 128), flat, 0, 0, tiled=True)
     (spread,) = call(total_kernel, [shape(16, 8, 128, dtype=f32)], 1, limit=4)(parts)
     parts = lax.all_to_all(spread, "glong", 0, 0, tiled=True)
-    (spread,) = call(total_kernel, [shape(32, 8, 128, dtype=f32)], 1, limit=4)(parts)
+    (spread,) = call(total_kernel, [shape(32, 8, 128, dtype=f32)], 2, limit=4)(parts, first)
     return lax.all_to_all(spread, flat, 0, 0, tiled=True).reshape(256, 128)
 
 
@@ -390,12 +397,12 @@
     right = lax.ppermute(low, ("glong", "ghi"), back)
 
     taps = jnp.transpose(kernel, (2, 3, 4, 0, 1)).reshape(TAPS, C, C)
-    fwd, bwd, packed, modded, styles, inv_norm, lifted, hidden, params, column = call(
+    fwd, bwd, packed, modded, styles, inv_norm, lifted, hidden, params, column, place = call(
         modulate_kernel,
         [
             shape(3 * C, 9 * C), shape(3 * C, 9 * C), shape(C, 896, dtype=f32), shape(C, 896, dtype=f32),
             shape(1, 896, dtype=f32), shape(C, 1, dtype=f32), shape(1, 256, dtype=f32), shape(1, 256, dtype=f32),
-            shape(2, 1, dtype=f32), shape(C, 1, dtype=f32),
+            shape(2, 1, dtype=f32), shape(C, 1, dtype=f32), shape(144, 14 * 128),
         ],
         7,
         limit=8,
@@ -418,7 +425,7 @@
     sums, upstream, rim = call(
         conv_kernel,
         [shape(256, 128, dtype=f32), shape(5, C, OUT), shape(5, C, 128)],
-        5,
+        6,
         flops=540_000_000,
         scratch=[
             pltpu.VMEM((8 * C, 12 * 128), bf16),
@@ -426,10 +433,10 @@
             pltpu.VMEM((9, 8 * C, 128), bf16),
             pltpu.VMEM((5, C, OUT), f32),
         ],
-    )(field_rows, cot_rows, faces, fwd, column)
-    (grad_field,) = call(
+    )(field_rows, cot_rows, faces, fwd, column, place)
+    grad_field, done = call(
         grad_kernel_body,
-        [shape(C, 3, 8, 128)],
+        [shape(C, 3, 8, 128), shape(8, 128, dtype=f32)],
         3,
         flops=170_000_000,
         scratch=[pltpu.VMEM((3, 5, C, OUT), bf16), pltpu.VMEM((3, C, OWN), f32)],
@@ -444,7 +451,7 @@
         9,
         limit=8,
     )(
-        summed(sums), packed, modded, styles, inv_norm, lifted, hidden, style_weight.T, params,
+        summed(sums, done), packed, modded, styles, inv_norm, lifted, hidden, style_weight.T, params,
     )
     grad_kernel = jnp.transpose(kernel_out.reshape(3, 3, 3, C, C), (3, 4, 0, 1, 2))
     return (

time: 97.4 us -> 96.8 us (level)
  blocking collectives: 40.1 us -> 34.6 us
  waiting for transfers between devices: 15.5 us -> 19.2 us
  starting transfers between devices: 28.7 us -> 30.2 us
    all_to_all x1, blocking collectives: 18.6 us -> 13 us  [summed(): return lax.all_to_all(spread, flat, 0, 0, tiled=True).reshape(256, 128)]
    all_to_all x1, waiting for transfers between devices: 5.97 us -> 9.73 us  [summed(): parts = lax.all_to_all(spread, 'glong', 0, 0, tiled=True)]
    all_to_all x1, starting transfers between devices: 5.7 us -> 7.21 us  [summed(): parts = lax.all_to_all(spread, 'glong', 0, 0, tiled=True)]
where the time goes in v7:
time: 96.8 us; the launch traced here: 96.4 us
  blocking collectives  34.6 us (36%)
  starting transfers between devices  30.2 us (31%)
  waiting for transfers between devices  19.2 us (20%)
  Pallas kernels  9.9 us (10%)
  local copies, waits for them, and re-layouts  1.7 us (2%)
    ppermute x1, starting transfers between devices, body(): right = lax.ppermute(low, ('glong', 'ghi'), back)  14.6 us
    all_to_all x1, blocking collectives, summed(): return lax.all_to_all(spread, flat, 0, 0, tiled=True).reshape(256, 128)  13 us
    all_to_all x1, blocking collectives, summed(): parts = lax.all_to_all(sums.reshape(32, 8, 128), flat, 0, 0, tiled=True)  12.8 us
    all_to_all x1, waiting for transfers between devices, summed(): parts = lax.all_to_all(spread, 'glong', 0, 0, tiled=True)  9.73 us
    all_to_all x1, blocking collectives, body(): faces = lax.all_to_all(faces, 'gz', 0, 0, tiled=True)  8.72 us
    all_to_all x1, starting transfers between devices, summed(): parts = lax.all_to_all(spread, 'glong', 0, 0, tiled=True)  7.21 us
    ppermute x1, waiting for transfers between devices, body(): left = lax.ppermute(high, ('glong', 'ghi'), ahead)  6.57 us
    ppermute x1, starting transfers between devices, body(): down = lax.ppermute(down, 'gy', back)  3.38 us
  transfers between devices with their start and end apart: 5, of which 4 were waited for; matrix products, arithmetic and copies ran while one was open for 0% of the time, Pallas kernels for 3%

profile of v7, /device:TPU:1, one launch (start us, length us, event | category | flops | bytes accessed | tf_op | source)
XLA Modules:
  0.0 96.4 jit_solution(16184877629965169662)
XLA Ops:
  0.6 1.5 %shard_map.144 = (bf16[3,8,32,128]{3,2,1,0:T(8,128)(2,1)S(1)}, bf16[3,8,32,128]{3,2,1,0:T(8,128)(2,1)S(1)}, bf16[1,8,32,128]{3,2,1,0:T(8,128)(2,1)S(1)}) custom-call(bf16[32,3,8,128]{3,2,1,0:T(8,128)(2,1)} %field_hbm.1, bf16[32,3,8,128]{3,2,1,0:T(8,128)(2,1)} %cot_hbm.1), custom_call_target="tpu_custom_call" | custom-call | tf_op jit(solution)/shard_map/pallas_call | solution.py:385
  2.2 14.6 %collective-permute-start.1 = (bf16[3,8,32,128]{3,2,1,0:T(8,128)(2,1)S(1)}, bf16[3,8,32,128]{3,2,1,0:T(8,128)(2,1)S(1)}, u32[]{:S(2)}, u32[]{:S(2)}) collective-permute-start(bf16[3,8,32,128]{3,2,1,0:T(8,128)(2,1)S(1)} %get-tuple-element.37.low_ref), channel_id=1, source_target_pairs={{16,0},{32,16},{48,32},{64,48},{80,64},{96,80},{112,96},{128,112},... | collective-permute-start | bytes 589832 | tf_op jit(solution)/shard_map/ppermute | solution.py:397
  16.8 1.9 %collective-permute-start = (bf16[3,8,32,128]{3,2,1,0:T(8,128)(2,1)S(1)}, bf16[3,8,32,128]{3,2,1,0:T(8,128)(2,1)S(1)}, u32[]{:S(2)}, u32[]{:S(2)}) collective-permute-start(bf16[3,8,32,128]{3,2,1,0:T(8,128)(2,1)S(1)} %get-tuple-element.38.high_ref), channel_id=1, source_target_pairs={{0,16},{16,32},{32,48},{48,64},{64,80},{80,96},{96,112},{112,128},... | collective-permute-start | bytes 589832 | tf_op jit(solution)/shard_map/ppermute | solution.py:396
  18.8 0.6 copy-done.5
  19.3 0.0 copy-done.6
  19.4 0.0 copy-done.2
  19.4 0.0 copy-done.3
  19.4 1.0 %copy-done = f32[32,32,3,3,3]{1,0,4,3,2:T(8,128)S(1)} copy-done((f32[32,32,3,3,3]{1,0,4,3,2:T(8,128)S(1)}, f32[32,32,3,3,3]{1,0,4,3,2:T(8,128)}, u32[]{:S(2)}) %copy-start) | copy-done | bytes 110616
  20.4 0.7 shard_map.145
  21.1 6.6 %collective-permute-done.left_ref = bf16[3,8,32,128]{3,2,1,0:T(8,128)(2,1)S(1)} collective-permute-done((bf16[3,8,32,128]{3,2,1,0:T(8,128)(2,1)S(1)}, bf16[3,8,32,128]{3,2,1,0:T(8,128)(2,1)S(1)}, u32[]{:S(2)}, u32[]{:S(2)}) %collective-permute-start) | collective-permute-done | bytes 196640 | tf_op jit(solution)/shard_map/ppermute | solution.py:396
  27.7 3.1 %collective-permute-start.2 = (bf16[19,32,128]{2,1,0:T(8,128)(2,1)S(1)}, bf16[19,32,128]{2,1,0:T(8,128)(2,1)S(1)}, u32[]{:S(2)}, u32[]{:S(2)}) collective-permute-start(bf16[19,32,128]{2,1,0:T(8,128)(2,1)S(1)} %get-tuple-element.41), channel_id=1, source_target_pairs={{0,4},{4,8},{8,12},{12,0},{1,5},{5,9},{9,13},{13,1},{2,6},{6,10},{... | collective-permute-start | bytes 466952 | tf_op jit(solution)/shard_map/ppermute | solution.py:417
  30.9 3.4 %collective-permute-start.3 = (bf16[19,32,128]{2,1,0:T(8,128)(2,1)S(1)}, bf16[19,32,128]{2,1,0:T(8,128)(2,1)S(1)}, u32[]{:S(2)}, u32[]{:S(2)}) collective-permute-start(bf16[19,32,128]{2,1,0:T(8,128)(2,1)S(1)} %get-tuple-element.42), channel_id=1, source_target_pairs={{4,0},{8,4},{12,8},{0,12},{5,1},{9,5},{13,9},{1,13},{6,2},{10,6},{... | collective-permute-start | bytes 466952 | tf_op jit(solution)/shard_map/ppermute | solution.py:418
  34.2 0.7 collective-permute-done.2.up_ref
  34.9 2.2 %collective-permute-done.3.down_ref = bf16[19,32,128]{2,1,0:T(8,128)(2,1)S(1)} collective-permute-done((bf16[19,32,128]{2,1,0:T(8,128)(2,1)S(1)}, bf16[19,32,128]{2,1,0:T(8,128)(2,1)S(1)}, u32[]{:S(2)}, u32[]{:S(2)}) %collective-permute-start.3) | collective-permute-done | bytes 155680 | tf_op jit(solution)/shard_map/ppermute | solution.py:418
  37.1 0.5 shard_map.147
  37.7 8.7 %all_to_all.20.faces_ref = bf16[4,48,256]{2,1,0:T(8,128)(2,1)S(1)} all-to-all(bf16[4,48,256]{2,1,0:T(8,128)(2,1)S(1)} %get-tuple-element.45), channel_id=1, replica_groups=mesh['glong'=16,'ghi'=2,'gy'=4,'gz'=4] {'gz'}, dimensions={0} | all-to-all | bytes 196608 | tf_op jit(solution)/shard_map/all_to_all | solution.py:423
  46.4 3.2 %shard_map.148 = (f32[256,128]{1,0:T(8,128)S(1)}, bf16[5,32,1280]{2,1,0:T(8,128)(2,1)S(1)}, bf16[5,32,128]{2,1,0:T(8,128)(2,1)S(1)}) custom-call(bf16[12,8,32,128]{3,2,1,0:T(8,128)(2,1)S(1)} %get-tuple-element.43.field_ref, bf16[10,8,32,128]{3,2,1,0:T(8,128)(2,1)S(1)} %get-tuple-element.44.cot_ref, bf16[4,48,256]{2,1,0:T(8,128)(2,1)S(1)} %all_to_all.20.faces_ref, ...), custom_call_target="tpu_custom_call" | custom-call | flops 540000000 | bytes 1048576 | tf_op jit(solution)/shard_map/pallas_call | solution.py:425
  49.6 12.8 %all_to_all.21.parts_ref = f32[32,8,128]{2,1,0:T(8,128)S(1)} all-to-all(f32[32,8,128]{2,1,0:T(8,128)S(1)} %bitcast.21), channel_id=1, replica_groups=mesh['glong'=16,'ghi'=2,'gy'=4,'gz'=4] {'ghi','gy','gz'}, dimensions={0} | all-to-all | bytes 262144 | tf_op jit(solution)/shard_map/all_to_all | solution.py:375
  62.5 0.7 shard_map.150
  63.1 7.2 %all-to-all-start.2 = ((f32[16,8,128]{2,1,0:T(8,128)}), f32[16,8,128]{2,1,0:T(8,128)S(1)}, u32[]{:S(2)}, u32[]{:S(2)}) async-start(f32[16,8,128]{2,1,0:T(8,128)} %shard_map.150), calls=%async_computation.2 | async-start | bytes 131072 | tf_op jit(solution)/shard_map/all_to_all | solution.py:377
  70.3 1.8 %shard_map.149 = (bf16[32,3,8,128]{3,2,1,0:T(8,128)(2,1)}, f32[8,128]{1,0:T(8,128)S(1)}) custom-call(bf16[5,32,1280]{2,1,0:T(8,128)(2,1)S(1)} %get-tuple-element.48.up_ref, bf16[5,32,128]{2,1,0:T(8,128)(2,1)S(1)} %get-tuple-element.49.rim_ref, bf16[96,288]{1,0:T(8,128)(2,1)S(1)} %get-tuple-element.50.bwd_ref), custom_call_target="tpu_custom_call" | custom-call | flops 170000000 | bytes 1048576 | tf_op jit(solution)/shard_map/pallas_call | solution.py:437
  72.2 9.7 %all-to-all-done.2.parts_ref = f32[16,8,128]{2,1,0:T(8,128)S(1)} async-done(((f32[16,8,128]{2,1,0:T(8,128)}), f32[16,8,128]{2,1,0:T(8,128)S(1)}, u32[]{:S(2)}, u32[]{:S(2)}) %all-to-all-start.2) | async-done | bytes 65568 | tf_op jit(solution)/shard_map/all_to_all | solution.py:377
  81.9 13.0 %all_to_all.22 = f32[32,8,128]{2,1,0:T(8,128)S(1)} all-to-all(f32[32,8,128]{2,1,0:T(8,128)S(1)} %shard_map.151), channel_id=1, replica_groups=mesh['glong'=16,'ghi'=2,'gy'=4,'gz'=4] {'ghi','gy','gz'}, dimensions={0} | all-to-all | bytes 262144 | tf_op jit(solution)/shard_map/all_to_all | solution.py:379
  95.0 1.4 %shard_map.152 = (f32[27,32,32]{2,1,0:T(8,128)}, f32[1,32]{1,0:T(1,128)}, f32[2,256]{1,0:T(2,128)}, f32[1,256]{1,0:T(1,128)}, f32[32,256]{1,0:T(8,128)}, /*index=5*/f32[1,32]{1,0:T(1,128)}) custom-call(f32[256,128]{1,0:T(8,128)S(1)} %bitcast.17, f32[32,896]{1,0:T(8,128)S(1)} %get-tuple-element.54.kernel_ref, f32[32,896]{1,0:T(8,128)S(1)} %get-tuple-element.55.modded_ref, ...), custom_call_target="tpu_custom_call" | custom-call | bytes 1048576 | tf_op jit(solution)/shard_map/pallas_call | solution.py:445
  (12 shorter events, 0.1 us)
Async XLA Ops:
  0.6 18.1 %copy-start.1 = (f32[256,32]{0,1:T(8,128)S(1)}, f32[256,32]{0,1:T(8,128)}, u32[]{:S(2)}) copy-start(f32[256,32]{0,1:T(8,128)} %param.14) | copy-start | bytes 98308
  2.2 19.0 %collective-permute-start.1 = (bf16[3,8,32,128]{3,2,1,0:T(8,128)(2,1)S(1)}, bf16[3,8,32,128]{3,2,1,0:T(8,128)(2,1)S(1)}, u32[]{:S(2)}, u32[]{:S(2)}) collective-permute-start(bf16[3,8,32,128]{3,2,1,0:T(8,128)(2,1)S(1)} %get-tuple-element.37.low_ref), channel_id=1, source_target_pairs={{16,0},{32,16},{48,32},{64,48},{80,64},{96,80},{112,96},{128,112},... | collective-permute-start | bytes 589832 | tf_op jit(solution)/shard_map/ppermute | solution.py:397
  16.8 11.0 %collective-permute-start = (bf16[3,8,32,128]{3,2,1,0:T(8,128)(2,1)S(1)}, bf16[3,8,32,128]{3,2,1,0:T(8,128)(2,1)S(1)}, u32[]{:S(2)}, u32[]{:S(2)}) collective-permute-start(bf16[3,8,32,128]{3,2,1,0:T(8,128)(2,1)S(1)} %get-tuple-element.38.high_ref), channel_id=1, source_target_pairs={{0,16},{16,32},{32,48},{48,64},{64,80},{80,96},{96,112},{112,128},... | collective-permute-start | bytes 589832 | tf_op jit(solution)/shard_map/ppermute | solution.py:396
  18.7 0.7 copy-start.5
  18.7 0.7 copy-start.6
  18.7 0.7 copy-start.2
  18.7 0.7 copy-start.3
  18.7 0.7 copy-start.4
  19.4 1.0 %copy-start = (f32[32,32,3,3,3]{1,0,4,3,2:T(8,128)S(1)}, f32[32,32,3,3,3]{1,0,4,3,2:T(8,128)}, u32[]{:S(2)}) copy-start(f32[32,32,3,3,3]{1,0,4,3,2:T(8,128)} %param.16) | copy-start | bytes 331780
  27.7 7.2 %collective-permute-start.2 = (bf16[19,32,128]{2,1,0:T(8,128)(2,1)S(1)}, bf16[19,32,128]{2,1,0:T(8,128)(2,1)S(1)}, u32[]{:S(2)}, u32[]{:S(2)}) collective-permute-start(bf16[19,32,128]{2,1,0:T(8,128)(2,1)S(1)} %get-tuple-element.41), channel_id=1, source_target_pairs={{0,4},{4,8},{8,12},{12,0},{1,5},{5,9},{9,13},{13,1},{2,6},{6,10},{... | collective-permute-start | bytes 466952 | tf_op jit(solution)/shard_map/ppermute | solution.py:417
  30.9 6.3 %collective-permute-start.3 = (bf16[19,32,128]{2,1,0:T(8,128)(2,1)S(1)}, bf16[19,32,128]{2,1,0:T(8,128)(2,1)S(1)}, u32[]{:S(2)}, u32[]{:S(2)}) collective-permute-start(bf16[19,32,128]{2,1,0:T(8,128)(2,1)S(1)} %get-tuple-element.42), channel_id=1, source_target_pairs={{4,0},{8,4},{12,8},{0,12},{5,1},{9,5},{13,9},{1,13},{6,2},{10,6},{... | collective-permute-start | bytes 466952 | tf_op jit(solution)/shard_map/ppermute | solution.py:418
  63.1 18.8 %all-to-all-start.2 = ((f32[16,8,128]{2,1,0:T(8,128)}), f32[16,8,128]{2,1,0:T(8,128)S(1)}, u32[]{:S(2)}, u32[]{:S(2)}) async-start(f32[16,8,128]{2,1,0:T(8,128)} %shard_map.150), calls=%async_computation.2 | async-start | bytes 131072 | tf_op jit(solution)/shard_map/all_to_all | solution.py:377

commit v8 on v7

--- a/solution.py
+++ b/solution.py
@@ -14,8 +14,8 @@
 EDGE = 6
 FIELD_LANES = 12 * 8 * C
 COT_LANES = 10 * 8 * C
-OUT = 10 * 128
 OWN = 8 * 128
+WITH_RIM = 9 * 128
 f32 = jnp.float32
 bf16 = jnp.bfloat16
 VMEM = pl.BlockSpec(memory_space=pltpu.VMEM)
@@ -47,7 +47,7 @@
     return hit.astype(bf16)
 
 
-def split_kernel(field_hbm, cot_hbm, low_ref, high_ref, mid_ref, field_ref, cot_ref, sems):
+def split_kernel(field_hbm, cot_hbm, low_ref, rest_ref, field_ref, cot_ref, sems):
     fetches = (
         pltpu.make_async_copy(field_hbm, field_ref, sems.at[0]),
         pltpu.make_async_copy(cot_hbm, cot_ref, sems.at[1]),
@@ -63,50 +63,35 @@
         return jnp.dot(perm, block, preferred_element_type=f32).astype(bf16).reshape(8, C, 128)
 
     fetches[0].wait()
-    f0, f1, f2 = (rows(field_ref, x) for x in range(3))
-    low_ref[0], low_ref[1] = f0, f1
-    high_ref[0], high_ref[1] = f1, f2
+    low_ref[0], low_ref[1], rest_ref[0] = (rows(field_ref, x) for x in range(3))
     fetches[1].wait()
-    c0, c1, c2 = (rows(cot_ref, x) for x in range(3))
-    low_ref[2], high_ref[2], mid_ref[0] = c0, c2, c1
-
-
-def planes(low_ref, high_ref, mid_ref, left_ref, right_ref):
-    field = (
-        (left_ref, 0), (left_ref, 1), (low_ref, 0), (low_ref, 1), (high_ref, 1), (right_ref, 0), (right_ref, 1),
-    )
-    cot = ((left_ref, 2), (low_ref, 2), (mid_ref, 0), (high_ref, 2), (right_ref, 2))
+    low_ref[2], rest_ref[1], rest_ref[2] = (rows(cot_ref, x) for x in range(3))
+
+
+def planes(low_ref, rest_ref, right_ref):
+    field = ((low_ref, 0), (low_ref, 1), (rest_ref, 0), (right_ref, 0), (right_ref, 1))
+    cot = ((rest_ref, 1), (rest_ref, 2), (right_ref, 2))
     return field, cot
 
 
-def pack_kernel(low_ref, high_ref, mid_ref, left_ref, right_ref, _, up_ref, down_ref):
-    field, cot = planes(low_ref, high_ref, mid_ref, left_ref, right_ref)
+def pack_kernel(low_ref, rest_ref, right_ref, _, down_ref):
+    field, cot = planes(low_ref, rest_ref, right_ref)
     for n, (ref, at) in enumerate(field):
-        up_ref[2 * n : 2 * n + 2] = ref[at, 6:8]
         down_ref[2 * n : 2 * n + 2] = ref[at, 0:2]
     for n, (ref, at) in enumerate(cot):
-        up_ref[14 + n] = ref[at, 7]
-        down_ref[14 + n] = ref[at, 0]
-
-
-def gather_kernel(
-    low_ref, high_ref, mid_ref, left_ref, right_ref, up_ref, down_ref, field_out, cot_out, faces_ref
-):
-    field, cot = planes(low_ref, high_ref, mid_ref, left_ref, right_ref)
+        down_ref[10 + n] = ref[at, 0]
+
+
+def gather_kernel(low_ref, rest_ref, right_ref, down_ref, field_out, cot_out, faces_ref):
+    field, cot = planes(low_ref, rest_ref, right_ref)
+    field_out[...] = jnp.zeros_like(field_out)
+    cot_out[...] = jnp.zeros_like(cot_out)
     for n, (ref, at) in enumerate(field):
-        for y in range(12):
-            if y < 2:
-                row = up_ref[2 * n + y]
-            elif y < 10:
-                row = ref[at, y - 2]
-            else:
-                row = down_ref[2 * n + y - 10]
-            field_out[y, n] = row
-    field_out[:, 7:] = jnp.zeros((12, 1, C, 128), bf16)
+        for y in range(10):
+            field_out[y, n] = ref[at, y] if y < 8 else down_ref[2 * n + y - 8]
     for n, (ref, at) in enumerate(cot):
-        for y in range(10):
-            cot_out[y, n] = up_ref[14 + n] if y == 0 else down_ref[14 + n] if y == 9 else ref[at, y - 1]
-    cot_out[:, 5:] = jnp.zeros((10, 3, C, 128), bf16)
+        for y in range(8):
+            cot_out[y, n] = ref[at, y + 1] if y < 7 else down_ref[10 + n]
 
     def faces(lanes, rows):
         pick = select((8, 128), 0, 1, lanes)
@@ -144,7 +129,7 @@
 
 def conv_kernel(
     field_ref, cot_ref, faces_ref, fwd_ref, offset_ref, place_ref,
-    sums_ref, up_ref, rim_ref,
+    sums_ref, up_ref, send_ref,
     halo, shifted, edge, acc,
 ):
     me = lax.axis_index("gz")
@@ -158,17 +143,17 @@
     rim, rim_cot = spread[:, :128], spread[:, 128:256]
     halo[...] = spread[:, 256:].astype(bf16)
     lane = lax.broadcasted_iota(jnp.int32, (C, 128), 1)
-    for x in range(7):
-        for y in range(12):
+    for x in range(5):
+        for y in range(10):
             row = field_ref[y, x]
             at = slice(y * 128, y * 128 + 128)
             ends = halo[x * C : x * C + C, at]
             shifted[0, x, :, at] = jnp.where(lane == 0, ends, pltpu.roll(row, 1, 1))
             shifted[1, x, :, at] = row
             shifted[2, x, :, at] = jnp.where(lane == 127, ends, pltpu.roll(row, 127, 1))
-        part = jnp.dot(fwd_ref[...], row_taps(shifted, x, OUT), preferred_element_type=f32)
+        part = jnp.dot(fwd_ref[...], row_taps(shifted, x, OWN), preferred_element_type=f32)
         for a in range(3):
-            if 0 <= x - a < 5:
+            if 0 <= x - a < 3:
                 if a == 0:
                     acc[x] = part[:C]
                 else:
@@ -178,42 +163,40 @@
         shift = (t // 3) * EDGE + t % 3
         edge[t] = (pltpu.roll(rim, 128 - shift, 1) if shift else rim).astype(bf16)
     block = jnp.concatenate(
-        [jnp.concatenate([edge[t, x * C : x * C + C] for t in range(9)], axis=0) for x in range(7)], axis=1
+        [jnp.concatenate([edge[t, x * C : x * C + C] for t in range(9)], axis=0) for x in range(5)], axis=1
     )
     part = jnp.dot(fwd_ref[...], block, preferred_element_type=f32)
     offset = offset_ref[...]
-    for x in range(5):
+    rims = []
+    for x in range(3):
         preact = offset + sum(
             part[a * C : a * C + C, (x + a) * 128 : (x + a) * 128 + 128] for a in range(3)
         )
-        rim_ref[x] = (rim_cot[x * C : x * C + C] * silu_slope(preact)).astype(bf16)
+        rims.append((rim_cot[x * C : x * C + C] * silu_slope(preact)).astype(bf16))
 
     ups = []
-    for x in range(5):
-        beside = jnp.concatenate([cot_ref[y, x] for y in range(10)], axis=1).astype(f32)
+    for x in range(3):
+        beside = jnp.concatenate([cot_ref[y, x] for y in range(8)], axis=1).astype(f32)
         upstream = (beside * silu_slope(acc[x] + offset)).astype(bf16)
-        up_ref[x] = upstream
-        ups.append(upstream[:, 128 : 128 + OWN] if 1 <= x <= 3 else jnp.zeros((C, OWN), bf16))
-
+        ups.append(upstream)
+        up_ref[x, :, :OWN] = upstream
+        up_ref[x, :, OWN:] = rims[x]
+        if x:
+            send_ref[x - 1, :, :OWN] = upstream
+            send_ref[x - 1, :, OWN:] = rims[x]
+
+    none = jnp.zeros((C, OWN), bf16)
     left = jnp.concatenate(
         [
-            jnp.concatenate([ups[x - a] if 0 <= x - a < 5 else ups[0] for a in range(3)], axis=0)
-            for x in range(1, 6)
+            jnp.concatenate([ups[x - a] if 0 <= x - a < 3 else none for a in range(3)], axis=0)
+            for x in range(5)
         ],
         axis=1,
     )
-    right = jnp.concatenate(
-        [
-            jnp.concatenate(
-                [shifted[c, x, :, b * 128 + 128 : b * 128 + 128 + OWN] for b in range(3) for c in range(3)], axis=0
-            )
-            for x in range(1, 6)
-        ],
-        axis=1,
-    )
+    right = jnp.concatenate([row_taps(shifted, x, OWN) for x in range(5)], axis=1)
     total = lax.dot_general(left, right, (((1,), (1,)), ((), ())), preferred_element_type=f32)
 
-    offsets = sum(jnp.sum(ups[x].astype(f32), axis=1, keepdims=True) for x in range(1, 4))
+    offsets = sum(jnp.sum(ups[x].astype(f32), axis=1, keepdims=True) for x in range(3))
     packed = jnp.concatenate(
         [total[a * C : a * C + C] for a in range(3)] + [jnp.broadcast_to(offsets, (C, C))], axis=1
     )
@@ -226,16 +209,28 @@
                 sums_ref[at : at + 8] = jnp.zeros((8, 128), f32)
 
 
-def grad_kernel_body(up_ref, rim_ref, bwd_ref, grad_ref, done_ref, shifted, acc):
-    done_ref[...] = jnp.zeros_like(done_ref)
+def pack_up_kernel(up_ref, before_ref, last_ref):
+    for x in range(5):
+        ref, at = (before_ref, x) if x < 2 else (up_ref, x - 2)
+        last_ref[x] = ref[at, :, 6 * 128 :]
+
+
+def grad_kernel_body(up_ref, before_ref, below_ref, bwd_ref, grad_ref, shifted, acc):
     lane = lax.broadcasted_iota(jnp.int32, (C, 128), 1)
     for x in range(5):
-        rim = rim_ref[x].astype(f32)
+        ref, from_x = (before_ref, x) if x < 2 else (up_ref, x - 2)
+        rim = ref[from_x, :, OWN:].astype(f32)
+        rim_below = below_ref[x, :, 256:].astype(f32)
         for y in range(10):
             at = slice(y * 128, y * 128 + 128)
-            row = up_ref[x, :, at]
-            low = jnp.broadcast_to(rim[:, y * EDGE : y * EDGE + 1], (C, 128)).astype(bf16)
-            high = jnp.broadcast_to(rim[:, y * EDGE + 3 : y * EDGE + 4], (C, 128)).astype(bf16)
+            if y < 2:
+                row = below_ref[x, :, at]
+                ends, n = rim_below, (y + 6) * EDGE
+            else:
+                row = ref[from_x, :, (y - 2) * 128 : (y - 1) * 128]
+                ends, n = rim, (y - 2) * EDGE
+            low = jnp.broadcast_to(ends[:, n : n + 1], (C, 128)).astype(bf16)
+            high = jnp.broadcast_to(ends[:, n + 3 : n + 4], (C, 128)).astype(bf16)
             shifted[0, x, :, at] = jnp.where(lane == 0, low, pltpu.roll(row, 1, 1))
             shifted[1, x, :, at] = row
             shifted[2, x, :, at] = jnp.where(lane == 127, high, pltpu.roll(row, 127, 1))
@@ -317,8 +312,7 @@
     column_ref[...] = jnp.sum(offset_ref[...] * eye, axis=1, keepdims=True)
 
 
-def total_kernel(parts_ref, *rest):
-    spread_ref = rest[-1]
+def total_kernel(parts_ref, spread_ref):
     part = jnp.sum(parts_ref[...], axis=0)
     for n in range(spread_ref.shape[0]):
         spread_ref[n] = part
@@ -370,30 +364,29 @@
     return ahead, [(j, i) for i, j in ahead]
 
 
-def summed(sums, first):
+def summed(sums):
     flat = ("ghi", "gy", "gz")
     parts = lax.all_to_all(sums.reshape(32, 8, 128), flat, 0, 0, tiled=True)
     (spread,) = call(total_kernel, [shape(16, 8, 128, dtype=f32)], 1, limit=4)(parts)
     parts = lax.all_to_all(spread, "glong", 0, 0, tiled=True)
-    (spread,) = call(total_kernel, [shape(32, 8, 128, dtype=f32)], 2, limit=4)(parts, first)
+    (spread,) = call(total_kernel, [shape(32, 8, 128, dtype=f32)], 1, limit=4)(parts)
     return lax.all_to_all(spread, flat, 0, 0, tiled=True).reshape(256, 128)
 
 
 def body(
     field, cotangent, cosmology, lift_weight, lift_bias, style_weight, style_bias, kernel, offset
 ):
-    low, high, mid = pl.pallas_call(
+    low, rest = pl.pallas_call(
         split_kernel,
-        out_shape=[shape(3, 8, C, 128), shape(3, 8, C, 128), shape(1, 8, C, 128)],
+        out_shape=[shape(3, 8, C, 128), shape(3, 8, C, 128)],
         in_specs=[pl.BlockSpec(memory_space=pltpu.HBM)] * 2,
-        out_specs=[VMEM] * 3,
+        out_specs=[VMEM] * 2,
         scratch_shapes=[
             pltpu.VMEM((C, 3, 8, 128), bf16), pltpu.VMEM((C, 3, 8, 128), bf16), pltpu.SemaphoreType.DMA((2,)),
         ],
         compiler_params=pltpu.CompilerParams(vmem_limit_bytes=4 * 1024 * 1024),
     )(*(pltpu.with_memory_space_constraint(block, pltpu.HBM) for block in (field, cotangent)))
-    ahead, back = shifts(("glong", "ghi"))
-    left = lax.ppermute(high, ("glong", "ghi"), ahead)
+    x_ahead, back = shifts(("glong", "ghi"))
     right = lax.ppermute(low, ("glong", "ghi"), back)
 
     taps = jnp.transpose(kernel, (2, 3, 4, 0, 1)).reshape(TAPS, C, C)
@@ -411,36 +404,38 @@
         offset[None, :],
     )
 
-    rows = (low, high, mid, left, right)
-    up, down = call(pack_kernel, [shape(19, C, 128), shape(19, C, 128)], 6, limit=8)(*rows, column)
-    ahead, back = shifts("gy")
-    up = lax.ppermute(up, "gy", ahead)
+    rows = (low, rest, right)
+    (down,) = call(pack_kernel, [shape(13, C, 128)], 4, limit=8)(*rows, column)
+    y_ahead, back = shifts("gy")
     down = lax.ppermute(down, "gy", back)
 
     field_rows, cot_rows, faces = call(
-        gather_kernel, [shape(12, 8, C, 128), shape(10, 8, C, 128), shape(4, 48, 256)], 7
-    )(*rows, up, down)
+        gather_kernel, [shape(12, 8, C, 128), shape(10, 8, C, 128), shape(4, 48, 256)], 4
+    )(*rows, down)
     faces = lax.all_to_all(faces, "gz", 0, 0, tiled=True)
 
-    sums, upstream, rim = call(
+    sums, upstream, send = call(
         conv_kernel,
-        [shape(256, 128, dtype=f32), shape(5, C, OUT), shape(5, C, 128)],
+        [shape(256, 128, dtype=f32), shape(3, C, WITH_RIM), shape(2, C, WITH_RIM)],
         6,
         flops=540_000_000,
         scratch=[
             pltpu.VMEM((8 * C, 12 * 128), bf16),
-            pltpu.VMEM((3, 7, C, 12 * 128), bf16),
+            pltpu.VMEM((3, 5, C, 10 * 128), bf16),
             pltpu.VMEM((9, 8 * C, 128), bf16),
-            pltpu.VMEM((5, C, OUT), f32),
+            pltpu.VMEM((3, C, OWN), f32),
         ],
     )(field_rows, cot_rows, faces, fwd, column, place)
-    grad_field, done = call(
+    before = lax.ppermute(send, ("glong", "ghi"), x_ahead)
+    (last,) = call(pack_up_kernel, [shape(5, C, 3 * 128)], 2, limit=4)(upstream, before)
+    below = lax.ppermute(last, "gy", y_ahead)
+    (grad_field,) = call(
         grad_kernel_body,
-        [shape(C, 3, 8, 128), shape(8, 128, dtype=f32)],
-        3,
+        [shape(C, 3, 8, 128)],
+        4,
         flops=170_000_000,
-        scratch=[pltpu.VMEM((3, 5, C, OUT), bf16), pltpu.VMEM((3, C, OWN), f32)],
-    )(upstream, rim, bwd)
+        scratch=[pltpu.VMEM((3, 5, C, 10 * 128), bf16), pltpu.VMEM((3, C, OWN), f32)],
+    )(upstream, before, below, bwd)
 
     kernel_out, grad_offset, grad_lift, grad_liftbias, grad_style, grad_stylebias = call(
         tail_kernel,
@@ -451,7 +446,7 @@
         9,
         limit=8,
     )(
-        summed(sums, done), packed, modded, styles, inv_norm, lifted, hidden, style_weight.T, params,
+        summed(sums), packed, modded, styles, inv_norm, lifted, hidden, style_weight.T, params,
     )
     grad_kernel = jnp.transpose(kernel_out.reshape(3, 3, 3, C, C), (3, 4, 0, 1, 2))
     return (

time: 96.8 us -> 91.8 us (0.948)
  blocking collectives: 34.6 us -> 21.6 us
  starting transfers between devices: 30.2 us -> 40.5 us
  waiting for transfers between devices: 19.2 us -> 16.5 us
    all_to_all x1 -> x0, blocking collectives: 13 us -> none  [summed(): return lax.all_to_all(spread, flat, 0, 0, tiled=True).reshape(256, 128)]
    all_to_all x1, waiting for transfers between devices: 9.73 us -> 0.01 us  [summed(): parts = lax.all_to_all(spread, 'glong', 0, 0, tiled=True)]
    all_to_all x0 -> x1, starting transfers between devices: none -> 6.6 us  [summed(): return lax.all_to_all(spread, flat, 0, 0, tiled=True).reshape(256, 128)]
    all_to_all x0 -> x1, waiting for transfers between devices: none -> 5.83 us  [summed(): return lax.all_to_all(spread, flat, 0, 0, tiled=True).reshape(256, 128)]
    all_to_all x1, starting transfers between devices: 7.21 us -> 10.3 us  [summed(): parts = lax.all_to_all(spread, 'glong', 0, 0, tiled=True)]
    ppermute x1, waiting for transfers between devices: 0.01 us -> 1.09 us  [body(): right = lax.ppermute(low, ('glong', 'ghi'), back)]
    ppermute x1, starting transfers between devices: 3.38 us -> 4.38 us  [body(): down = lax.ppermute(down, 'gy', back)]
    pallas_call x4 -> x5, Pallas kernels: 5.13 us -> 5.29 us  [the longest x1 2.75 us: body(): call(conv_kernel, [shape(256, 128, dtype=f32), shape(3, C, WITH_RIM), sha...]
  transfers between devices with their start and end apart: 5 -> 6, of which waited for: 4 -> 4; matrix products, arithmetic and copies ran while one was open for 0% -> 0% of each run, Pallas kernels for 3% -> 4%
where the time goes in v8:
time: 91.8 us; the launch traced here: 91.3 us
  starting transfers between devices  40.5 us (44%)
  blocking collectives  21.6 us (24%)
  waiting for transfers between devices  16.5 us (18%)
  Pallas kernels  10.2 us (11%)
  local copies, waits for them, and re-layouts  1.7 us (2%)
    ppermute x1, starting transfers between devices, body(): right = lax.ppermute(low, ('glong', 'ghi'), back)  14.6 us
    all_to_all x1, blocking collectives, summed(): parts = lax.all_to_all(sums.reshape(32, 8, 128), flat, 0, 0, tiled=True)  13.5 us
    all_to_all x1, starting transfers between devices, summed(): parts = lax.all_to_all(spread, 'glong', 0, 0, tiled=True)  10.3 us
    all_to_all x1, blocking collectives, body(): faces = lax.all_to_all(faces, 'gz', 0, 0, tiled=True)  8.12 us
    ppermute x1, waiting for transfers between devices, body(): before = lax.ppermute(send, ('glong', 'ghi'), x_ahead)  7.89 us
    all_to_all x1, starting transfers between devices, summed(): return lax.all_to_all(spread, flat, 0, 0, tiled=True).reshape(256, 128)  6.6 us
    all_to_all x1, waiting for transfers between devices, summed(): return lax.all_to_all(spread, flat, 0, 0, tiled=True).reshape(256, 128)  5.83 us
    ppermute x1, starting transfers between devices, body(): down = lax.ppermute(down, 'gy', back)  4.38 us
  transfers between devices with their start and end apart: 6, of which 4 were waited for; matrix products, arithmetic and copies ran while one was open for 0% of the time, Pallas kernels for 4%

profile of v8, /device:TPU:1, one launch (start us, length us, event | category | flops | bytes accessed | tf_op | source)
XLA Modules:
  0.0 91.3 jit_solution(3873890502445662274)
XLA Ops:
  0.6 1.5 %shard_map.144 = (bf16[3,8,32,128]{3,2,1,0:T(8,128)(2,1)S(1)}, bf16[3,8,32,128]{3,2,1,0:T(8,128)(2,1)S(1)}) custom-call(bf16[32,3,8,128]{3,2,1,0:T(8,128)(2,1)} %field_hbm.1, bf16[32,3,8,128]{3,2,1,0:T(8,128)(2,1)} %cot_hbm.1), custom_call_target="tpu_custom_call" | custom-call | tf_op jit(solution)/shard_map/pallas_call | solution.py:379
  2.2 14.6 %collective-permute-start = (bf16[3,8,32,128]{3,2,1,0:T(8,128)(2,1)S(1)}, bf16[3,8,32,128]{3,2,1,0:T(8,128)(2,1)S(1)}, u32[]{:S(2)}, u32[]{:S(2)}) collective-permute-start(bf16[3,8,32,128]{3,2,1,0:T(8,128)(2,1)S(1)} %get-tuple-element.32.low_ref), channel_id=1, source_target_pairs={{16,0},{32,16},{48,32},{64,48},{80,64},{96,80},{112,96},{128,112},... | collective-permute-start | bytes 589832 | tf_op jit(solution)/shard_map/ppermute | solution.py:390
  16.8 0.6 copy-done.5
  17.4 0.0 copy-done.6
  17.4 0.0 copy-done.2
  17.5 1.0 %copy-done = f32[32,32,3,3,3]{1,0,4,3,2:T(8,128)S(1)} copy-done((f32[32,32,3,3,3]{1,0,4,3,2:T(8,128)S(1)}, f32[32,32,3,3,3]{1,0,4,3,2:T(8,128)}, u32[]{:S(2)}) %copy-start) | copy-done | bytes 110616
  18.5 0.7 shard_map.145
  19.2 1.1 %collective-permute-done.right_ref = bf16[3,8,32,128]{3,2,1,0:T(8,128)(2,1)S(1)} collective-permute-done((bf16[3,8,32,128]{3,2,1,0:T(8,128)(2,1)S(1)}, bf16[3,8,32,128]{3,2,1,0:T(8,128)(2,1)S(1)}, u32[]{:S(2)}, u32[]{:S(2)}) %collective-permute-start) | collective-permute-done | bytes 196640 | tf_op jit(solution)/shard_map/ppermute | solution.py:390
  20.3 4.4 %collective-permute-start.1 = (bf16[13,32,128]{2,1,0:T(8,128)(2,1)S(1)}, bf16[13,32,128]{2,1,0:T(8,128)(2,1)S(1)}, u32[]{:S(2)}, u32[]{:S(2)}) collective-permute-start(bf16[13,32,128]{2,1,0:T(8,128)(2,1)S(1)} %shard_map.146), channel_id=1, source_target_pairs={{4,0},{8,4},{12,8},{0,12},{5,1},{9,5},{13,9},{1,13},{6,2},{10,6},{... | collective-permute-start | bytes 319496 | tf_op jit(solution)/shard_map/ppermute | solution.py:410
  24.7 1.7 %collective-permute-done.1.down_ref = bf16[13,32,128]{2,1,0:T(8,128)(2,1)S(1)} collective-permute-done((bf16[13,32,128]{2,1,0:T(8,128)(2,1)S(1)}, bf16[13,32,128]{2,1,0:T(8,128)(2,1)S(1)}, u32[]{:S(2)}, u32[]{:S(2)}) %collective-permute-start.1) | collective-permute-done | bytes 106528 | tf_op jit(solution)/shard_map/ppermute | solution.py:410
  26.4 0.6 shard_map.147
  27.0 8.1 %all_to_all.20.faces_ref = bf16[4,48,256]{2,1,0:T(8,128)(2,1)S(1)} all-to-all(bf16[4,48,256]{2,1,0:T(8,128)(2,1)S(1)} %get-tuple-element.37), channel_id=1, replica_groups=mesh['glong'=16,'ghi'=2,'gy'=4,'gz'=4] {'gz'}, dimensions={0} | all-to-all | bytes 196608 | tf_op jit(solution)/shard_map/all_to_all | solution.py:415
  35.1 2.8 %shard_map.148 = (f32[256,128]{1,0:T(8,128)S(1)}, bf16[3,32,1152]{2,1,0:T(8,128)(2,1)S(1)}, bf16[2,32,1152]{2,1,0:T(8,128)(2,1)S(1)}) custom-call(bf16[12,8,32,128]{3,2,1,0:T(8,128)(2,1)S(1)} %get-tuple-element.35.field_ref, bf16[10,8,32,128]{3,2,1,0:T(8,128)(2,1)S(1)} %get-tuple-element.36.cot_ref, bf16[4,48,256]{2,1,0:T(8,128)(2,1)S(1)} %all_to_all.20.faces_ref, ...), custom_call_target="tpu_custom_call" | custom-call | flops 540000000 | bytes 1048576 | tf_op jit(solution)/shard_map/pallas_call | solution.py:417
  37.9 13.5 %all_to_all.21.parts_ref = f32[32,8,128]{2,1,0:T(8,128)S(1)} all-to-all(f32[32,8,128]{2,1,0:T(8,128)S(1)} %bitcast.21), channel_id=1, replica_groups=mesh['glong'=16,'ghi'=2,'gy'=4,'gz'=4] {'ghi','gy','gz'}, dimensions={0} | all-to-all | bytes 262144 | tf_op jit(solution)/shard_map/all_to_all | solution.py:369
  51.4 0.7 shard_map.151
  52.1 10.3 %all-to-all-start.2 = ((f32[16,8,128]{2,1,0:T(8,128)}), f32[16,8,128]{2,1,0:T(8,128)S(1)}, u32[]{:S(2)}, u32[]{:S(2)}) async-start(f32[16,8,128]{2,1,0:T(8,128)} %shard_map.151), calls=%async_computation.2 | async-start | bytes 131072 | tf_op jit(solution)/shard_map/all_to_all | solution.py:371
  62.4 2.7 %collective-permute-start.2 = (bf16[2,32,1152]{2,1,0:T(8,128)(2,1)S(1)}, bf16[2,32,1152]{2,1,0:T(8,128)(2,1)S(1)}, u32[]{:S(2)}, u32[]{:S(2)}) collective-permute-start(bf16[2,32,1152]{2,1,0:T(8,128)(2,1)S(1)} %get-tuple-element.41), channel_id=1, source_target_pairs={{0,16},{16,32},{32,48},{48,64},{64,80},{80,96},{96,112},{112,128},... | collective-permute-start | bytes 442376 | tf_op jit(solution)/shard_map/ppermute | solution.py:429
  65.1 7.9 %collective-permute-done.2.before_ref = bf16[2,32,1152]{2,1,0:T(8,128)(2,1)S(1)} collective-permute-done((bf16[2,32,1152]{2,1,0:T(8,128)(2,1)S(1)}, bf16[2,32,1152]{2,1,0:T(8,128)(2,1)S(1)}, u32[]{:S(2)}, u32[]{:S(2)}) %collective-permute-start.2) | collective-permute-done | bytes 147488 | tf_op jit(solution)/shard_map/ppermute | solution.py:429
  73.0 1.9 %collective-permute-start.3 = (bf16[5,32,384]{2,1,0:T(8,128)(2,1)S(1)}, bf16[5,32,384]{2,1,0:T(8,128)(2,1)S(1)}, u32[]{:S(2)}, u32[]{:S(2)}) collective-permute-start(bf16[5,32,384]{2,1,0:T(8,128)(2,1)S(1)} %shard_map.149), channel_id=1, source_target_pairs={{0,4},{4,8},{8,12},{12,0},{1,5},{5,9},{9,13},{13,1},{2,6},{6,10},{... | collective-permute-start | bytes 368648 | tf_op jit(solution)/shard_map/ppermute | solution.py:431
  74.9 0.7 shard_map.152
  75.6 6.6 %all-to-all-start.3 = ((f32[32,8,128]{2,1,0:T(8,128)}), f32[32,8,128]{2,1,0:T(8,128)S(1)}, u32[]{:S(2)}, u32[]{:S(2)}) async-start(f32[32,8,128]{2,1,0:T(8,128)} %shard_map.152), calls=%async_computation.3 | async-start | bytes 262144 | tf_op jit(solution)/shard_map/all_to_all | solution.py:373
  82.2 1.8 %shard_map.150 = bf16[32,3,8,128]{3,2,1,0:T(8,128)(2,1)} custom-call(bf16[3,32,1152]{2,1,0:T(8,128)(2,1)S(1)} %get-tuple-element.40.up_ref, bf16[2,32,1152]{2,1,0:T(8,128)(2,1)S(1)} %collective-permute-done.2.before_ref, bf16[5,32,384]{2,1,0:T(8,128)(2,1)S(1)} %collective-permute-done.3.below_ref, bf16[96,288]{1,0:T(8,128)(2,1)S(1)} %get-tuple-element.42.bwd_ref), custom_call_target="tpu_custom_call" | custom-call | flops 170000000 | bytes 1048576 | tf_op jit(solution)/shard_map/pallas_call | solution.py:432
  84.1 5.8 %all-to-all-done.3 = f32[32,8,128]{2,1,0:T(8,128)S(1)} async-done(((f32[32,8,128]{2,1,0:T(8,128)}), f32[32,8,128]{2,1,0:T(8,128)S(1)}, u32[]{:S(2)}, u32[]{:S(2)}) %all-to-all-start.3) | async-done | bytes 131104 | tf_op jit(solution)/shard_map/all_to_all | solution.py:373
  89.9 1.4 %shard_map.153 = (f32[27,32,32]{2,1,0:T(8,128)}, f32[1,32]{1,0:T(1,128)}, f32[2,256]{1,0:T(2,128)}, f32[1,256]{1,0:T(1,128)}, f32[32,256]{1,0:T(8,128)}, /*index=5*/f32[1,32]{1,0:T(1,128)}) custom-call(f32[256,128]{1,0:T(8,128)S(1)} %bitcast.17, f32[32,896]{1,0:T(8,128)S(1)} %get-tuple-element.44.kernel_ref, f32[32,896]{1,0:T(8,128)S(1)} %get-tuple-element.45.modded_ref, ...), custom_call_target="tpu_custom_call" | custom-call | bytes 1048576 | tf_op jit(solution)/shard_map/pallas_call | solution.py:440
  (14 shorter events, 0.1 us)
Async XLA Ops:
  0.6 16.2 %copy-start.1 = (f32[256,32]{0,1:T(8,128)S(1)}, f32[256,32]{0,1:T(8,128)}, u32[]{:S(2)}) copy-start(f32[256,32]{0,1:T(8,128)} %param.14) | copy-start | bytes 98308
  2.2 18.1 %collective-permute-start = (bf16[3,8,32,128]{3,2,1,0:T(8,128)(2,1)S(1)}, bf16[3,8,32,128]{3,2,1,0:T(8,128)(2,1)S(1)}, u32[]{:S(2)}, u32[]{:S(2)}) collective-permute-start(bf16[3,8,32,128]{3,2,1,0:T(8,128)(2,1)S(1)} %get-tuple-element.32.low_ref), channel_id=1, source_target_pairs={{16,0},{32,16},{48,32},{64,48},{80,64},{96,80},{112,96},{128,112},... | collective-permute-start | bytes 589832 | tf_op jit(solution)/shard_map/ppermute | solution.py:390
  16.8 0.7 copy-start.5
  16.8 0.7 copy-start.6
  16.8 0.7 copy-start.2
  16.8 0.7 copy-start.3
  16.8 0.7 copy-start.4
  17.5 1.0 %copy-start = (f32[32,32,3,3,3]{1,0,4,3,2:T(8,128)S(1)}, f32[32,32,3,3,3]{1,0,4,3,2:T(8,128)}, u32[]{:S(2)}) copy-start(f32[32,32,3,3,3]{1,0,4,3,2:T(8,128)} %param.16) | copy-start | bytes 331780
  20.3 6.1 %collective-permute-start.1 = (bf16[13,32,128]{2,1,0:T(8,128)(2,1)S(1)}, bf16[13,32,128]{2,1,0:T(8,128)(2,1)S(1)}, u32[]{:S(2)}, u32[]{:S(2)}) collective-permute-start(bf16[13,32,128]{2,1,0:T(8,128)(2,1)S(1)} %shard_map.146), channel_id=1, source_target_pairs={{4,0},{8,4},{12,8},{0,12},{5,1},{9,5},{13,9},{1,13},{6,2},{10,6},{... | collective-permute-start | bytes 319496 | tf_op jit(solution)/shard_map/ppermute | solution.py:410
  52.1 22.9 %all-to-all-start.2 = ((f32[16,8,128]{2,1,0:T(8,128)}), f32[16,8,128]{2,1,0:T(8,128)S(1)}, u32[]{:S(2)}, u32[]{:S(2)}) async-start(f32[16,8,128]{2,1,0:T(8,128)} %shard_map.151), calls=%async_computation.2 | async-start | bytes 131072 | tf_op jit(solution)/shard_map/all_to_all | solution.py:371
  62.4 10.6 %collective-permute-start.2 = (bf16[2,32,1152]{2,1,0:T(8,128)(2,1)S(1)}, bf16[2,32,1152]{2,1,0:T(8,128)(2,1)S(1)}, u32[]{:S(2)}, u32[]{:S(2)}) collective-permute-start(bf16[2,32,1152]{2,1,0:T(8,128)(2,1)S(1)} %get-tuple-element.41), channel_id=1, source_target_pairs={{0,16},{16,32},{32,48},{48,64},{64,80},{80,96},{96,112},{112,128},... | collective-permute-start | bytes 442376 | tf_op jit(solution)/shard_map/ppermute | solution.py:429
  73.0 9.2 %collective-permute-start.3 = (bf16[5,32,384]{2,1,0:T(8,128)(2,1)S(1)}, bf16[5,32,384]{2,1,0:T(8,128)(2,1)S(1)}, u32[]{:S(2)}, u32[]{:S(2)}) collective-permute-start(bf16[5,32,384]{2,1,0:T(8,128)(2,1)S(1)} %shard_map.149), channel_id=1, source_target_pairs={{0,4},{4,8},{8,12},{12,0},{1,5},{5,9},{9,13},{13,1},{2,6},{6,10},{... | collective-permute-start | bytes 368648 | tf_op jit(solution)/shard_map/ppermute | solution.py:431
  75.6 14.3 %all-to-all-start.3 = ((f32[32,8,128]{2,1,0:T(8,128)}), f32[32,8,128]{2,1,0:T(8,128)S(1)}, u32[]{:S(2)}, u32[]{:S(2)}) async-start(f32[32,8,128]{2,1,0:T(8,128)} %shard_map.152), calls=%async_computation.3 | async-start | bytes 262144 | tf_op jit(solution)/shard_map/all_to_all | solution.py:373

commit v9 on v8

--- a/solution.py
+++ b/solution.py
@@ -47,7 +47,7 @@
     return hit.astype(bf16)
 
 
-def split_kernel(field_hbm, cot_hbm, low_ref, rest_ref, field_ref, cot_ref, sems):
+def split_kernel(field_hbm, cot_hbm, low_ref, rest_ref, row_ref, corner_ref, field_ref, cot_ref, sems):
     fetches = (
         pltpu.make_async_copy(field_hbm, field_ref, sems.at[0]),
         pltpu.make_async_copy(cot_hbm, cot_ref, sems.at[1]),
@@ -66,6 +66,10 @@
     low_ref[0], low_ref[1], rest_ref[0] = (rows(field_ref, x) for x in range(3))
     fetches[1].wait()
     low_ref[2], rest_ref[1], rest_ref[2] = (rows(cot_ref, x) for x in range(3))
+    for n, (ref, at) in enumerate(((low_ref, 0), (low_ref, 1), (rest_ref, 0))):
+        row_ref[2 * n : 2 * n + 2] = ref[at, 0:2]
+    row_ref[6], row_ref[7] = rest_ref[1, 0], rest_ref[2, 0]
+    corner_ref[0:2], corner_ref[2:4], corner_ref[4] = low_ref[0, 0:2], low_ref[1, 0:2], low_ref[2, 0]
 
 
 def planes(low_ref, rest_ref, right_ref):
@@ -74,24 +78,24 @@
     return field, cot
 
 
-def pack_kernel(low_ref, rest_ref, right_ref, _, down_ref):
-    field, cot = planes(low_ref, rest_ref, right_ref)
-    for n, (ref, at) in enumerate(field):
-        down_ref[2 * n : 2 * n + 2] = ref[at, 0:2]
-    for n, (ref, at) in enumerate(cot):
-        down_ref[10 + n] = ref[at, 0]
-
-
-def gather_kernel(low_ref, rest_ref, right_ref, down_ref, field_out, cot_out, faces_ref):
+def gather_kernel(low_ref, rest_ref, right_ref, row_ref, corner_ref, _, field_out, cot_out, faces_ref):
     field, cot = planes(low_ref, rest_ref, right_ref)
     field_out[...] = jnp.zeros_like(field_out)
     cot_out[...] = jnp.zeros_like(cot_out)
     for n, (ref, at) in enumerate(field):
         for y in range(10):
-            field_out[y, n] = ref[at, y] if y < 8 else down_ref[2 * n + y - 8]
+            if y < 8:
+                field_out[y, n] = ref[at, y]
+            elif n < 3:
+                field_out[y, n] = row_ref[2 * n + y - 8]
+            else:
+                field_out[y, n] = corner_ref[2 * (n - 3) + y - 8]
     for n, (ref, at) in enumerate(cot):
         for y in range(8):
-            cot_out[y, n] = ref[at, y + 1] if y < 7 else down_ref[10 + n]
+            if y < 7:
+                cot_out[y, n] = ref[at, y + 1]
+            else:
+                cot_out[y, n] = row_ref[6 + n] if n < 2 else corner_ref[4]
 
     def faces(lanes, rows):
         pick = select((8, 128), 0, 1, lanes)
@@ -376,11 +380,11 @@
 def body(
     field, cotangent, cosmology, lift_weight, lift_bias, style_weight, style_bias, kernel, offset
 ):
-    low, rest = pl.pallas_call(
+    low, rest, row, corner = pl.pallas_call(
         split_kernel,
-        out_shape=[shape(3, 8, C, 128), shape(3, 8, C, 128)],
+        out_shape=[shape(3, 8, C, 128), shape(3, 8, C, 128), shape(8, C, 128), shape(5, C, 128)],
         in_specs=[pl.BlockSpec(memory_space=pltpu.HBM)] * 2,
-        out_specs=[VMEM] * 2,
+        out_specs=[VMEM] * 4,
         scratch_shapes=[
             pltpu.VMEM((C, 3, 8, 128), bf16), pltpu.VMEM((C, 3, 8, 128), bf16), pltpu.SemaphoreType.DMA((2,)),
         ],
@@ -404,14 +408,14 @@
         offset[None, :],
     )
 
-    rows = (low, rest, right)
-    (down,) = call(pack_kernel, [shape(13, C, 128)], 4, limit=8)(*rows, column)
+    diagonal = [(4 * i + j, 4 * ((i + 31) % 32) + (j + 3) % 4) for i in range(32) for j in range(4)]
+    corner = lax.ppermute(corner, ("glong", "ghi", "gy"), diagonal)
     y_ahead, back = shifts("gy")
-    down = lax.ppermute(down, "gy", back)
+    row = lax.ppermute(row, "gy", back)
 
     field_rows, cot_rows, faces = call(
-        gather_kernel, [shape(12, 8, C, 128), shape(10, 8, C, 128), shape(4, 48, 256)], 4
-    )(*rows, down)
+        gather_kernel, [shape(12, 8, C, 128), shape(10, 8, C, 128), shape(4, 48, 256)], 6
+    )(low, rest, right, row, corner, column)
     faces = lax.all_to_all(faces, "gz", 0, 0, tiled=True)
 
     sums, upstream, send = call(

time: 91.8 us -> 89.3 us (0.973)
  blocking collectives: 21.6 us -> 20 us
    all_to_all x1, starting transfers between devices: 10.3 us -> 7.53 us  [summed(): parts = lax.all_to_all(spread, 'glong', 0, 0, tiled=True)]
    ppermute x1 -> x2, starting transfers between devices: 4.38 us -> 6.61 us  [the longest x1 4.39 us: body(): row = lax.ppermute(row, 'gy', back)]
    all_to_all x1, blocking collectives: 13.5 us -> 11.9 us  [summed(): parts = lax.all_to_all(sums.reshape(32, 8, 128), flat, 0, 0, tiled=True)]
    ppermute x1, waiting for transfers between devices: 1.09 us -> 0.01 us  [body(): right = lax.ppermute(low, ('glong', 'ghi'), back)]
    ppermute x1 -> x2, waiting for transfers between devices: 1.69 us -> 2.46 us  [the longest x1 2.46 us: body(): corner = lax.ppermute(corner, ('glong', 'ghi', 'gy'), diagonal)]
  transfers between devices with their start and end apart: 6 -> 7, of which waited for: 4 -> 3; matrix products, arithmetic and copies ran while one was open for 0% -> 0% of each run, Pallas kernels for 4% -> 4%
where the time goes in v9:
time: 89.3 us; the launch traced here: 88.8 us
  starting transfers between devices  40 us (45%)
  blocking collectives  20 us (22%)
  waiting for transfers between devices  16.2 us (18%)
  Pallas kernels  10.1 us (11%)
  local copies, waits for them, and re-layouts  1.7 us (2%)
    ppermute x1, starting transfers between devices, body(): right = lax.ppermute(low, ('glong', 'ghi'), back)  14.6 us
    all_to_all x1, blocking collectives, summed(): parts = lax.all_to_all(sums.reshape(32, 8, 128), flat, 0, 0, tiled=True)  11.9 us
    all_to_all x1, blocking collectives, body(): faces = lax.all_to_all(faces, 'gz', 0, 0, tiled=True)  8.11 us
    ppermute x1, waiting for transfers between devices, body(): before = lax.ppermute(send, ('glong', 'ghi'), x_ahead)  7.89 us
    all_to_all x1, starting transfers between devices, summed(): parts = lax.all_to_all(spread, 'glong', 0, 0, tiled=True)  7.53 us
    all_to_all x1, starting transfers between devices, summed(): return lax.all_to_all(spread, flat, 0, 0, tiled=True).reshape(256, 128)  6.6 us
    all_to_all x1, waiting for transfers between devices, summed(): return lax.all_to_all(spread, flat, 0, 0, tiled=True).reshape(256, 128)  5.83 us
    ppermute x1, starting transfers between devices, body(): row = lax.ppermute(row, 'gy', back)  4.39 us
  transfers between devices with their start and end apart: 7, of which 3 were waited for; matrix products, arithmetic and copies ran while one was open for 0% of the time, Pallas kernels for 4%

profile of v9, /device:TPU:1, one launch (start us, length us, event | category | flops | bytes accessed | tf_op | source)
XLA Modules:
  0.0 88.8 jit_solution(4232321260972343082)
XLA Ops:
  0.6 1.5 %shard_map.144 = (bf16[3,8,32,128]{3,2,1,0:T(8,128)(2,1)S(1)}, bf16[3,8,32,128]{3,2,1,0:T(8,128)(2,1)S(1)}, bf16[8,32,128]{2,1,0:T(8,128)(2,1)S(1)}, bf16[5,32,128]{2,1,0:T(8,128)(2,1)S(1)}) custom-call(bf16[32,3,8,128]{3,2,1,0:T(8,128)(2,1)} %field_hbm.1, bf16[32,3,8,128]{3,2,1,0:T(8,128)(2,1)} %cot_hbm.1), custom_call_target="tpu_custom_call" | custom-call | tf_op jit(solution)/shard_map/pallas_call | solution.py:383
  2.2 14.6 %collective-permute-start = (bf16[3,8,32,128]{3,2,1,0:T(8,128)(2,1)S(1)}, bf16[3,8,32,128]{3,2,1,0:T(8,128)(2,1)S(1)}, u32[]{:S(2)}, u32[]{:S(2)}) collective-permute-start(bf16[3,8,32,128]{3,2,1,0:T(8,128)(2,1)S(1)} %get-tuple-element.34.low_ref), channel_id=1, source_target_pairs={{16,0},{32,16},{48,32},{64,48},{80,64},{96,80},{112,96},{128,112},... | collective-permute-start | bytes 589832 | tf_op jit(solution)/shard_map/ppermute | solution.py:394
  16.8 4.4 %collective-permute-start.1 = (bf16[8,32,128]{2,1,0:T(8,128)(2,1)S(1)}, bf16[8,32,128]{2,1,0:T(8,128)(2,1)S(1)}, u32[]{:S(2)}, u32[]{:S(2)}) collective-permute-start(bf16[8,32,128]{2,1,0:T(8,128)(2,1)S(1)} %get-tuple-element.36), channel_id=1, source_target_pairs={{4,0},{8,4},{12,8},{0,12},{5,1},{9,5},{13,9},{1,13},{6,2},{10,6},{... | collective-permute-start | bytes 196616 | tf_op jit(solution)/shard_map/ppermute | solution.py:414
  21.2 2.2 %collective-permute-start.2 = (bf16[5,32,128]{2,1,0:T(8,128)(2,1)S(1)}, bf16[5,32,128]{2,1,0:T(8,128)(2,1)S(1)}, u32[]{:S(2)}, u32[]{:S(2)}) collective-permute-start(bf16[5,32,128]{2,1,0:T(8,128)(2,1)S(1)} %get-tuple-element.37), channel_id=1, source_target_pairs={{0,508},{4,496},{8,500},{12,504},{16,12},{20,0},{24,4},{28,8},{32,... | collective-permute-start | bytes 122888 | tf_op jit(solution)/shard_map/ppermute | solution.py:412
  23.5 0.6 copy-done.5
  24.1 0.0 copy-done.6
  24.1 0.0 copy-done.2
  24.1 1.0 %copy-done = f32[32,32,3,3,3]{1,0,4,3,2:T(8,128)S(1)} copy-done((f32[32,32,3,3,3]{1,0,4,3,2:T(8,128)S(1)}, f32[32,32,3,3,3]{1,0,4,3,2:T(8,128)}, u32[]{:S(2)}) %copy-start) | copy-done | bytes 110616
  25.1 0.7 shard_map.145
  25.9 2.5 %collective-permute-done.2.corner_ref = bf16[5,32,128]{2,1,0:T(8,128)(2,1)S(1)} collective-permute-done((bf16[5,32,128]{2,1,0:T(8,128)(2,1)S(1)}, bf16[5,32,128]{2,1,0:T(8,128)(2,1)S(1)}, u32[]{:S(2)}, u32[]{:S(2)}) %collective-permute-start.2) | collective-permute-done | bytes 40992 | tf_op jit(solution)/shard_map/ppermute | solution.py:412
  28.3 0.6 shard_map.146
  28.9 8.1 %all_to_all.20.faces_ref = bf16[4,48,256]{2,1,0:T(8,128)(2,1)S(1)} all-to-all(bf16[4,48,256]{2,1,0:T(8,128)(2,1)S(1)} %get-tuple-element.41), channel_id=1, replica_groups=mesh['glong'=16,'ghi'=2,'gy'=4,'gz'=4] {'gz'}, dimensions={0} | all-to-all | bytes 196608 | tf_op jit(solution)/shard_map/all_to_all | solution.py:419
  37.0 2.7 %shard_map.147 = (f32[256,128]{1,0:T(8,128)S(1)}, bf16[3,32,1152]{2,1,0:T(8,128)(2,1)S(1)}, bf16[2,32,1152]{2,1,0:T(8,128)(2,1)S(1)}) custom-call(bf16[12,8,32,128]{3,2,1,0:T(8,128)(2,1)S(1)} %get-tuple-element.39.field_ref, bf16[10,8,32,128]{3,2,1,0:T(8,128)(2,1)S(1)} %get-tuple-element.40.cot_ref, bf16[4,48,256]{2,1,0:T(8,128)(2,1)S(1)} %all_to_all.20.faces_ref, ...), custom_call_target="tpu_custom_call" | custom-call | flops 540000000 | bytes 1048576 | tf_op jit(solution)/shard_map/pallas_call | solution.py:421
  39.8 11.9 %all_to_all.21.parts_ref = f32[32,8,128]{2,1,0:T(8,128)S(1)} all-to-all(f32[32,8,128]{2,1,0:T(8,128)S(1)} %bitcast.21), channel_id=1, replica_groups=mesh['glong'=16,'ghi'=2,'gy'=4,'gz'=4] {'ghi','gy','gz'}, dimensions={0} | all-to-all | bytes 262144 | tf_op jit(solution)/shard_map/all_to_all | solution.py:373
  51.7 0.7 shard_map.150
  52.3 7.5 %all-to-all-start.2 = ((f32[16,8,128]{2,1,0:T(8,128)}), f32[16,8,128]{2,1,0:T(8,128)S(1)}, u32[]{:S(2)}, u32[]{:S(2)}) async-start(f32[16,8,128]{2,1,0:T(8,128)} %shard_map.150), calls=%async_computation.2 | async-start | bytes 131072 | tf_op jit(solution)/shard_map/all_to_all | solution.py:375
  59.9 2.7 %collective-permute-start.3 = (bf16[2,32,1152]{2,1,0:T(8,128)(2,1)S(1)}, bf16[2,32,1152]{2,1,0:T(8,128)(2,1)S(1)}, u32[]{:S(2)}, u32[]{:S(2)}) collective-permute-start(bf16[2,32,1152]{2,1,0:T(8,128)(2,1)S(1)} %get-tuple-element.45), channel_id=1, source_target_pairs={{0,16},{16,32},{32,48},{48,64},{64,80},{80,96},{96,112},{112,128},... | collective-permute-start | bytes 442376 | tf_op jit(solution)/shard_map/ppermute | solution.py:433
  62.6 7.9 %collective-permute-done.3.before_ref = bf16[2,32,1152]{2,1,0:T(8,128)(2,1)S(1)} collective-permute-done((bf16[2,32,1152]{2,1,0:T(8,128)(2,1)S(1)}, bf16[2,32,1152]{2,1,0:T(8,128)(2,1)S(1)}, u32[]{:S(2)}, u32[]{:S(2)}) %collective-permute-start.3) | collective-permute-done | bytes 147488 | tf_op jit(solution)/shard_map/ppermute | solution.py:433
  70.5 1.9 %collective-permute-start.4 = (bf16[5,32,384]{2,1,0:T(8,128)(2,1)S(1)}, bf16[5,32,384]{2,1,0:T(8,128)(2,1)S(1)}, u32[]{:S(2)}, u32[]{:S(2)}) collective-permute-start(bf16[5,32,384]{2,1,0:T(8,128)(2,1)S(1)} %shard_map.148), channel_id=1, source_target_pairs={{0,4},{4,8},{8,12},{12,0},{1,5},{5,9},{9,13},{13,1},{2,6},{6,10},{... | collective-permute-start | bytes 368648 | tf_op jit(solution)/shard_map/ppermute | solution.py:435
  72.4 0.7 shard_map.151
  73.1 6.6 %all-to-all-start.3 = ((f32[32,8,128]{2,1,0:T(8,128)}), f32[32,8,128]{2,1,0:T(8,128)S(1)}, u32[]{:S(2)}, u32[]{:S(2)}) async-start(f32[32,8,128]{2,1,0:T(8,128)} %shard_map.151), calls=%async_computation.3 | async-start | bytes 262144 | tf_op jit(solution)/shard_map/all_to_all | solution.py:377
  79.7 1.8 %shard_map.149 = bf16[32,3,8,128]{3,2,1,0:T(8,128)(2,1)} custom-call(bf16[3,32,1152]{2,1,0:T(8,128)(2,1)S(1)} %get-tuple-element.44.up_ref, bf16[2,32,1152]{2,1,0:T(8,128)(2,1)S(1)} %collective-permute-done.3.before_ref, bf16[5,32,384]{2,1,0:T(8,128)(2,1)S(1)} %collective-permute-done.4.below_ref, bf16[96,288]{1,0:T(8,128)(2,1)S(1)} %get-tuple-element.46.bwd_ref), custom_call_target="tpu_custom_call" | custom-call | flops 170000000 | bytes 1048576 | tf_op jit(solution)/shard_map/pallas_call | solution.py:436
  81.6 5.8 %all-to-all-done.3 = f32[32,8,128]{2,1,0:T(8,128)S(1)} async-done(((f32[32,8,128]{2,1,0:T(8,128)}), f32[32,8,128]{2,1,0:T(8,128)S(1)}, u32[]{:S(2)}, u32[]{:S(2)}) %all-to-all-start.3) | async-done | bytes 131104 | tf_op jit(solution)/shard_map/all_to_all | solution.py:377
  87.4 1.4 %shard_map.152 = (f32[27,32,32]{2,1,0:T(8,128)}, f32[1,32]{1,0:T(1,128)}, f32[2,256]{1,0:T(2,128)}, f32[1,256]{1,0:T(1,128)}, f32[32,256]{1,0:T(8,128)}, /*index=5*/f32[1,32]{1,0:T(1,128)}) custom-call(f32[256,128]{1,0:T(8,128)S(1)} %bitcast.17, f32[32,896]{1,0:T(8,128)S(1)} %get-tuple-element.48.kernel_ref, f32[32,896]{1,0:T(8,128)S(1)} %get-tuple-element.49.modded_ref, ...), custom_call_target="tpu_custom_call" | custom-call | bytes 1048576 | tf_op jit(solution)/shard_map/pallas_call | solution.py:444
  (15 shorter events, 0.1 us)
Async XLA Ops:
  0.6 22.8 %copy-start.1 = (f32[256,32]{0,1:T(8,128)S(1)}, f32[256,32]{0,1:T(8,128)}, u32[]{:S(2)}) copy-start(f32[256,32]{0,1:T(8,128)} %param.14) | copy-start | bytes 98308
  2.2 26.1 %collective-permute-start = (bf16[3,8,32,128]{3,2,1,0:T(8,128)(2,1)S(1)}, bf16[3,8,32,128]{3,2,1,0:T(8,128)(2,1)S(1)}, u32[]{:S(2)}, u32[]{:S(2)}) collective-permute-start(bf16[3,8,32,128]{3,2,1,0:T(8,128)(2,1)S(1)} %get-tuple-element.34.low_ref), channel_id=1, source_target_pairs={{16,0},{32,16},{48,32},{64,48},{80,64},{96,80},{112,96},{128,112},... | collective-permute-start | bytes 589832 | tf_op jit(solution)/shard_map/ppermute | solution.py:394
  16.8 11.5 %collective-permute-start.1 = (bf16[8,32,128]{2,1,0:T(8,128)(2,1)S(1)}, bf16[8,32,128]{2,1,0:T(8,128)(2,1)S(1)}, u32[]{:S(2)}, u32[]{:S(2)}) collective-permute-start(bf16[8,32,128]{2,1,0:T(8,128)(2,1)S(1)} %get-tuple-element.36), channel_id=1, source_target_pairs={{4,0},{8,4},{12,8},{0,12},{5,1},{9,5},{13,9},{1,13},{6,2},{10,6},{... | collective-permute-start | bytes 196616 | tf_op jit(solution)/shard_map/ppermute | solution.py:414
  21.2 7.1 %collective-permute-start.2 = (bf16[5,32,128]{2,1,0:T(8,128)(2,1)S(1)}, bf16[5,32,128]{2,1,0:T(8,128)(2,1)S(1)}, u32[]{:S(2)}, u32[]{:S(2)}) collective-permute-start(bf16[5,32,128]{2,1,0:T(8,128)(2,1)S(1)} %get-tuple-element.37), channel_id=1, source_target_pairs={{0,508},{4,496},{8,500},{12,504},{16,12},{20,0},{24,4},{28,8},{32,... | collective-permute-start | bytes 122888 | tf_op jit(solution)/shard_map/ppermute | solution.py:412
  23.4 0.7 copy-start.5
  23.4 0.7 copy-start.6
  23.4 0.7 copy-start.2
  23.4 0.7 copy-start.3
  23.4 0.7 copy-start.4
  24.1 1.0 %copy-start = (f32[32,32,3,3,3]{1,0,4,3,2:T(8,128)S(1)}, f32[32,32,3,3,3]{1,0,4,3,2:T(8,128)}, u32[]{:S(2)}) copy-start(f32[32,32,3,3,3]{1,0,4,3,2:T(8,128)} %param.16) | copy-start | bytes 331780
  52.3 20.1 %all-to-all-start.2 = ((f32[16,8,128]{2,1,0:T(8,128)}), f32[16,8,128]{2,1,0:T(8,128)S(1)}, u32[]{:S(2)}, u32[]{:S(2)}) async-start(f32[16,8,128]{2,1,0:T(8,128)} %shard_map.150), calls=%async_computation.2 | async-start | bytes 131072 | tf_op jit(solution)/shard_map/all_to_all | solution.py:375
  59.9 10.6 %collective-permute-start.3 = (bf16[2,32,1152]{2,1,0:T(8,128)(2,1)S(1)}, bf16[2,32,1152]{2,1,0:T(8,128)(2,1)S(1)}, u32[]{:S(2)}, u32[]{:S(2)}) collective-permute-start(bf16[2,32,1152]{2,1,0:T(8,128)(2,1)S(1)} %get-tuple-element.45), channel_id=1, source_target_pairs={{0,16},{16,32},{32,48},{48,64},{64,80},{80,96},{96,112},{112,128},... | collective-permute-start | bytes 442376 | tf_op jit(solution)/shard_map/ppermute | solution.py:433
  70.5 9.2 %collective-permute-start.4 = (bf16[5,32,384]{2,1,0:T(8,128)(2,1)S(1)}, bf16[5,32,384]{2,1,0:T(8,128)(2,1)S(1)}, u32[]{:S(2)}, u32[]{:S(2)}) collective-permute-start(bf16[5,32,384]{2,1,0:T(8,128)(2,1)S(1)} %shard_map.148), channel_id=1, source_target_pairs={{0,4},{4,8},{8,12},{12,0},{1,5},{5,9},{9,13},{13,1},{2,6},{6,10},{... | collective-permute-start | bytes 368648 | tf_op jit(solution)/shard_map/ppermute | solution.py:435
  73.1 14.3 %all-to-all-start.3 = ((f32[32,8,128]{2,1,0:T(8,128)}), f32[32,8,128]{2,1,0:T(8,128)S(1)}, u32[]{:S(2)}, u32[]{:S(2)}) async-start(f32[32,8,128]{2,1,0:T(8,128)} %shard_map.151), calls=%async_computation.3 | async-start | bytes 262144 | tf_op jit(solution)/shard_map/all_to_all | solution.py:377

commit v10 on v9

--- a/solution.py
+++ b/solution.py
@@ -70,6 +70,7 @@
         row_ref[2 * n : 2 * n + 2] = ref[at, 0:2]
     row_ref[6], row_ref[7] = rest_ref[1, 0], rest_ref[2, 0]
     corner_ref[0:2], corner_ref[2:4], corner_ref[4] = low_ref[0, 0:2], low_ref[1, 0:2], low_ref[2, 0]
+    corner_ref[5:9] = jnp.zeros((4, C, 128), bf16)
 
 
 def planes(low_ref, rest_ref, right_ref):
@@ -382,7 +383,7 @@
 ):
     low, rest, row, corner = pl.pallas_call(
         split_kernel,
-        out_shape=[shape(3, 8, C, 128), shape(3, 8, C, 128), shape(8, C, 128), shape(5, C, 128)],
+        out_shape=[shape(3, 8, C, 128), shape(3, 8, C, 128), shape(8, C, 128), shape(9, C, 128)],
         in_specs=[pl.BlockSpec(memory_space=pltpu.HBM)] * 2,
         out_specs=[VMEM] * 4,
         scratch_shapes=[

time: 89.3 us -> 88.1 us (0.987)
  blocking collectives: 20 us -> 22.6 us
  waiting for transfers between devices: 16.2 us -> 13.9 us
  starting transfers between devices: 40 us -> 38.4 us
    ppermute x1, waiting for transfers between devices: 2.46 us -> 0.01 us  [body(): corner = lax.ppermute(corner, ('glong', 'ghi', 'gy'), diagonal)]
    all_to_all x1, blocking collectives: 11.9 us -> 14.3 us  [summed(): parts = lax.all_to_all(sums.reshape(32, 8, 128), flat, 0, 0, tiled=True)]
    ppermute x1, starting transfers between devices: 4.39 us -> 2.46 us  [body(): row = lax.ppermute(row, 'gy', back)]
    ppermute x1, starting transfers between devices: 2.23 us -> 4.15 us  [body(): corner = lax.ppermute(corner, ('glong', 'ghi', 'gy'), diagonal)]
    all_to_all x1, starting transfers between devices: 7.53 us -> 5.98 us  [summed(): parts = lax.all_to_all(spread, 'glong', 0, 0, tiled=True)]
where the time goes in v10:
time: 88.1 us; the launch traced here: 87.5 us
  starting transfers between devices  38.4 us (44%)
  blocking collectives  22.6 us (26%)
  waiting for transfers between devices  13.9 us (16%)
  Pallas kernels  10.2 us (12%)
  local copies, waits for them, and re-layouts  1.7 us (2%)
    ppermute x1, starting transfers between devices, body(): right = lax.ppermute(low, ('glong', 'ghi'), back)  14.6 us
    all_to_all x1, blocking collectives, summed(): parts = lax.all_to_all(sums.reshape(32, 8, 128), flat, 0, 0, tiled=True)  14.3 us
    all_to_all x1, blocking collectives, body(): faces = lax.all_to_all(faces, 'gz', 0, 0, tiled=True)  8.35 us
    ppermute x1, waiting for transfers between devices, body(): before = lax.ppermute(send, ('glong', 'ghi'), x_ahead)  7.89 us
    all_to_all x1, starting transfers between devices, summed(): return lax.all_to_all(spread, flat, 0, 0, tiled=True).reshape(256, 128)  6.6 us
    all_to_all x1, starting transfers between devices, summed(): parts = lax.all_to_all(spread, 'glong', 0, 0, tiled=True)  5.98 us
    all_to_all x1, waiting for transfers between devices, summed(): return lax.all_to_all(spread, flat, 0, 0, tiled=True).reshape(256, 128)  5.83 us
    ppermute x1, starting transfers between devices, body(): corner = lax.ppermute(corner, ('glong', 'ghi', 'gy'), diagonal)  4.15 us
  transfers between devices with their start and end apart: 7, of which 3 were waited for; matrix products, arithmetic and copies ran while one was open for 0% of the time, Pallas kernels for 4%

profile of v10, /device:TPU:1, one launch (start us, length us, event | category | flops | bytes accessed | tf_op | source)
XLA Modules:
  0.0 87.5 jit_solution(4686222565871049064)
XLA Ops:
  0.6 1.5 %shard_map.144 = (bf16[3,8,32,128]{3,2,1,0:T(8,128)(2,1)S(1)}, bf16[3,8,32,128]{3,2,1,0:T(8,128)(2,1)S(1)}, bf16[8,32,128]{2,1,0:T(8,128)(2,1)S(1)}, bf16[9,32,128]{2,1,0:T(8,128)(2,1)S(1)}) custom-call(bf16[32,3,8,128]{3,2,1,0:T(8,128)(2,1)} %field_hbm.1, bf16[32,3,8,128]{3,2,1,0:T(8,128)(2,1)} %cot_hbm.1), custom_call_target="tpu_custom_call" | custom-call | tf_op jit(solution)/shard_map/pallas_call | solution.py:384
  2.2 14.6 %collective-permute-start = (bf16[3,8,32,128]{3,2,1,0:T(8,128)(2,1)S(1)}, bf16[3,8,32,128]{3,2,1,0:T(8,128)(2,1)S(1)}, u32[]{:S(2)}, u32[]{:S(2)}) collective-permute-start(bf16[3,8,32,128]{3,2,1,0:T(8,128)(2,1)S(1)} %get-tuple-element.34.low_ref), channel_id=1, source_target_pairs={{16,0},{32,16},{48,32},{64,48},{80,64},{96,80},{112,96},{128,112},... | collective-permute-start | bytes 589832 | tf_op jit(solution)/shard_map/ppermute | solution.py:395
  16.8 4.2 %collective-permute-start.2 = (bf16[9,32,128]{2,1,0:T(8,128)(2,1)S(1)}, bf16[9,32,128]{2,1,0:T(8,128)(2,1)S(1)}, u32[]{:S(2)}, u32[]{:S(2)}) collective-permute-start(bf16[9,32,128]{2,1,0:T(8,128)(2,1)S(1)} %get-tuple-element.37), channel_id=1, source_target_pairs={{0,508},{4,496},{8,500},{12,504},{16,12},{20,0},{24,4},{28,8},{32,... | collective-permute-start | bytes 221192 | tf_op jit(solution)/shard_map/ppermute | solution.py:413
  20.9 2.5 %collective-permute-start.1 = (bf16[8,32,128]{2,1,0:T(8,128)(2,1)S(1)}, bf16[8,32,128]{2,1,0:T(8,128)(2,1)S(1)}, u32[]{:S(2)}, u32[]{:S(2)}) collective-permute-start(bf16[8,32,128]{2,1,0:T(8,128)(2,1)S(1)} %get-tuple-element.36), channel_id=1, source_target_pairs={{4,0},{8,4},{12,8},{0,12},{5,1},{9,5},{13,9},{1,13},{6,2},{10,6},{... | collective-permute-start | bytes 196616 | tf_op jit(solution)/shard_map/ppermute | solution.py:415
  23.5 0.6 copy-done.5
  24.1 0.0 copy-done.6
  24.1 0.0 copy-done.2
  24.1 1.0 %copy-done = f32[32,32,3,3,3]{1,0,4,3,2:T(8,128)S(1)} copy-done((f32[32,32,3,3,3]{1,0,4,3,2:T(8,128)S(1)}, f32[32,32,3,3,3]{1,0,4,3,2:T(8,128)}, u32[]{:S(2)}) %copy-start) | copy-done | bytes 110616
  25.1 0.7 shard_map.145
  25.9 0.1 collective-permute-done.1.row_ref
  26.0 0.6 shard_map.146
  26.6 8.3 %all_to_all.20.faces_ref = bf16[4,48,256]{2,1,0:T(8,128)(2,1)S(1)} all-to-all(bf16[4,48,256]{2,1,0:T(8,128)(2,1)S(1)} %get-tuple-element.41), channel_id=1, replica_groups=mesh['glong'=16,'ghi'=2,'gy'=4,'gz'=4] {'gz'}, dimensions={0} | all-to-all | bytes 196608 | tf_op jit(solution)/shard_map/all_to_all | solution.py:420
  34.9 2.7 %shard_map.147 = (f32[256,128]{1,0:T(8,128)S(1)}, bf16[3,32,1152]{2,1,0:T(8,128)(2,1)S(1)}, bf16[2,32,1152]{2,1,0:T(8,128)(2,1)S(1)}) custom-call(bf16[12,8,32,128]{3,2,1,0:T(8,128)(2,1)S(1)} %get-tuple-element.39.field_ref, bf16[10,8,32,128]{3,2,1,0:T(8,128)(2,1)S(1)} %get-tuple-element.40.cot_ref, bf16[4,48,256]{2,1,0:T(8,128)(2,1)S(1)} %all_to_all.20.faces_ref, ...), custom_call_target="tpu_custom_call" | custom-call | flops 540000000 | bytes 1048576 | tf_op jit(solution)/shard_map/pallas_call | solution.py:422
  37.7 14.3 %all_to_all.21.parts_ref = f32[32,8,128]{2,1,0:T(8,128)S(1)} all-to-all(f32[32,8,128]{2,1,0:T(8,128)S(1)} %bitcast.21), channel_id=1, replica_groups=mesh['glong'=16,'ghi'=2,'gy'=4,'gz'=4] {'ghi','gy','gz'}, dimensions={0} | all-to-all | bytes 262144 | tf_op jit(solution)/shard_map/all_to_all | solution.py:374
  52.0 0.7 shard_map.150
  52.6 6.0 %all-to-all-start.2 = ((f32[16,8,128]{2,1,0:T(8,128)}), f32[16,8,128]{2,1,0:T(8,128)S(1)}, u32[]{:S(2)}, u32[]{:S(2)}) async-start(f32[16,8,128]{2,1,0:T(8,128)} %shard_map.150), calls=%async_computation.2 | async-start | bytes 131072 | tf_op jit(solution)/shard_map/all_to_all | solution.py:376
  58.6 2.7 %collective-permute-start.3 = (bf16[2,32,1152]{2,1,0:T(8,128)(2,1)S(1)}, bf16[2,32,1152]{2,1,0:T(8,128)(2,1)S(1)}, u32[]{:S(2)}, u32[]{:S(2)}) collective-permute-start(bf16[2,32,1152]{2,1,0:T(8,128)(2,1)S(1)} %get-tuple-element.45), channel_id=1, source_target_pairs={{0,16},{16,32},{32,48},{48,64},{64,80},{80,96},{96,112},{112,128},... | collective-permute-start | bytes 442376 | tf_op jit(solution)/shard_map/ppermute | solution.py:434
  61.3 7.9 %collective-permute-done.3.before_ref = bf16[2,32,1152]{2,1,0:T(8,128)(2,1)S(1)} collective-permute-done((bf16[2,32,1152]{2,1,0:T(8,128)(2,1)S(1)}, bf16[2,32,1152]{2,1,0:T(8,128)(2,1)S(1)}, u32[]{:S(2)}, u32[]{:S(2)}) %collective-permute-start.3) | collective-permute-done | bytes 147488 | tf_op jit(solution)/shard_map/ppermute | solution.py:434
  69.3 1.9 %collective-permute-start.4 = (bf16[5,32,384]{2,1,0:T(8,128)(2,1)S(1)}, bf16[5,32,384]{2,1,0:T(8,128)(2,1)S(1)}, u32[]{:S(2)}, u32[]{:S(2)}) collective-permute-start(bf16[5,32,384]{2,1,0:T(8,128)(2,1)S(1)} %shard_map.148), channel_id=1, source_target_pairs={{0,4},{4,8},{8,12},{12,0},{1,5},{5,9},{9,13},{13,1},{2,6},{6,10},{... | collective-permute-start | bytes 368648 | tf_op jit(solution)/shard_map/ppermute | solution.py:436
  71.2 0.7 shard_map.151
  71.9 6.6 %all-to-all-start.3 = ((f32[32,8,128]{2,1,0:T(8,128)}), f32[32,8,128]{2,1,0:T(8,128)S(1)}, u32[]{:S(2)}, u32[]{:S(2)}) async-start(f32[32,8,128]{2,1,0:T(8,128)} %shard_map.151), calls=%async_computation.3 | async-start | bytes 262144 | tf_op jit(solution)/shard_map/all_to_all | solution.py:378
  78.5 1.8 %shard_map.149 = bf16[32,3,8,128]{3,2,1,0:T(8,128)(2,1)} custom-call(bf16[3,32,1152]{2,1,0:T(8,128)(2,1)S(1)} %get-tuple-element.44.up_ref, bf16[2,32,1152]{2,1,0:T(8,128)(2,1)S(1)} %collective-permute-done.3.before_ref, bf16[5,32,384]{2,1,0:T(8,128)(2,1)S(1)} %collective-permute-done.4.below_ref, bf16[96,288]{1,0:T(8,128)(2,1)S(1)} %get-tuple-element.46.bwd_ref), custom_call_target="tpu_custom_call" | custom-call | flops 170000000 | bytes 1048576 | tf_op jit(solution)/shard_map/pallas_call | solution.py:437
  80.3 5.8 %all-to-all-done.3 = f32[32,8,128]{2,1,0:T(8,128)S(1)} async-done(((f32[32,8,128]{2,1,0:T(8,128)}), f32[32,8,128]{2,1,0:T(8,128)S(1)}, u32[]{:S(2)}, u32[]{:S(2)}) %all-to-all-start.3) | async-done | bytes 131104 | tf_op jit(solution)/shard_map/all_to_all | solution.py:378
  86.2 1.4 %shard_map.152 = (f32[27,32,32]{2,1,0:T(8,128)}, f32[1,32]{1,0:T(1,128)}, f32[2,256]{1,0:T(2,128)}, f32[1,256]{1,0:T(1,128)}, f32[32,256]{1,0:T(8,128)}, /*index=5*/f32[1,32]{1,0:T(1,128)}) custom-call(f32[256,128]{1,0:T(8,128)S(1)} %bitcast.17, f32[32,896]{1,0:T(8,128)S(1)} %get-tuple-element.48.kernel_ref, f32[32,896]{1,0:T(8,128)S(1)} %get-tuple-element.49.modded_ref, ...), custom_call_target="tpu_custom_call" | custom-call | bytes 1048576 | tf_op jit(solution)/shard_map/pallas_call | solution.py:445
  (15 shorter events, 0.1 us)
Async XLA Ops:
  0.6 22.8 %copy-start.1 = (f32[256,32]{0,1:T(8,128)S(1)}, f32[256,32]{0,1:T(8,128)}, u32[]{:S(2)}) copy-start(f32[256,32]{0,1:T(8,128)} %param.14) | copy-start | bytes 98308
  2.2 23.8 %collective-permute-start = (bf16[3,8,32,128]{3,2,1,0:T(8,128)(2,1)S(1)}, bf16[3,8,32,128]{3,2,1,0:T(8,128)(2,1)S(1)}, u32[]{:S(2)}, u32[]{:S(2)}) collective-permute-start(bf16[3,8,32,128]{3,2,1,0:T(8,128)(2,1)S(1)} %get-tuple-element.34.low_ref), channel_id=1, source_target_pairs={{16,0},{32,16},{48,32},{64,48},{80,64},{96,80},{112,96},{128,112},... | collective-permute-start | bytes 589832 | tf_op jit(solution)/shard_map/ppermute | solution.py:395
  16.8 9.2 %collective-permute-start.2 = (bf16[9,32,128]{2,1,0:T(8,128)(2,1)S(1)}, bf16[9,32,128]{2,1,0:T(8,128)(2,1)S(1)}, u32[]{:S(2)}, u32[]{:S(2)}) collective-permute-start(bf16[9,32,128]{2,1,0:T(8,128)(2,1)S(1)} %get-tuple-element.37), channel_id=1, source_target_pairs={{0,508},{4,496},{8,500},{12,504},{16,12},{20,0},{24,4},{28,8},{32,... | collective-permute-start | bytes 221192 | tf_op jit(solution)/shard_map/ppermute | solution.py:413
  20.9 5.0 %collective-permute-start.1 = (bf16[8,32,128]{2,1,0:T(8,128)(2,1)S(1)}, bf16[8,32,128]{2,1,0:T(8,128)(2,1)S(1)}, u32[]{:S(2)}, u32[]{:S(2)}) collective-permute-start(bf16[8,32,128]{2,1,0:T(8,128)(2,1)S(1)} %get-tuple-element.36), channel_id=1, source_target_pairs={{4,0},{8,4},{12,8},{0,12},{5,1},{9,5},{13,9},{1,13},{6,2},{10,6},{... | collective-permute-start | bytes 196616 | tf_op jit(solution)/shard_map/ppermute | solution.py:415
  23.4 0.7 copy-start.5
  23.4 0.7 copy-start.6
  23.4 0.7 copy-start.2
  23.4 0.7 copy-start.3
  23.4 0.7 copy-start.4
  24.1 1.0 %copy-start = (f32[32,32,3,3,3]{1,0,4,3,2:T(8,128)S(1)}, f32[32,32,3,3,3]{1,0,4,3,2:T(8,128)}, u32[]{:S(2)}) copy-start(f32[32,32,3,3,3]{1,0,4,3,2:T(8,128)} %param.16) | copy-start | bytes 331780
  52.6 18.5 %all-to-all-start.2 = ((f32[16,8,128]{2,1,0:T(8,128)}), f32[16,8,128]{2,1,0:T(8,128)S(1)}, u32[]{:S(2)}, u32[]{:S(2)}) async-start(f32[16,8,128]{2,1,0:T(8,128)} %shard_map.150), calls=%async_computation.2 | async-start | bytes 131072 | tf_op jit(solution)/shard_map/all_to_all | solution.py:376
  58.6 10.6 %collective-permute-start.3 = (bf16[2,32,1152]{2,1,0:T(8,128)(2,1)S(1)}, bf16[2,32,1152]{2,1,0:T(8,128)(2,1)S(1)}, u32[]{:S(2)}, u32[]{:S(2)}) collective-permute-start(bf16[2,32,1152]{2,1,0:T(8,128)(2,1)S(1)} %get-tuple-element.45), channel_id=1, source_target_pairs={{0,16},{16,32},{32,48},{48,64},{64,80},{80,96},{96,112},{112,128},... | collective-permute-start | bytes 442376 | tf_op jit(solution)/shard_map/ppermute | solution.py:434
  69.3 9.2 %collective-permute-start.4 = (bf16[5,32,384]{2,1,0:T(8,128)(2,1)S(1)}, bf16[5,32,384]{2,1,0:T(8,128)(2,1)S(1)}, u32[]{:S(2)}, u32[]{:S(2)}) collective-permute-start(bf16[5,32,384]{2,1,0:T(8,128)(2,1)S(1)} %shard_map.148), channel_id=1, source_target_pairs={{0,4},{4,8},{8,12},{12,0},{1,5},{5,9},{9,13},{13,1},{2,6},{6,10},{... | collective-permute-start | bytes 368648 | tf_op jit(solution)/shard_map/ppermute | solution.py:436
  71.9 14.3 %all-to-all-start.3 = ((f32[32,8,128]{2,1,0:T(8,128)}), f32[32,8,128]{2,1,0:T(8,128)S(1)}, u32[]{:S(2)}, u32[]{:S(2)}) async-start(f32[32,8,128]{2,1,0:T(8,128)} %shard_map.151), calls=%async_computation.3 | async-start | bytes 262144 | tf_op jit(solution)/shard_map/all_to_all | solution.py:378
